TPU v7x, 256 devices: a whole 4x4x8 slice. The times are simulated.
256 devices in a mesh: blk: 64 (over x_lo, z, y), head: 4 (over x_hi, core).
Axes of the slice: x: 4 (x_hi: 2, x_lo: 2; x = x_hi * 2 + x_lo), y: 4, z: 8, core: 2. Of those that a mesh axis runs over, the one named last changes fastest.
Arguments:
- queries: bfloat16 [8192, 1536], P('blk', 'head'), may hold values from -5 to 5
- keys: bfloat16 [8192, 1536], P('blk', 'head'), may hold values from -5 to 5
- values: bfloat16 [8192, 1536], P('blk', 'head'), may hold values from -6 to 6
- tan_queries: bfloat16 [8192, 1536], P('blk', 'head'), may hold values from -6 to 6
- tan_keys: bfloat16 [8192, 1536], P('blk', 'head'), may hold values from -6 to 6
- tan_values: bfloat16 [8192, 1536], P('blk', 'head'), may hold values from -6 to 6
- out_weight: bfloat16 [1536, 3072], P('head'), may hold values from -0.625 to 0.625
Outputs:
- attended: bfloat16 [8192, 3072], P(('blk', 'head'))
- tan_attended: bfloat16 [8192, 3072], P(('blk', 'head'))
All inputs are finite; a program needn't handle non-finite values.
Results may differ from a plain program's by a relative error of at most 0.013.
Values may be sent and summed in bfloat16 or wider, within the bound.
No kernel may reach another device: no remote copies, remote signals or barrier semaphores. Data moves between devices by JAX's collectives and lax.ppermute only.
A program may use at most 128 MiB of HBM per device.

v0:
```python
import math

import jax
import jax.numpy as jnp
from jax import lax
from jax.sharding import PartitionSpec as P

HEAD_DIM = 128


NEG_FLOOR = -1e30


def absorb_block(carry_state, queries3, tan_queries3, portion, score_scale):
    run_max, denom, tan_denom, accum, tan_accum = carry_state
    key_count = portion[0].shape[0]
    head_count = queries3.shape[1]
    keys3, values3, tan_keys3, tan_values3 = [
        tensor_part.reshape(key_count, head_count, -1) for tensor_part in portion
    ]
    scores = (
        jnp.einsum("thd,shd->ths", queries3, keys3, preferred_element_type=jnp.float32)
        * score_scale
    )
    tan_scores = (
        jnp.einsum("thd,shd->ths", tan_queries3, keys3, preferred_element_type=jnp.float32)
        + jnp.einsum("thd,shd->ths", queries3, tan_keys3, preferred_element_type=jnp.float32)
    ) * score_scale
    new_max = jnp.maximum(run_max, jnp.max(scores, axis=2, keepdims=True))
    rescale = jnp.exp(run_max - new_max)
    weights = jnp.exp(scores - new_max)
    tangent_weights = weights * tan_scores
    denom = denom * rescale + jnp.sum(weights, axis=2, keepdims=True)
    tan_denom = tan_denom * rescale + jnp.sum(tangent_weights, axis=2, keepdims=True)
    weights_low = weights.astype(jnp.bfloat16)
    tangent_low = tangent_weights.astype(jnp.bfloat16)
    accum = accum * rescale + jnp.einsum(
        "ths,shd->thd", weights_low, values3, preferred_element_type=jnp.float32
    )
    tan_accum = (
        tan_accum * rescale
        + jnp.einsum("ths,shd->thd", tangent_low, values3, preferred_element_type=jnp.float32)
        + jnp.einsum("ths,shd->thd", weights_low, tan_values3, preferred_element_type=jnp.float32)
    )
    return (new_max, denom, tan_denom, accum, tan_accum)


def absorb_rows(carry_state, queries3, tan_queries3, portion, score_scale):
    total_rows = portion[0].shape[0]
    block_span = math.gcd(total_rows, 1024)

    def advance(block_index, inner_state):
        sliced = tuple(
            (
                lax.dynamic_slice_in_dim(tensor_part, block_index * block_span, block_span, 0)
                for tensor_part in portion
            )
        )
        return absorb_block(inner_state, queries3, tan_queries3, sliced, score_scale)

    return lax.fori_loop(0, total_rows // block_span, advance, carry_state)


def on_device(queries, keys, values, tan_queries, tan_keys, tan_values, out_weight):
    tok_rows = queries.shape[0]
    feature_width = queries.shape[1]
    head_count = feature_width // HEAD_DIM
    score_scale = 1.0 / math.sqrt(HEAD_DIM)
    queries3 = queries.reshape(tok_rows, head_count, HEAD_DIM)
    tan_queries3 = tan_queries.reshape(tok_rows, head_count, HEAD_DIM)
    stat_zero = jnp.zeros((tok_rows, head_count, 1), jnp.float32)
    accum_zero = jnp.zeros((tok_rows, head_count, HEAD_DIM), jnp.float32)
    initial = (
        jnp.full((tok_rows, head_count, 1), NEG_FLOOR, jnp.float32),
        stat_zero,
        stat_zero,
        accum_zero,
        accum_zero,
    )
    gathered = (
        lax.all_gather(keys, "blk", axis=0, tiled=True),
        lax.all_gather(values, "blk", axis=0, tiled=True),
        lax.all_gather(tan_keys, "blk", axis=0, tiled=True),
        lax.all_gather(tan_values, "blk", axis=0, tiled=True),
    )
    final_state = absorb_rows(initial, queries3, tan_queries3, tuple(gathered), score_scale)
    run_max, denom, tan_denom, accum, tan_accum = final_state
    head_out = accum / denom
    head_tan = tan_accum / denom - head_out * (tan_denom / denom)
    out_rows = head_out.astype(jnp.bfloat16).reshape(tok_rows, feature_width)
    tan_rows = head_tan.astype(jnp.bfloat16).reshape(tok_rows, feature_width)
    share_rows = tok_rows // lax.axis_size("head")
    summed = lax.psum(
        jnp.concatenate(
            [
                jnp.dot(out_rows, out_weight, preferred_element_type=jnp.float32),
                jnp.dot(tan_rows, out_weight, preferred_element_type=jnp.float32),
            ],
            axis=1,
        ),
        "head",
    )
    combined = lax.dynamic_slice_in_dim(summed, lax.axis_index("head") * share_rows, share_rows, 0)
    out_width = out_weight.shape[1]
    return (
        combined[:, :out_width].astype(jnp.bfloat16),
        combined[:, out_width:].astype(jnp.bfloat16),
    )


def solution(mesh):
    return jax.shard_map(
        on_device,
        mesh=mesh,
        in_specs=(
            P("blk", "head"),
            P("blk", "head"),
            P("blk", "head"),
            P("blk", "head"),
            P("blk", "head"),
            P("blk", "head"),
            P("head", None),
        ),
        out_specs=(P(("blk", "head"), None), P(("blk", "head"), None)),
        check_vma=False,
    )
```

profile of v0, /device:TPU:1, one launch (start us, length us, event | category | flops | bytes accessed | tf_op | source)
XLA Modules:
  0.0 1192.0 jit_solution(3688843908535172440)
XLA Ops:
  7.2 1.8 copy.25
  9.1 1.6 copy.20
  10.8 1.6 copy.23
  12.5 1.6 copy.24
  14.2 1.0 copy.21
  15.7 219.4 %all-gather.11.cloned.1.call-done = bf16[8192,384]{0,1:T(8,128)(2,1)} async-done(((bf16[128,384]{0,1:T(8,128)(2,1)}), bf16[8192,384]{0,1:T(8,128)(2,1)}) %all-gather.11.cloned.1.call-update) | async-done | bytes 6291472 | tf_op jit(solution)/shard_map/all_gather | solution.py:84
  235.0 256.7 %all-gather.5.cloned.1.call-done = bf16[8192,384]{0,1:T(8,128)(2,1)} async-done(((bf16[128,384]{0,1:T(8,128)(2,1)}), bf16[8192,384]{0,1:T(8,128)(2,1)}) %all-gather.5.cloned.1.call-update) | async-done | bytes 6291472 | tf_op jit(solution)/shard_map/all_gather | solution.py:81
  491.7 256.2 %all-gather.7.cloned.1.call-done = bf16[8192,384]{0,1:T(8,128)(2,1)} async-done(((bf16[128,384]{0,1:T(8,128)(2,1)}), bf16[8192,384]{0,1:T(8,128)(2,1)}) %all-gather.7.cloned.1.call-update) | async-done | bytes 6291472 | tf_op jit(solution)/shard_map/all_gather | solution.py:83
  747.9 256.0 %all-gather.9.cloned.1.call-done = bf16[8192,384]{0,1:T(8,128)(2,1)} async-done(((bf16[128,384]{0,1:T(8,128)(2,1)}), bf16[8192,384]{0,1:T(8,128)(2,1)}) %all-gather.9.cloned.1.call-update) | async-done | bytes 6291472 | tf_op jit(solution)/shard_map/all_gather | solution.py:82
  1003.9 80.6 %while.22 = (s32[]{:T(128)}, f32[128,3,1]{0,1,2:T(4,128)S(1)}, f32[128,3,1]{0,1,2:T(4,128)S(1)}, f32[128,3,1]{0,1,2:T(4,128)S(1)}, f32[128,3,128]{0,2,1:T(8,128)...) while((s32[]{:T(128)}, f32[128,3,1]{0,1,2:T(4,128)S(1)}, ...), condition=%wide.region_4.0_spmd.clone, body=%wide.region_0.0_spmd.clone.sunk | while | flops 609831936 | bytes 35326760 | solution.py:61
  1003.9 2.4 constant_dynamic-slice_fusion.6
  1006.3 1.7 bitcast_reduce_fusion.2
  1008.4 1.0 copy-done.1
  1010.2 1.5 constant_dynamic-slice_fusion.7
  1012.1 1.1 fusion.67
  1014.0 2.4 constant_dynamic-slice_fusion.6
  1016.4 1.7 bitcast_reduce_fusion.2
  1018.5 1.0 copy-done.1
  1020.3 1.5 constant_dynamic-slice_fusion.7
  1022.2 1.1 fusion.67
  1024.0 2.4 constant_dynamic-slice_fusion.6
  1026.4 1.7 bitcast_reduce_fusion.2
  1030.4 1.5 constant_dynamic-slice_fusion.7
  1032.3 1.1 fusion.67
  1034.1 2.4 constant_dynamic-slice_fusion.6
  1036.5 1.7 bitcast_reduce_fusion.2
  1040.4 1.5 constant_dynamic-slice_fusion.7
  1042.4 1.1 fusion.67
  1044.2 2.4 constant_dynamic-slice_fusion.6
  1046.6 1.7 bitcast_reduce_fusion.2
  1050.5 1.5 constant_dynamic-slice_fusion.7
  1052.4 1.1 fusion.67
  1054.3 2.4 constant_dynamic-slice_fusion.6
  1056.7 1.7 bitcast_reduce_fusion.2
  1060.6 1.5 constant_dynamic-slice_fusion.7
  1062.5 1.1 fusion.67
  1064.4 2.4 constant_dynamic-slice_fusion.6
  1066.8 1.7 bitcast_reduce_fusion.2
  1070.7 1.5 constant_dynamic-slice_fusion.7
  1072.6 1.1 fusion.67
  1074.4 2.4 constant_dynamic-slice_fusion.6
  1076.8 1.7 bitcast_reduce_fusion.2
  1080.8 1.5 constant_dynamic-slice_fusion.7
  1082.7 1.1 fusion.67
  1084.5 1.0 fusion.10
  1086.7 1.9 pad_maximum_fusion
  1088.6 95.1 %all-reduce.1 = bf16[128,6144]{1,0:T(8,128)(2,1)} all-reduce(f32[128,6144]{1,0:T(8,128)} %pad_maximum_fusion), channel_id=1, replica_groups=mesh['blk'=64,'head'=4] {'head'}, use_global_device_ids=true, to_apply=%region_5.0 | all-reduce | flops 786432 | bytes 4718592 | tf_op jit(solution)/shard_map/psum | solution.py:93
  1183.7 1.0 dynamic-slice_convert_fusion
  (134 shorter events, 27.2 us)
Async XLA Ops:
  7.2 1078.3 %copy-start = (bf16[384,3072]{1,0:T(8,128)(2,1)S(1)}, bf16[384,3072]{1,0:T(8,128)(2,1)}, u32[]{:S(2)}) copy-start(bf16[384,3072]{1,0:T(8,128)(2,1)} %param.15) | copy-start | bytes 7077892
  7.2 8.2 copy-start.4
  7.2 227.8 %all-gather.11.cloned.1.call-start = ((), (), s32[]{:S(2)}) async-start(), calls=%async_computation.3 | async-start | bytes 6389760 | tf_op jit(solution)/shard_map/all_gather | solution.py:84
  9.0 482.7 %all-gather.5.cloned.1.call-start = ((), (), s32[]{:S(2)}) async-start(), calls=%async_computation | async-start | bytes 6389760 | tf_op jit(solution)/shard_map/all_gather | solution.py:81
  10.8 737.1 %all-gather.7.cloned.1.call-start = ((), (), s32[]{:S(2)}) async-start(), calls=%async_computation.1 | async-start | bytes 6389760 | tf_op jit(solution)/shard_map/all_gather | solution.py:83
  12.5 991.4 %all-gather.9.cloned.1.call-start = ((), (), s32[]{:S(2)}) async-start(), calls=%async_computation.2 | async-start | bytes 6389760 | tf_op jit(solution)/shard_map/all_gather | solution.py:82
  1007.9 1.4 copy-start.1
  1007.9 1.6 copy-start.2
  1010.2 1.6 copy-start.3
  1018.0 1.4 copy-start.1
  1018.0 1.6 copy-start.2
  1020.3 1.6 copy-start.3
  1028.1 1.4 copy-start.1
  1028.1 1.6 copy-start.2
  1030.3 1.6 copy-start.3
  1038.2 1.4 copy-start.1
  1038.2 1.6 copy-start.2
  1040.4 1.6 copy-start.3
  1048.3 1.4 copy-start.1
  1048.3 1.6 copy-start.2
  1050.5 1.6 copy-start.3
  1058.3 1.4 copy-start.1
  1058.3 1.6 copy-start.2
  1060.6 1.6 copy-start.3
  1068.4 1.4 copy-start.1
  1068.4 1.6 copy-start.2
  1070.7 1.6 copy-start.3
  1078.5 1.4 copy-start.1
  1078.5 1.6 copy-start.2
  1080.7 1.6 copy-start.3
Sparse Core Ops, SparseCore 0:
  9.7 225.2 all-gather.10
  237.3 254.3 all-gather.4
  493.4 254.3 all-gather.6
  749.4 254.3 all-gather.8
where the time goes:
time: 1190 us
  waiting for transfers between devices  988 us (83%)
  blocking collectives  95.1 us (8%)
  local copies, waits for them, and re-layouts  50.7 us (4%)
  matrix products  38.4 us (3%)
  between operations  13.9 us (1%)
    all_gather x1, waiting for transfers between devices, on_device(): lax.all_gather(keys, 'blk', axis=0, tiled=True)  257 us
    all_gather x1, waiting for transfers between devices, on_device(): lax.all_gather(tan_keys, 'blk', axis=0, tiled=True)  256 us
    all_gather x1, waiting for transfers between devices, on_device(): lax.all_gather(values, 'blk', axis=0, tiled=True)  256 us
    all_gather x1, waiting for transfers between devices, on_device(): lax.all_gather(tan_values, 'blk', axis=0, tiled=True)  219 us
    psum x1, blocking collectives, on_device(): lax.psum(jnp.concatenate([jnp.dot(out_rows, out_weight, preferred_element...  95.1 us
    dynamic_slice x16, local copies, waits for them, and re-layouts, advance(): lax.dynamic_slice_in_dim(tensor_part, block_index * block_span, block_spa...  31.5 us
  transfers between devices with their start and end apart: 4, of which 4 were waited for; matrix products, arithmetic and copies ran while one was open for 1% of the time, Pallas kernels for 0%

commit v1 on v0

v1 whole, which is shorter than its diff:
```python
import functools
import math

import jax
import jax.numpy as jnp
from jax import lax
from jax.experimental import pallas as pl
from jax.experimental.pallas import tpu as pltpu
from jax.sharding import Mesh, PartitionSpec as P

DH = 128
NH = 3
TB = 128
SCALE = 1.0 / math.sqrt(DH)
SCALE2 = SCALE * math.log2(math.e)
SIZES = {"xlo": 2, "z": 8, "y": 4, "xhi": 2, "core": 2}
AXES = ("xlo", "z", "y", "xhi", "core")
PART = 2 * NH * 32 + 16
F32, BF16 = jnp.float32, jnp.bfloat16
VMEM = pl.BlockSpec(memory_space=pltpu.VMEM)
SMEM = pl.BlockSpec(memory_space=pltpu.SMEM)


def shift(x, axis, by):
    n = SIZES[axis]
    return lax.ppermute(x, axis, [(i, (i + by) % n) for i in range(n)])


def mm(a, b):
    return jnp.dot(a, b, preferred_element_type=F32)


def pack_kernel(q, k, v, tq, tk, tv, kp, qp):
    for h in range(NH):
        cols = slice(h * DH, (h + 1) * DH)
        kp[2 * h] = k[:, cols]
        kp[2 * h + 1] = tk[:, cols]
        kp[2 * NH + 2 * h] = v[:, cols].T
        kp[2 * NH + 2 * h + 1] = tv[:, cols].T
        qp[2 * h] = q[:, cols].T
        qp[2 * h + 1] = tq[:, cols].T


def pack(q, k, v, tq, tk, tv):
    return pl.pallas_call(
        pack_kernel,
        out_shape=(
            jax.ShapeDtypeStruct((4 * NH, TB, DH), BF16),
            jax.ShapeDtypeStruct((2 * NH, DH, TB), BF16),
        ),
        in_specs=[VMEM] * 6,
        out_specs=(VMEM, VMEM),
        name="pack",
    )(q, k, v, tq, tk, tv)


def unit(qs, ks, vs, s, h):
    q = jnp.concatenate([qs[s][0, 2 * h], qs[s][1, 2 * h]], axis=1)
    tq = jnp.concatenate([qs[s][0, 2 * h + 1], qs[s][1, 2 * h + 1]], axis=1)
    k = jnp.concatenate([r[2 * h] for r in ks], axis=0)
    tk = jnp.concatenate([r[2 * h + 1] for r in ks], axis=0)
    scores = mm(k, q)
    tan = mm(jnp.concatenate([k, tk], axis=1), jnp.concatenate([tq, q], axis=0))
    return scores, tan


def attend_kernel(nk, first, last, *refs):
    refs = list(refs)
    pos = refs.pop(0) if last else None
    qs = [refs.pop(0) for _ in range(4)]
    if nk == 0:
        kparts, vparts, vbase = [refs.pop(0)], [refs.pop(0)], 0
    else:
        kparts = [refs.pop(0) for _ in range(nk)]
        vparts, vbase = kparts, 2 * NH
    if not first:
        acc_in, st_in = refs.pop(0), refs.pop(0)
    if last:
        (out,) = refs
    else:
        acc_out, st_out = refs
    for s in range(4):
        stat_rows = [[], []]
        for h in range(NH):
            scores, tan = unit(qs, kparts, vparts, s, h)
            top = jnp.max(scores, axis=0, keepdims=True) * SCALE2
            if not first:
                st = st_in[s, h]
                old = st[0:1]
                top = jnp.maximum(old, top)
                keep = jnp.exp2(old - top)
            w = jnp.exp2(scores * SCALE2 - top)
            tw = w * tan
            den = jnp.sum(w, axis=0, keepdims=True)
            tden = jnp.sum(tw, axis=0, keepdims=True)
            wl, twl = w.astype(BF16), tw.astype(BF16)
            v = jnp.concatenate([r[vbase + 2 * h] for r in vparts], axis=1)
            tv = jnp.concatenate([r[vbase + 2 * h + 1] for r in vparts], axis=1)
            both = mm(jnp.concatenate([v, tv], axis=0), wl)
            a = both[:DH]
            b = both[DH:] + mm(v, twl) * SCALE
            if not first:
                a = a + acc_in[s, h, :DH] * keep
                b = b + acc_in[s, h, DH:] * keep
                den = den + st[1:2] * keep
                tden = tden + st[2:3] * keep
            if not last:
                acc_out[s, h, :DH] = a
                acc_out[s, h, DH:] = b
                st_out[s, h] = jnp.concatenate([top, den, tden, jnp.zeros((5, 2 * TB), F32)], axis=0)
                continue
            inv = 1.0 / den
            ratio = tden * SCALE * inv
            o = a * inv
            t = b * inv - o * ratio
            lse = top + jnp.log2(den)
            l0 = lse.astype(BF16)
            rest = lse - l0.astype(F32)
            l1 = rest.astype(BF16)
            l2 = (rest - l1.astype(F32)).astype(BF16)
            r0 = ratio.astype(BF16)
            r1 = (ratio - r0.astype(F32)).astype(BF16)
            for x in range(2):
                lanes = slice(x * TB, (x + 1) * TB)
                place = pos[2 * s + x]
                ot = o[:, lanes].T.astype(BF16)
                tt = t[:, lanes].T.astype(BF16)
                for to in range(4):
                    rows = slice(to * 32, (to + 1) * 32)
                    out[place, to, 64 * h : 64 * h + 32] = ot[rows]
                    out[place, to, 64 * h + 32 : 64 * h + 64] = tt[rows]
                stat_rows[x] += [piece[:, lanes].astype(F32) for piece in (l0, l1, l2, r0, r1)]
        if last:
            for x in range(2):
                rows = jnp.concatenate(stat_rows[x] + [jnp.zeros((1, TB), F32)], axis=0).astype(BF16)
                for to in range(4):
                    out[pos[2 * s + x], to, 64 * NH : PART] = rows


def attend(qs, blocks, state=None, pos=None):
    halves = blocks[0].shape[0] == 2 * NH
    first, last = state is None, pos is not None
    nk = 0 if halves else len(blocks)
    keys = TB * max(nk, 1)
    operands = ([pos] if last else []) + list(qs) + list(blocks) + ([] if first else list(state))
    specs = ([SMEM] if last else []) + [VMEM] * (len(operands) - last)
    if last:
        out_shape = jax.ShapeDtypeStruct((8, 4, PART, DH), BF16)
        out_specs = VMEM
    else:
        out_shape = (
            jax.ShapeDtypeStruct((4, NH, 2 * DH, 2 * TB), F32),
            jax.ShapeDtypeStruct((4, NH, 8, 2 * TB), F32),
        )
        out_specs = (VMEM, VMEM)
    n = len(operands)
    alias = {} if first or last else {n - 2: 0, n - 1: 1}
    return pl.pallas_call(
        functools.partial(attend_kernel, nk, first, last),
        out_shape=out_shape,
        in_specs=specs,
        out_specs=out_specs,
        input_output_aliases=alias,
        compiler_params=pltpu.CompilerParams(vmem_limit_bytes=32 << 20),
        cost_estimate=pl.CostEstimate(
            flops=2 * 8 * TB * DH * NH * keys * 8, bytes_accessed=8 << 20, transcendentals=8 * TB * NH * keys
        ),
        name=f"attend{keys}",
    )(*operands)


def project_kernel(me, got, w0, w1, w2, w3, out, tan_out, cols, rows):
    @pl.when(pl.program_id(0) == 0)
    def _():
        share, tilt = [], []
        for g in range(4):
            st = got[:, lax.bitwise_xor(me[0], g), 64 * NH : PART].astype(F32)
            for h in range(NH):
                lse = st[:, 5 * h] + st[:, 5 * h + 1] + st[:, 5 * h + 2]
                ratio = st[:, 5 * h + 3] + st[:, 5 * h + 4]
                w = jnp.exp2(lse - jnp.max(lse, axis=0, keepdims=True))
                w = w / jnp.sum(w, axis=0, keepdims=True)
                share.append(w)
                tilt.append(w * (ratio - jnp.sum(w * ratio, axis=0, keepdims=True)))
        pad = jnp.zeros((32, TB), F32)
        cols[:, :128] = jnp.concatenate(share + [pad], axis=0).T
        cols[:, 128:] = jnp.concatenate(tilt + [pad], axis=0).T
        mine = cols[pl.ds(pl.multiple_of(me[0] * 32, 32), 32)]
        for g in range(4):
            j = lax.bitwise_xor(me[0], g)
            for h in range(NH):
                o = t = None
                for i in range(8):
                    c = (g * NH + h) * 8 + i
                    oi = got[i, j, 64 * h : 64 * h + 32].astype(F32)
                    ti = got[i, j, 64 * h + 32 : 64 * h + 64].astype(F32)
                    a, b = mine[:, c : c + 1], mine[:, 128 + c : 129 + c]
                    o = oi * a if o is None else o + oi * a
                    t = ti * a + oi * b if t is None else t + (ti * a + oi * b)
                rows[g, :32, h * DH : (h + 1) * DH] = o.astype(BF16)
                rows[g, 32:, h * DH : (h + 1) * DH] = t.astype(BF16)

    total = mm(rows[0], w0[...]) + mm(rows[1], w1[...]) + mm(rows[2], w2[...]) + mm(rows[3], w3[...])
    out[...] = total[:32].astype(BF16)
    tan_out[...] = total[32:].astype(BF16)


def project(me, got, weights):
    depth, width = weights[0].shape
    step = 512
    wspec = pl.BlockSpec((depth, step), lambda i: (0, i))
    ospec = pl.BlockSpec((32, step), lambda i: (0, i))
    oshape = jax.ShapeDtypeStruct((32, width), BF16)
    return pl.pallas_call(
        project_kernel,
        out_shape=(oshape, oshape),
        grid=(width // step,),
        in_specs=[SMEM, pl.BlockSpec((8, 4, PART, DH), lambda i: (0, 0, 0, 0))] + [wspec] * 4,
        out_specs=(ospec, ospec),
        scratch_shapes=[pltpu.VMEM((TB, 256), F32), pltpu.VMEM((4, 64, NH * DH), BF16)],
        compiler_params=pltpu.CompilerParams(vmem_limit_bytes=32 << 20),
        cost_estimate=pl.CostEstimate(
            flops=2 * 64 * 4 * depth * width, bytes_accessed=4 * depth * width * 2, transcendentals=0
        ),
        name="project",
    )(me, got, *weights)


def on_device(queries, keys, values, tan_queries, tan_keys, tan_values, out_weight):
    xlo, y = lax.axis_index("xlo"), lax.axis_index("y")
    me = lax.axis_index("xhi") * 2 + lax.axis_index("core")
    kp, qp = pack(queries, keys, values, tan_queries, tan_keys, tan_values)

    right, left = [kp], [kp]
    for _ in range(3):
        right.append(shift(right[-1], "z", 1))
        left.append(shift(left[-1], "z", -1))
    far = (shift(right[-1][: 2 * NH], "z", 1), shift(left[-1][2 * NH :], "z", -1))

    q0 = jnp.stack([qp, shift(qp, "xlo", 1)])
    qs = (q0, shift(q0, "y", 1), shift(q0, "y", -1), shift(q0, "y", 2))
    pos = jnp.stack([(xlo ^ x) * 4 + (y + d) % 4 for d in (0, 3, 1, 2) for x in (0, 1)]).astype(jnp.int32)

    across = lax.ppermute(out_weight, ("xlo", "xhi"), [(2, 1), (1, 2), (3, 0), (0, 3)])
    weights = (out_weight, shift(out_weight, "core", 1), across, shift(across, "core", 1))

    state = attend(qs, (kp, right[1], left[1]))
    state = attend(qs, (right[2], left[2]), state)
    state = attend(qs, (right[3], left[3]), state)
    sent = attend(qs, far, state, pos)
    got = lax.all_to_all(sent.reshape(32, PART, DH), ("xlo", "y", "xhi", "core"), 0, 0, tiled=True)
    return project(jnp.reshape(me, (1,)).astype(jnp.int32), got.reshape(8, 4, PART, DH), weights)


def solution(mesh):
    fine = Mesh(mesh.devices.reshape([SIZES[a] for a in AXES]), AXES)
    blk, head = ("xlo", "z", "y"), ("xhi", "core")
    spec = P(blk, head)
    return jax.shard_map(
        on_device,
        mesh=fine,
        in_specs=(spec,) * 6 + (P(head, None),),
        out_specs=(P(blk + head, None),) * 2,
        check_vma=False,
    )
```

time: 1190 us -> 125 us (0.11)
  waiting for transfers between devices: 988 us -> 43.8 us
  blocking collectives: 95.1 us -> 0 us
  local copies, waits for them, and re-layouts: 50.7 us -> 2.77 us
  starting transfers between devices: 0.16 us -> 46.5 us
  matrix products: 38.4 us -> 0 us
  Pallas kernels: 0 us -> 30.1 us
  between operations: 13.9 us -> 0.74 us
    all_gather x4 -> x0, waiting for transfers between devices: 988 us -> none  [the longest x1 257 us: on_device(): lax.all_gather(keys, 'blk', axis=0, tiled=True)]
    psum x1 -> x0, blocking collectives: 95.1 us -> none  [on_device(): lax.psum(jnp.concatenate([jnp.dot(out_rows, out_weight, preferred_element...]
    ppermute x0 -> x15, starting transfers between devices: none -> 39.4 us  [the longest x14 36 us: shift(): return lax.ppermute(x, axis, [(i, (i + by) % n) for i in range(n)])]
    dot_general x50 -> x0, matrix products: 38.4 us -> none  [the longest x8 13.2 us: absorb_block(): jnp.einsum('thd,shd->ths', queries3, keys3, preferred_element_type=jnp.fl...]
    dynamic_slice x16 -> x0, local copies, waits for them, and re-layouts: 31.5 us -> none  [advance(): lax.dynamic_slice_in_dim(tensor_part, block_index * block_span, block_spa...]
    pallas_call x0 -> x6, Pallas kernels: none -> 30.1 us  [the longest x4 20.3 us: attend(): pl.pallas_call(functools.partial(attend_kernel, nk, first, last), out_sha...]
    all_to_all x0 -> x1, waiting for transfers between devices: none -> 24.1 us  [on_device(): lax.all_to_all(sent.reshape(32, PART, DH), ('xlo', 'y', 'xhi', 'core'), 0...]
    ppermute x0 -> x15, waiting for transfers between devices: none -> 19.7 us  [the longest x1 11.1 us: on_device(): lax.ppermute(out_weight, ('xlo', 'xhi'), [(2, 1), (1, 2), (3, 0), (0, 3)])]
  transfers between devices with their start and end apart: 4 -> 16, of which waited for: 4 -> 5; matrix products, arithmetic and copies ran while one was open for 1% -> 1% of each run, Pallas kernels for 0% -> 18%
where the time goes in v1:
time: 125 us
  starting transfers between devices  46.5 us (37%)
  waiting for transfers between devices  43.8 us (35%)
  Pallas kernels  30.1 us (24%)
  local copies, waits for them, and re-layouts  2.77 us (2%)
    ppermute x14, starting transfers between devices, shift(): return lax.ppermute(x, axis, [(i, (i + by) % n) for i in range(n)])  36 us
    all_to_all x1, waiting for transfers between devices, on_device(): lax.all_to_all(sent.reshape(32, PART, DH), ('xlo', 'y', 'xhi', 'core'), 0...  24.1 us
    pallas_call x4, Pallas kernels, attend(): pl.pallas_call(functools.partial(attend_kernel, nk, first, last), out_sha...  20.3 us
    ppermute x1, waiting for transfers between devices, on_device(): lax.ppermute(out_weight, ('xlo', 'xhi'), [(2, 1), (1, 2), (3, 0), (0, 3)])  11.1 us
    ppermute x14, waiting for transfers between devices, shift(): return lax.ppermute(x, axis, [(i, (i + by) % n) for i in range(n)])  8.54 us
    pallas_call x1, Pallas kernels, project(): pl.pallas_call(project_kernel, out_shape=(oshape, oshape), grid=(width //...  7.78 us
    all_to_all x1, starting transfers between devices, on_device(): lax.all_to_all(sent.reshape(32, PART, DH), ('xlo', 'y', 'xhi', 'core'), 0...  7.1 us
    ppermute x1, starting transfers between devices, on_device(): lax.ppermute(out_weight, ('xlo', 'xhi'), [(2, 1), (1, 2), (3, 0), (0, 3)])  3.39 us
  transfers between devices with their start and end apart: 16, of which 5 were waited for; matrix products, arithmetic and copies ran while one was open for 1% of the time, Pallas kernels for 18%

profile of v1, /device:TPU:1, one launch (start us, length us, event | category | flops | bytes accessed | tf_op | source)
XLA Modules:
  0.0 124.9 jit_solution(16488531235765805981)
XLA Ops:
  0.6 3.4 %collective-permute-start.13 = (bf16[384,3072]{1,0:T(8,128)(2,1)}, bf16[384,3072]{1,0:T(8,128)(2,1)}, u32[]{:S(2)}, u32[]{:S(2)}) collective-permute-start(bf16[384,3072]{1,0:T(8,128)(2,1)} %w0.1), channel_id=1, source_target_pairs={{128,2},{2,128},{130,0},{0,130},{129,3},{3,129},{131,1},{1,131},{1... | collective-permute-start | bytes 7077896 | tf_op jit(solution)/shard_map/ppermute | solution.py:244
  4.0 2.1 %pack.1 = (bf16[12,128,128]{2,1,0:T(8,128)(2,1)}, bf16[6,128,128]{2,1,0:T(8,128)(2,1)}) custom-call(bf16[128,384]{1,0:T(8,128)(2,1)} %q.1, bf16[128,384]{1,0:T(8,128)(2,1)} %k.1, bf16[128,384]{1,0:T(8,128)(2,1)} %v.1, bf16[128,384]{1,0:T(8,128)(2,1)} %tq.1, bf16[128,384]{1,0:T(8,128)(2,1)} %tk.1, bf16[128,384]{1,0:T(8,128)(2,1)} %tv.1), custom_call_target="tpu_custom_call" | custom-call | tf_op jit(solution)/shard_map/pack/pallas_call | solution.py:45
  6.1 0.0 collective-permute-start
  6.1 5.6 %collective-permute-start.8 = (bf16[12,128,128]{2,1,0:T(8,128)(2,1)}, bf16[12,128,128]{2,1,0:T(8,128)(2,1)S(1)}, u32[]{:S(2)}, u32[]{:S(2)}) collective-permute-start(bf16[12,128,128]{2,1,0:T(8,128)(2,1)} %get-tuple-element.11.refs_4_), channel_id=1, source_target_pairs={{0,112},{16,0},{32,16},{48,32},{64,48},{80,64},{96,80},{112,96},{1... | collective-permute-start | bytes 1179656 | tf_op jit(solution)/shard_map/ppermute | solution.py:26
  11.7 0.0 collective-permute-start.4
  11.7 0.2 collective-permute-done
  11.9 1.0 pad_maximum_fusion.refs_0_.refs_1_
  12.8 1.4 %collective-permute-start.1 = (bf16[2,6,128,128]{3,2,1,0:T(8,128)(2,1)S(1)}, bf16[2,6,128,128]{3,2,1,0:T(8,128)(2,1)S(1)}, u32[]{:S(2)}, u32[]{:S(2)}) collective-permute-start(bf16[2,6,128,128]{3,2,1,0:T(8,128)(2,1)S(1)} %pad_maximum_fusion.refs_0_.refs_1_), channel_id=1, source_target_pairs={{0,4},{4,8},{8,12},{12,0},{1,5},{5,9},{9,13},{13,1},{2,6},{6,10},{... | collective-permute-start | bytes 1179656 | tf_op jit(solution)/shard_map/ppermute | solution.py:26
  14.2 5.0 %collective-permute-done.8.refs_6_ = bf16[12,128,128]{2,1,0:T(8,128)(2,1)S(1)} collective-permute-done((bf16[12,128,128]{2,1,0:T(8,128)(2,1)}, bf16[12,128,128]{2,1,0:T(8,128)(2,1)S(1)}, u32[]{:S(2)}, u32[]{:S(2)}) %collective-permute-start.8) | collective-permute-done | bytes 393248 | tf_op jit(solution)/shard_map/ppermute | solution.py:26
  19.2 3.4 %collective-permute-start.9 = (bf16[12,128,128]{2,1,0:T(8,128)(2,1)S(1)}, bf16[12,128,128]{2,1,0:T(8,128)(2,1)S(1)}, u32[]{:S(2)}, u32[]{:S(2)}) collective-permute-start(bf16[12,128,128]{2,1,0:T(8,128)(2,1)S(1)} %collective-permute-done.8.refs_6_), channel_id=1, source_target_pairs={{0,112},{16,0},{32,16},{48,32},{64,48},{80,64},{96,80},{112,96},{1... | collective-permute-start | bytes 1179656 | tf_op jit(solution)/shard_map/ppermute | solution.py:26
  22.6 0.0 collective-permute-done.4.refs_5_
  22.6 0.0 collective-permute-start.5
  22.6 2.7 %collective-permute-start.2 = (bf16[2,6,128,128]{3,2,1,0:T(8,128)(2,1)S(1)}, bf16[2,6,128,128]{3,2,1,0:T(8,128)(2,1)S(1)}, u32[]{:S(2)}, u32[]{:S(2)}) collective-permute-start(bf16[2,6,128,128]{3,2,1,0:T(8,128)(2,1)S(1)} %pad_maximum_fusion.refs_0_.refs_1_), channel_id=1, source_target_pairs={{0,12},{4,0},{8,4},{12,8},{1,13},{5,1},{9,5},{13,9},{2,14},{6,2},{... | collective-permute-start | bytes 1179656 | tf_op jit(solution)/shard_map/ppermute | solution.py:26
  25.4 0.0 collective-permute-done.1.refs_1_.refs_2_
  25.4 0.3 collective-permute-start.3
  25.7 3.3 %collective-permute-done.9.refs_5_ = bf16[12,128,128]{2,1,0:T(8,128)(2,1)S(1)} collective-permute-done((bf16[12,128,128]{2,1,0:T(8,128)(2,1)S(1)}, bf16[12,128,128]{2,1,0:T(8,128)(2,1)S(1)}, u32[]{:S(2)}, u32[]{:S(2)}) %collective-permute-start.9) | collective-permute-done | bytes 393248 | tf_op jit(solution)/shard_map/ppermute | solution.py:26
  29.0 3.5 %collective-permute-start.10 = (bf16[12,128,128]{2,1,0:T(8,128)(2,1)S(1)}, bf16[12,128,128]{2,1,0:T(8,128)(2,1)S(1)}, u32[]{:S(2)}, u32[]{:S(2)}) collective-permute-start(bf16[12,128,128]{2,1,0:T(8,128)(2,1)S(1)} %collective-permute-done.9.refs_5_), channel_id=1, source_target_pairs={{0,112},{16,0},{32,16},{48,32},{64,48},{80,64},{96,80},{112,96},{1... | collective-permute-start | bytes 1179656 | tf_op jit(solution)/shard_map/ppermute | solution.py:26
  32.6 0.0 collective-permute-done.5.refs_4_
  32.6 0.0 collective-permute-start.6
  32.6 0.0 collective-permute-done.2.refs_2_.refs_3_
  32.6 10.6 %collective-permute-start.12 = (bf16[384,3072]{1,0:T(8,128)(2,1)}, bf16[384,3072]{1,0:T(8,128)(2,1)}, u32[]{:S(2)}, u32[]{:S(2)}) collective-permute-start(bf16[384,3072]{1,0:T(8,128)(2,1)} %w0.1), channel_id=1, source_target_pairs={{0,1},{1,0},{2,3},{3,2},{4,5},{5,4},{6,7},{7,6},{8,9},{9,8},{10,11... | collective-permute-start | bytes 7077896 | tf_op jit(solution)/shard_map/ppermute | solution.py:26
  43.1 11.1 %collective-permute-done.13.w2 = bf16[384,3072]{1,0:T(8,128)(2,1)} collective-permute-done((bf16[384,3072]{1,0:T(8,128)(2,1)}, bf16[384,3072]{1,0:T(8,128)(2,1)}, u32[]{:S(2)}, u32[]{:S(2)}) %collective-permute-start.13) | collective-permute-done | bytes 2359328 | tf_op jit(solution)/shard_map/ppermute | solution.py:244
  54.3 2.3 %collective-permute-start.14 = (bf16[384,3072]{1,0:T(8,128)(2,1)}, bf16[384,3072]{1,0:T(8,128)(2,1)}, u32[]{:S(2)}, u32[]{:S(2)}) collective-permute-start(bf16[384,3072]{1,0:T(8,128)(2,1)} %collective-permute-done.13.w2), channel_id=1, source_target_pairs={{0,1},{1,0},{2,3},{3,2},{4,5},{5,4},{6,7},{7,6},{8,9},{9,8},{10,11... | collective-permute-start | bytes 7077896 | tf_op jit(solution)/shard_map/ppermute | solution.py:26
  56.5 0.1 stack.44.refs_0_
  56.6 0.0 collective-permute-done.3.refs_3_.refs_4_
  56.6 0.0 copy-start.1
  56.6 1.0 copy-done.1
  57.6 5.3 %attend384.1 = (f32[4,3,256,256]{3,2,1,0:T(8,128)S(1)}, f32[4,3,8,256]{3,2,1,0:T(8,128)S(1)}) custom-call(bf16[2,6,128,128]{3,2,1,0:T(8,128)(2,1)S(1)} %pad_maximum_fusion.refs_0_.refs_1_, bf16[2,6,128,128]{3,2,1,0:T(8,128)(2,1)S(1)} %collective-permute-done.1.refs_1_.refs_2_, bf16[2,6,128,128]{3,2,1,0:T(8,128)(2,1)S(1)} %collective-permute-done.2.refs_2_.refs_3_, ...), custom_call_target="tpu_custom_call" | custom-call | flops 2415919104 | bytes 8388608 | tf_op jit(solution)/shard_map/attend384/pallas_call | solution.py:158
  63.0 0.0 collective-permute-done.10.refs_5_
  63.0 5.8 %collective-permute-start.11 = (bf16[6,128,128]{2,1,0:T(8,128)(2,1)S(1)}, bf16[6,128,128]{2,1,0:T(8,128)(2,1)S(1)}, u32[]{:S(2)}, u32[]{:S(2)}) collective-permute-start(bf16[6,128,128]{2,1,0:T(8,128)(2,1)S(1)} %slice.9), channel_id=1, source_target_pairs={{0,112},{16,0},{32,16},{48,32},{64,48},{80,64},{96,80},{112,96},{1... | collective-permute-start | bytes 589832 | tf_op jit(solution)/shard_map/ppermute | solution.py:26
  68.8 0.0 collective-permute-done.6.refs_4_
  68.9 0.3 collective-permute-start.7
  69.2 5.5 %attend256.2 = (f32[4,3,256,256]{3,2,1,0:T(8,128)S(1)}, f32[4,3,8,256]{3,2,1,0:T(8,128)S(1)}) custom-call(bf16[2,6,128,128]{3,2,1,0:T(8,128)(2,1)S(1)} %pad_maximum_fusion.refs_0_.refs_1_, bf16[2,6,128,128]{3,2,1,0:T(8,128)(2,1)S(1)} %collective-permute-done.1.refs_1_.refs_2_, ...), custom_call_target="tpu_custom_call", output_to_operand_aliasing={{0}: (6, {}), {1}: (7, {})} | custom-call | flops 1610612736 | bytes 8388608 | tf_op jit(solution)/shard_map/attend256/pallas_call | solution.py:158
  74.6 4.4 %attend256.3 = (f32[4,3,256,256]{3,2,1,0:T(8,128)S(1)}, f32[4,3,8,256]{3,2,1,0:T(8,128)S(1)}) custom-call(bf16[2,6,128,128]{3,2,1,0:T(8,128)(2,1)S(1)} %pad_maximum_fusion.refs_0_.refs_1_, bf16[2,6,128,128]{3,2,1,0:T(8,128)(2,1)S(1)} %collective-permute-done.1.refs_1_.refs_2_, ...), custom_call_target="tpu_custom_call", output_to_operand_aliasing={{0}: (6, {}), {1}: (7, {})} | custom-call | flops 1610612736 | bytes 8388608 | tf_op jit(solution)/shard_map/attend256/pallas_call | solution.py:158
  79.1 0.0 collective-permute-done.11.refs_6_
  79.1 0.0 collective-permute-done.7.refs_5_
  79.1 5.1 %attend128.1 = bf16[8,4,208,128]{3,2,1,0:T(8,128)(2,1)} custom-call(s32[8]{0:T(128)S(1)} %stack.44.refs_0_, bf16[2,6,128,128]{3,2,1,0:T(8,128)(2,1)S(1)} %pad_maximum_fusion.refs_0_.refs_1_, bf16[2,6,128,128]{3,2,1,0:T(8,128)(2,1)S(1)} %collective-permute-done.1.refs_1_.refs_2_, bf16[2,6,128,128]{3,2,1,0:T(8,128)(2,1)S(1)} %collective-permute-done.2.refs_2_.refs_3_, ...), custom_call_target="tpu_custom_call" | custom-call | flops 805306368 | bytes 8388608 | tf_op jit(solution)/shard_map/attend128/pallas_call | solution.py:158
  84.2 7.1 %all-to-all-start = ((bf16[32,208,128]{2,1,0:T(8,128)(2,1)}), bf16[32,208,128]{2,1,0:T(8,128)(2,1)S(1)}, u32[]{:S(2)}, u32[]{:S(2)}) async-start(bf16[32,208,128]{2,1,0:T(8,128)(2,1)} %bitcast.11), calls=%async_computation | async-start | bytes 3407872 | tf_op jit(solution)/shard_map/all_to_all | solution.py:251
  91.3 0.0 collective-permute-done.12.w1
  91.3 24.1 %all-to-all-done = bf16[32,208,128]{2,1,0:T(8,128)(2,1)S(1)} async-done(((bf16[32,208,128]{2,1,0:T(8,128)(2,1)}), bf16[32,208,128]{2,1,0:T(8,128)(2,1)S(1)}, u32[]{:S(2)}, u32[]{:S(2)}) %all-to-all-start) | async-done | bytes 1703968 | tf_op jit(solution)/shard_map/all_to_all | solution.py:251
  115.4 0.0 collective-permute-done.14.w3
  115.4 0.0 copy-start
  115.4 1.7 %copy-done = bf16[384,3072]{1,0:T(8,128)(2,1)S(1)} copy-done((bf16[384,3072]{1,0:T(8,128)(2,1)S(1)}, bf16[384,3072]{1,0:T(8,128)(2,1)}, u32[]{:S(2)}) %copy-start) | copy-done | bytes 2359320
  117.1 7.8 %project.1 = (bf16[32,3072]{1,0:T(8,128)(2,1)}, bf16[32,3072]{1,0:T(8,128)(2,1)}) custom-call(s32[1]{0:T(128)} %bitcast.me, bf16[8,4,208,128]{3,2,1,0:T(8,128)(2,1)S(1)} %bitcast.13, bf16[384,3072]{1,0:T(8,128)(2,1)S(1)} %copy-done, bf16[384,3072]{1,0:T(8,128)(2,1)} %collective-permute-done.12.w1, bf16[384,3072]{1,0:T(8,128)(2,1)} %collective-permute-done.13.w2, ...), custom_call_target="tpu_custom_call" | custom-call | flops 603979776 | bytes 9437184 | tf_op jit(solution)/shard_map/project/pallas_call | solution.py:214
  (2 shorter events, 0.0 us)
Async XLA Ops:
  0.6 53.6 %collective-permute-start.13 = (bf16[384,3072]{1,0:T(8,128)(2,1)}, bf16[384,3072]{1,0:T(8,128)(2,1)}, u32[]{:S(2)}, u32[]{:S(2)}) collective-permute-start(bf16[384,3072]{1,0:T(8,128)(2,1)} %w0.1), channel_id=1, source_target_pairs={{128,2},{2,128},{130,0},{0,130},{129,3},{3,129},{131,1},{1,131},{1... | collective-permute-start | bytes 7077896 | tf_op jit(solution)/shard_map/ppermute | solution.py:244
  6.1 5.8 %collective-permute-start = (bf16[6,128,128]{2,1,0:T(8,128)(2,1)}, bf16[6,128,128]{2,1,0:T(8,128)(2,1)S(1)}, u32[]{:S(2)}, u32[]{:S(2)}) collective-permute-start(bf16[6,128,128]{2,1,0:T(8,128)(2,1)} %get-tuple-element.10), channel_id=1, source_target_pairs={{0,128},{128,0},{1,129},{129,1},{2,130},{130,2},{3,131},{131,3},{4... | collective-permute-start | bytes 589832 | tf_op jit(solution)/shard_map/ppermute | solution.py:26
  6.1 13.1 %collective-permute-start.8 = (bf16[12,128,128]{2,1,0:T(8,128)(2,1)}, bf16[12,128,128]{2,1,0:T(8,128)(2,1)S(1)}, u32[]{:S(2)}, u32[]{:S(2)}) collective-permute-start(bf16[12,128,128]{2,1,0:T(8,128)(2,1)} %get-tuple-element.11.refs_4_), channel_id=1, source_target_pairs={{0,112},{16,0},{32,16},{48,32},{64,48},{80,64},{96,80},{112,96},{1... | collective-permute-start | bytes 1179656 | tf_op jit(solution)/shard_map/ppermute | solution.py:26
  11.7 11.0 %collective-permute-start.4 = (bf16[12,128,128]{2,1,0:T(8,128)(2,1)}, bf16[12,128,128]{2,1,0:T(8,128)(2,1)S(1)}, u32[]{:S(2)}, u32[]{:S(2)}) collective-permute-start(bf16[12,128,128]{2,1,0:T(8,128)(2,1)} %get-tuple-element.11.refs_4_), channel_id=1, source_target_pairs={{0,16},{16,32},{32,48},{48,64},{64,80},{80,96},{96,112},{112,0},{1... | collective-permute-start | bytes 1179656 | tf_op jit(solution)/shard_map/ppermute | solution.py:26
  12.8 12.5 %collective-permute-start.1 = (bf16[2,6,128,128]{3,2,1,0:T(8,128)(2,1)S(1)}, bf16[2,6,128,128]{3,2,1,0:T(8,128)(2,1)S(1)}, u32[]{:S(2)}, u32[]{:S(2)}) collective-permute-start(bf16[2,6,128,128]{3,2,1,0:T(8,128)(2,1)S(1)} %pad_maximum_fusion.refs_0_.refs_1_), channel_id=1, source_target_pairs={{0,4},{4,8},{8,12},{12,0},{1,5},{5,9},{9,13},{13,1},{2,6},{6,10},{... | collective-permute-start | bytes 1179656 | tf_op jit(solution)/shard_map/ppermute | solution.py:26
  19.2 9.8 %collective-permute-start.9 = (bf16[12,128,128]{2,1,0:T(8,128)(2,1)S(1)}, bf16[12,128,128]{2,1,0:T(8,128)(2,1)S(1)}, u32[]{:S(2)}, u32[]{:S(2)}) collective-permute-start(bf16[12,128,128]{2,1,0:T(8,128)(2,1)S(1)} %collective-permute-done.8.refs_6_), channel_id=1, source_target_pairs={{0,112},{16,0},{32,16},{48,32},{64,48},{80,64},{96,80},{112,96},{1... | collective-permute-start | bytes 1179656 | tf_op jit(solution)/shard_map/ppermute | solution.py:26
  22.6 9.9 %collective-permute-start.5 = (bf16[12,128,128]{2,1,0:T(8,128)(2,1)S(1)}, bf16[12,128,128]{2,1,0:T(8,128)(2,1)}, u32[]{:S(2)}, u32[]{:S(2)}) collective-permute-start(bf16[12,128,128]{2,1,0:T(8,128)(2,1)S(1)} %collective-permute-done.4.refs_5_), channel_id=1, source_target_pairs={{0,16},{16,32},{32,48},{48,64},{64,80},{80,96},{96,112},{112,0},{1... | collective-permute-start | bytes 1179656 | tf_op jit(solution)/shard_map/ppermute | solution.py:26
  22.6 9.9 %collective-permute-start.2 = (bf16[2,6,128,128]{3,2,1,0:T(8,128)(2,1)S(1)}, bf16[2,6,128,128]{3,2,1,0:T(8,128)(2,1)S(1)}, u32[]{:S(2)}, u32[]{:S(2)}) collective-permute-start(bf16[2,6,128,128]{3,2,1,0:T(8,128)(2,1)S(1)} %pad_maximum_fusion.refs_0_.refs_1_), channel_id=1, source_target_pairs={{0,12},{4,0},{8,4},{12,8},{1,13},{5,1},{9,5},{13,9},{2,14},{6,2},{... | collective-permute-start | bytes 1179656 | tf_op jit(solution)/shard_map/ppermute | solution.py:26
  25.4 31.3 %collective-permute-start.3 = (bf16[2,6,128,128]{3,2,1,0:T(8,128)(2,1)S(1)}, bf16[2,6,128,128]{3,2,1,0:T(8,128)(2,1)S(1)}, u32[]{:S(2)}, u32[]{:S(2)}) collective-permute-start(bf16[2,6,128,128]{3,2,1,0:T(8,128)(2,1)S(1)} %pad_maximum_fusion.refs_0_.refs_1_), channel_id=1, source_target_pairs={{0,8},{4,12},{8,0},{12,4},{1,9},{5,13},{9,1},{13,5},{2,10},{6,14},... | collective-permute-start | bytes 1179656 | tf_op jit(solution)/shard_map/ppermute | solution.py:26
  29.0 33.9 %collective-permute-start.10 = (bf16[12,128,128]{2,1,0:T(8,128)(2,1)S(1)}, bf16[12,128,128]{2,1,0:T(8,128)(2,1)S(1)}, u32[]{:S(2)}, u32[]{:S(2)}) collective-permute-start(bf16[12,128,128]{2,1,0:T(8,128)(2,1)S(1)} %collective-permute-done.9.refs_5_), channel_id=1, source_target_pairs={{0,112},{16,0},{32,16},{48,32},{64,48},{80,64},{96,80},{112,96},{1... | collective-permute-start | bytes 1179656 | tf_op jit(solution)/shard_map/ppermute | solution.py:26
  32.6 36.3 %collective-permute-start.6 = (bf16[12,128,128]{2,1,0:T(8,128)(2,1)}, bf16[12,128,128]{2,1,0:T(8,128)(2,1)S(1)}, u32[]{:S(2)}, u32[]{:S(2)}) collective-permute-start(bf16[12,128,128]{2,1,0:T(8,128)(2,1)} %collective-permute-done.5.refs_4_), channel_id=1, source_target_pairs={{0,16},{16,32},{32,48},{48,64},{64,80},{80,96},{96,112},{112,0},{1... | collective-permute-start | bytes 1179656 | tf_op jit(solution)/shard_map/ppermute | solution.py:26
  32.6 58.7 %collective-permute-start.12 = (bf16[384,3072]{1,0:T(8,128)(2,1)}, bf16[384,3072]{1,0:T(8,128)(2,1)}, u32[]{:S(2)}, u32[]{:S(2)}) collective-permute-start(bf16[384,3072]{1,0:T(8,128)(2,1)} %w0.1), channel_id=1, source_target_pairs={{0,1},{1,0},{2,3},{3,2},{4,5},{5,4},{6,7},{7,6},{8,9},{9,8},{10,11... | collective-permute-start | bytes 7077896 | tf_op jit(solution)/shard_map/ppermute | solution.py:26
  54.3 61.2 %collective-permute-start.14 = (bf16[384,3072]{1,0:T(8,128)(2,1)}, bf16[384,3072]{1,0:T(8,128)(2,1)}, u32[]{:S(2)}, u32[]{:S(2)}) collective-permute-start(bf16[384,3072]{1,0:T(8,128)(2,1)} %collective-permute-done.13.w2), channel_id=1, source_target_pairs={{0,1},{1,0},{2,3},{3,2},{4,5},{5,4},{6,7},{7,6},{8,9},{9,8},{10,11... | collective-permute-start | bytes 7077896 | tf_op jit(solution)/shard_map/ppermute | solution.py:26
  56.6 1.0 copy-start.1
  63.0 16.1 %collective-permute-start.11 = (bf16[6,128,128]{2,1,0:T(8,128)(2,1)S(1)}, bf16[6,128,128]{2,1,0:T(8,128)(2,1)S(1)}, u32[]{:S(2)}, u32[]{:S(2)}) collective-permute-start(bf16[6,128,128]{2,1,0:T(8,128)(2,1)S(1)} %slice.9), channel_id=1, source_target_pairs={{0,112},{16,0},{32,16},{48,32},{64,48},{80,64},{96,80},{112,96},{1... | collective-permute-start | bytes 589832 | tf_op jit(solution)/shard_map/ppermute | solution.py:26
  68.9 10.2 %collective-permute-start.7 = (bf16[6,128,128]{2,1,0:T(8,128)(2,1)S(1)}, bf16[6,128,128]{2,1,0:T(8,128)(2,1)S(1)}, u32[]{:S(2)}, u32[]{:S(2)}) collective-permute-start(bf16[6,128,128]{2,1,0:T(8,128)(2,1)S(1)} %slice.8), channel_id=1, source_target_pairs={{0,16},{16,32},{32,48},{48,64},{64,80},{80,96},{96,112},{112,0},{1... | collective-permute-start | bytes 589832 | tf_op jit(solution)/shard_map/ppermute | solution.py:26
  84.2 31.2 %all-to-all-start = ((bf16[32,208,128]{2,1,0:T(8,128)(2,1)}), bf16[32,208,128]{2,1,0:T(8,128)(2,1)S(1)}, u32[]{:S(2)}, u32[]{:S(2)}) async-start(bf16[32,208,128]{2,1,0:T(8,128)(2,1)} %bitcast.11), calls=%async_computation | async-start | bytes 3407872 | tf_op jit(solution)/shard_map/all_to_all | solution.py:251
  115.4 1.7 %copy-start = (bf16[384,3072]{1,0:T(8,128)(2,1)S(1)}, bf16[384,3072]{1,0:T(8,128)(2,1)}, u32[]{:S(2)}) copy-start(bf16[384,3072]{1,0:T(8,128)(2,1)} %w0.1) | copy-start | bytes 7077892

commit v2 on v1

v2 whole, which is shorter than its diff:
```python
import functools
import math

import jax
import jax.numpy as jnp
from jax import lax
from jax.experimental import pallas as pl
from jax.experimental.pallas import tpu as pltpu
from jax.sharding import Mesh, PartitionSpec as P

DH = 128
NH = 3
TB = 128
SCALE = 1.0 / math.sqrt(DH)
SCALE2 = SCALE * math.log2(math.e)
SIZES = {"xlo": 2, "z": 8, "y": 4, "xhi": 2, "core": 2}
AXES = ("xlo", "z", "y", "xhi", "core")
PART = 2 * NH * 32 + 16
F32, BF16 = jnp.float32, jnp.bfloat16
VMEM = pl.BlockSpec(memory_space=pltpu.VMEM)
SMEM = pl.BlockSpec(memory_space=pltpu.SMEM)


def shift(x, axis, by):
    n = SIZES[axis]
    return lax.ppermute(x, axis, [(i, (i + by) % n) for i in range(n)])


def mm(a, b):
    return jnp.dot(a, b, preferred_element_type=F32)


def pack_kernel(q, k, v, tq, tk, tv, kp, qp):
    for h in range(NH):
        cols = slice(h * DH, (h + 1) * DH)
        kp[2 * h] = k[:, cols]
        kp[2 * h + 1] = tk[:, cols]
        kp[2 * NH + 2 * h] = v[:, cols].T
        kp[2 * NH + 2 * h + 1] = tv[:, cols].T
        qp[2 * h] = q[:, cols].T
        qp[2 * h + 1] = tq[:, cols].T


def pack(q, k, v, tq, tk, tv):
    return pl.pallas_call(
        pack_kernel,
        out_shape=(
            jax.ShapeDtypeStruct((4 * NH, TB, DH), BF16),
            jax.ShapeDtypeStruct((2 * NH, DH, TB), BF16),
        ),
        in_specs=[VMEM] * 6,
        out_specs=(VMEM, VMEM),
        name="pack",
    )(q, k, v, tq, tk, tv)


def unit(qs, ks, vs, s, h):
    q = jnp.concatenate([qs[s][0, 2 * h], qs[s][1, 2 * h]], axis=1)
    tq = jnp.concatenate([qs[s][0, 2 * h + 1], qs[s][1, 2 * h + 1]], axis=1)
    k = jnp.concatenate([r[2 * h] for r in ks], axis=0)
    tk = jnp.concatenate([r[2 * h + 1] for r in ks], axis=0)
    scores = mm(k, q)
    tan = mm(jnp.concatenate([k, tk], axis=1), jnp.concatenate([tq, q], axis=0))
    return scores, tan


def attend_kernel(nk, first, last, *refs):
    refs = list(refs)
    at = refs.pop(0) if last else None
    qs = [refs.pop(0) for _ in range(4)]
    if nk == 0:
        kparts, vparts, vbase = [refs.pop(0)], [refs.pop(0)], 0
    else:
        kparts = [refs.pop(0) for _ in range(nk)]
        vparts, vbase = kparts, 2 * NH
    if not first:
        acc_in, st_in = refs.pop(0), refs.pop(0)
    if last:
        (out,) = refs
    else:
        acc_out, st_out = refs
    stat_rows = {}

    def block(s, x):
        return lax.bitwise_xor(at[0], x) * 4 + lax.bitwise_and(at[1] + (0, 3, 1, 2)[s], 3)

    def finish(s, h, scores, tan):
        top = jnp.max(scores, axis=0, keepdims=True) * SCALE2
        if not first:
            st = st_in[s, h]
            old = st[0:1]
            top = jnp.maximum(old, top)
            keep = jnp.exp2(old - top)
        w = jnp.exp2(scores * SCALE2 - top)
        tw = w * tan
        den = jnp.sum(w, axis=0, keepdims=True)
        tden = jnp.sum(tw, axis=0, keepdims=True)
        wl, twl = w.astype(BF16), tw.astype(BF16)
        v = jnp.concatenate([r[vbase + 2 * h] for r in vparts], axis=1)
        tv = jnp.concatenate([r[vbase + 2 * h + 1] for r in vparts], axis=1)
        both = mm(jnp.concatenate([v, tv], axis=0), wl)
        a = both[:DH]
        b = both[DH:] + mm(v, twl) * SCALE
        if not first:
            a = a + acc_in[s, h, :DH] * keep
            b = b + acc_in[s, h, DH:] * keep
            den = den + st[1:2] * keep
            tden = tden + st[2:3] * keep
        if not last:
            acc_out[s, h, :DH] = a
            acc_out[s, h, DH:] = b
            st_out[s, h] = jnp.concatenate([top, den, tden, jnp.zeros((5, 2 * TB), F32)], axis=0)
            return
        inv = 1.0 / den
        ratio = tden * SCALE * inv
        o = a * inv
        t = b * inv - o * ratio
        lse = top + jnp.log2(den)
        l0 = lse.astype(BF16)
        rest = lse - l0.astype(F32)
        l1 = rest.astype(BF16)
        l2 = (rest - l1.astype(F32)).astype(BF16)
        r0 = ratio.astype(BF16)
        r1 = (ratio - r0.astype(F32)).astype(BF16)
        for x in range(2):
            lanes = slice(x * TB, (x + 1) * TB)
            ot = o[:, lanes].astype(BF16).T
            tt = t[:, lanes].astype(BF16).T
            for to in range(4):
                rows = slice(to * 32, (to + 1) * 32)
                out[block(s, x), to, 64 * h : 64 * h + 32] = ot[rows]
                out[block(s, x), to, 64 * h + 32 : 64 * h + 64] = tt[rows]
            stat_rows.setdefault((s, x), []).extend(
                piece[:, lanes].astype(F32) for piece in (l0, l1, l2, r0, r1)
            )
        if h == NH - 1:
            for x in range(2):
                rows = jnp.concatenate(stat_rows[s, x] + [jnp.zeros((1, TB), F32)], axis=0).astype(BF16)
                for to in range(4):
                    out[block(s, x), to, 64 * NH : PART] = rows

    waiting = []
    for s in range(4):
        for h in range(NH):
            waiting.append((s, h, *unit(qs, kparts, vparts, s, h)))
            if len(waiting) > 2:
                finish(*waiting.pop(0))
    for item in waiting:
        finish(*item)


def attend(qs, blocks, state=None, at=None):
    halves = blocks[0].shape[0] == 2 * NH
    first, last = state is None, at is not None
    nk = 0 if halves else len(blocks)
    keys = TB * max(nk, 1)
    operands = ([at] if last else []) + list(qs) + list(blocks) + ([] if first else list(state))
    specs = ([SMEM] if last else []) + [VMEM] * (len(operands) - last)
    if last:
        out_shape = jax.ShapeDtypeStruct((8, 4, PART, DH), BF16)
        out_specs = VMEM
    else:
        out_shape = (
            jax.ShapeDtypeStruct((4, NH, 2 * DH, 2 * TB), F32),
            jax.ShapeDtypeStruct((4, NH, 8, 2 * TB), F32),
        )
        out_specs = (VMEM, VMEM)
    n = len(operands)
    alias = {} if first or last else {n - 2: 0, n - 1: 1}
    return pl.pallas_call(
        functools.partial(attend_kernel, nk, first, last),
        out_shape=out_shape,
        in_specs=specs,
        out_specs=out_specs,
        input_output_aliases=alias,
        compiler_params=pltpu.CompilerParams(vmem_limit_bytes=32 << 20),
        cost_estimate=pl.CostEstimate(
            flops=2 * 8 * TB * DH * NH * keys * 8, bytes_accessed=8 << 20, transcendentals=8 * TB * NH * keys
        ),
        name=f"attend{keys}",
    )(*operands)


def project_kernel(me, got, w0, w1, w2, w3, out, tan_out, rows):
    share, tilt = [], []
    for g in range(4):
        st = got[:, lax.bitwise_xor(me[0], g), 64 * NH : PART].astype(F32)
        for h in range(NH):
            lse = st[:, 5 * h] + st[:, 5 * h + 1] + st[:, 5 * h + 2]
            ratio = st[:, 5 * h + 3] + st[:, 5 * h + 4]
            w = jnp.exp2(lse - jnp.max(lse, axis=0, keepdims=True))
            w = w / jnp.sum(w, axis=0, keepdims=True)
            share.append(w)
            tilt.append(w * (ratio - jnp.sum(w * ratio, axis=0, keepdims=True)))
    group = lax.broadcasted_iota(jnp.int32, (8, TB), 1) // 32
    part = lax.broadcasted_iota(jnp.int32, (8, TB), 0) % 4
    row = lax.broadcasted_iota(jnp.int32, (32, TB), 0)
    diagonal = lax.broadcasted_iota(jnp.int32, (32, TB), 1) % 32 == row

    def spread(w):
        turned = w
        for i in range(1, 4):
            turned = jnp.where(part == i, pltpu.roll(w, 32 * i, axis=1), turned)
        turned = pltpu.roll(turned, lax.rem(4 - me[0], 4) * 32, axis=1)
        picked = jnp.where(group == part, turned, 0.0)
        halves = [jnp.sum(picked[4 * i : 4 * i + 4], axis=0, keepdims=True) for i in range(2)]
        return jnp.concatenate([jnp.where(diagonal, half, 0.0) for half in halves], axis=1).astype(BF16)

    for g in range(4):
        j = lax.bitwise_xor(me[0], g)
        for h in range(NH):
            mix = jnp.concatenate([spread(share[g * NH + h]), spread(tilt[g * NH + h])], axis=0)
            o = jnp.concatenate([got[i, j, 64 * h : 64 * h + 32] for i in range(8)], axis=0)
            t = jnp.concatenate([got[i, j, 64 * h + 32 : 64 * h + 64] for i in range(8)], axis=0)
            both = mm(mix, jnp.concatenate([o, t], axis=1))
            rows[g, :32, h * DH : (h + 1) * DH] = both[:32, :DH].astype(BF16)
            rows[g, 32:, h * DH : (h + 1) * DH] = (both[:32, DH:] + both[32:, :DH]).astype(BF16)

    width = out.shape[1]
    for c in range(0, width, 512):
        cols = slice(c, c + 512)
        total = mm(rows[0], w0[:, cols]) + mm(rows[1], w1[:, cols])
        total = total + mm(rows[2], w2[:, cols]) + mm(rows[3], w3[:, cols])
        out[:, cols] = total[:32].astype(BF16)
        tan_out[:, cols] = total[32:].astype(BF16)


def project(me, got, weights):
    depth, width = weights[0].shape
    oshape = jax.ShapeDtypeStruct((32, width), BF16)
    return pl.pallas_call(
        project_kernel,
        out_shape=(oshape, oshape),
        in_specs=[SMEM] + [VMEM] * 5,
        out_specs=(VMEM, VMEM),
        scratch_shapes=[pltpu.VMEM((4, 64, NH * DH), BF16)],
        compiler_params=pltpu.CompilerParams(vmem_limit_bytes=32 << 20),
        cost_estimate=pl.CostEstimate(
            flops=2 * 64 * 4 * depth * width, bytes_accessed=4 * depth * width * 2, transcendentals=0
        ),
        name="project",
    )(me, got, *weights)


def on_device(queries, keys, values, tan_queries, tan_keys, tan_values, out_weight):
    xlo, y = lax.axis_index("xlo"), lax.axis_index("y")
    me = lax.axis_index("xhi") * 2 + lax.axis_index("core")
    kp, qp = pack(queries, keys, values, tan_queries, tan_keys, tan_values)

    across = lax.ppermute(out_weight, ("xlo", "xhi"), [(2, 1), (1, 2), (3, 0), (0, 3)])

    r1, l1 = shift(kp, "z", 1), shift(kp, "z", -1)
    q0 = jnp.stack([qp, shift(qp, "xlo", 1)])
    qa, qb = shift(q0, "y", 1), shift(q0, "y", -1)
    r2, l2 = shift(r1, "z", 1), shift(l1, "z", -1)
    r2, l2, qa, qb = lax.optimization_barrier((r2, l2, qa, qb))
    qc = shift(q0, "y", 2)
    r3, l3 = shift(r2, "z", 1), shift(l2, "z", -1)
    qs = (q0, qa, qb, qc)
    at = jnp.stack([xlo, y]).astype(jnp.int32)

    state = attend(qs, (kp, r1, l1, r2, l2))
    r3, l3, *state = lax.optimization_barrier((r3, l3, *state))
    far = (shift(r3[: 2 * NH], "z", 1), shift(l3[2 * NH :], "z", -1))
    state = attend(qs, (r3, l3), state)
    sent = attend(qs, far, state, at)
    sent, across, out_weight = lax.optimization_barrier((sent, across, out_weight))
    weights = (out_weight, shift(out_weight, "core", 1), across, shift(across, "core", 1))
    got = lax.all_to_all(sent.reshape(32, PART, DH), ("xlo", "y", "xhi", "core"), 0, 0, tiled=True)
    return project(jnp.reshape(me, (1,)).astype(jnp.int32), got.reshape(8, 4, PART, DH), weights)


def solution(mesh):
    fine = Mesh(mesh.devices.reshape([SIZES[a] for a in AXES]), AXES)
    blk, head = ("xlo", "z", "y"), ("xhi", "core")
    spec = P(blk, head)
    return jax.shard_map(
        on_device,
        mesh=fine,
        in_specs=(spec,) * 6 + (P(head, None),),
        out_specs=(P(blk + head, None),) * 2,
        check_vma=False,
    )
```

time: 125 us -> 96.6 us (0.77)
  starting transfers between devices: 46.5 us -> 35.4 us
  Pallas kernels: 30.1 us -> 21.6 us
  waiting for transfers between devices: 43.8 us -> 36.5 us
  local copies, waits for them, and re-layouts: 2.77 us -> 1.03 us
    ppermute x1, waiting for transfers between devices: 11.1 us -> 0.01 us  [on_device(): lax.ppermute(out_weight, ('xlo', 'xhi'), [(2, 1), (1, 2), (3, 0), (0, 3)])]
    ppermute x14, starting transfers between devices: 36 us -> 27.8 us  [shift(): return lax.ppermute(x, axis, [(i, (i + by) % n) for i in range(n)])]
    pallas_call x4 -> x3, Pallas kernels: 20.3 us -> 12.8 us  [attend(): pl.pallas_call(functools.partial(attend_kernel, nk, first, last), out_sha...]
    ppermute x14, waiting for transfers between devices: 8.54 us -> 12.3 us  [shift(): return lax.ppermute(x, axis, [(i, (i + by) % n) for i in range(n)])]
    all_to_all x1, starting transfers between devices: 7.1 us -> 4.14 us  [on_device(): lax.all_to_all(sent.reshape(32, PART, DH), ('xlo', 'y', 'xhi', 'core'), 0...]
    unnamed x4 -> x2, local copies, waits for them, and re-layouts: 2.66 us -> 1 us
  transfers between devices with their start and end apart: 16 -> 16, of which waited for: 5 -> 6; matrix products, arithmetic and copies ran while one was open for 1% -> 1% of each run, Pallas kernels for 18% -> 15%
where the time goes in v2:
time: 96.6 us; the launch traced here: 96.3 us
  waiting for transfers between devices  36.5 us (38%)
  starting transfers between devices  35.4 us (37%)
  Pallas kernels  21.6 us (22%)
  other arithmetic  1.04 us (1%)
  local copies, waits for them, and re-layouts  1.03 us (1%)
    ppermute x14, starting transfers between devices, shift(): return lax.ppermute(x, axis, [(i, (i + by) % n) for i in range(n)])  27.8 us
    all_to_all x1, waiting for transfers between devices, on_device(): lax.all_to_all(sent.reshape(32, PART, DH), ('xlo', 'y', 'xhi', 'core'), 0...  24.2 us
    pallas_call x3, Pallas kernels, attend(): pl.pallas_call(functools.partial(attend_kernel, nk, first, last), out_sha...  12.8 us
    ppermute x14, waiting for transfers between devices, shift(): return lax.ppermute(x, axis, [(i, (i + by) % n) for i in range(n)])  12.3 us
    pallas_call x1, Pallas kernels, project(): pl.pallas_call(project_kernel, out_shape=(oshape, oshape), in_specs=[SMEM...  6.75 us
    all_to_all x1, starting transfers between devices, on_device(): lax.all_to_all(sent.reshape(32, PART, DH), ('xlo', 'y', 'xhi', 'core'), 0...  4.14 us
    ppermute x1, starting transfers between devices, on_device(): lax.ppermute(out_weight, ('xlo', 'xhi'), [(2, 1), (1, 2), (3, 0), (0, 3)])  3.39 us
    pallas_call x1, Pallas kernels, pack(): pl.pallas_call(pack_kernel, out_shape=(jax.ShapeDtypeStruct((4 * NH, TB,...  2.07 us
  transfers between devices with their start and end apart: 16, of which 6 were waited for; matrix products, arithmetic and copies ran while one was open for 1% of the time, Pallas kernels for 15%

profile of v2, /device:TPU:1, one launch (start us, length us, event | category | flops | bytes accessed | tf_op | source)
XLA Modules:
  0.0 96.3 jit_solution(1707176479976725079)
XLA Ops:
  0.6 3.4 %collective-permute-start.12 = (bf16[384,3072]{1,0:T(8,128)(2,1)}, bf16[384,3072]{1,0:T(8,128)(2,1)}, u32[]{:S(2)}, u32[]{:S(2)}) collective-permute-start(bf16[384,3072]{1,0:T(8,128)(2,1)} %w0), channel_id=1, source_target_pairs={{128,2},{2,128},{130,0},{0,130},{129,3},{3,129},{131,1},{1,131},{1... | collective-permute-start | bytes 7077896 | tf_op jit(solution)/shard_map/ppermute | solution.py:250
  4.0 2.1 %pack.1 = (bf16[12,128,128]{2,1,0:T(8,128)(2,1)}, bf16[6,128,128]{2,1,0:T(8,128)(2,1)}) custom-call(bf16[128,384]{1,0:T(8,128)(2,1)} %q.1, bf16[128,384]{1,0:T(8,128)(2,1)} %k.1, bf16[128,384]{1,0:T(8,128)(2,1)} %v.1, bf16[128,384]{1,0:T(8,128)(2,1)} %tq.1, bf16[128,384]{1,0:T(8,128)(2,1)} %tk.1, bf16[128,384]{1,0:T(8,128)(2,1)} %tv.1), custom_call_target="tpu_custom_call" | custom-call | tf_op jit(solution)/shard_map/pack/pallas_call | solution.py:45
  6.1 0.0 collective-permute-start
  6.1 5.6 %collective-permute-start.3 = (bf16[12,128,128]{2,1,0:T(8,128)(2,1)}, bf16[12,128,128]{2,1,0:T(8,128)(2,1)S(1)}, u32[]{:S(2)}, u32[]{:S(2)}) collective-permute-start(bf16[12,128,128]{2,1,0:T(8,128)(2,1)} %get-tuple-element.20.refs_4_), channel_id=1, source_target_pairs={{0,112},{16,0},{32,16},{48,32},{64,48},{80,64},{96,80},{112,96},{1... | collective-permute-start | bytes 1179656 | tf_op jit(solution)/shard_map/ppermute | solution.py:26
  11.7 0.0 collective-permute-start.1
  11.7 0.2 collective-permute-done
  11.9 1.0 %pad_maximum_fusion.refs_0_.refs_1_ = bf16[2,6,128,128]{3,2,1,0:T(8,128)(2,1)S(1)} fusion(bf16[1,6,128,128]{3,2,1,0:T(8,128)(2,1)S(1)} %bitcast.9, bf16[1,6,128,128]{3,2,1,0:T(8,128)(2,1)} %bitcast.8), kind=kLoop, calls=%fused_computation | loop fusion | flops 196608 | bytes 786432 | tf_op jit(solution)/shard_map/stack | solution.py:253
  12.8 2.8 %collective-permute-start.6 = (bf16[2,6,128,128]{3,2,1,0:T(8,128)(2,1)S(1)}, bf16[2,6,128,128]{3,2,1,0:T(8,128)(2,1)S(1)}, u32[]{:S(2)}, u32[]{:S(2)}) collective-permute-start(bf16[2,6,128,128]{3,2,1,0:T(8,128)(2,1)S(1)} %pad_maximum_fusion.refs_0_.refs_1_), channel_id=1, source_target_pairs={{0,12},{4,0},{8,4},{12,8},{1,13},{5,1},{9,5},{13,9},{2,14},{6,2},{... | collective-permute-start | bytes 1179656 | tf_op jit(solution)/shard_map/ppermute | solution.py:26
  15.6 0.0 collective-permute-start.5
  15.7 3.6 %collective-permute-done.3.refs_6_ = bf16[12,128,128]{2,1,0:T(8,128)(2,1)S(1)} collective-permute-done((bf16[12,128,128]{2,1,0:T(8,128)(2,1)}, bf16[12,128,128]{2,1,0:T(8,128)(2,1)S(1)}, u32[]{:S(2)}, u32[]{:S(2)}) %collective-permute-start.3) | collective-permute-done | bytes 393248 | tf_op jit(solution)/shard_map/ppermute | solution.py:26
  19.2 3.4 %collective-permute-start.4 = (bf16[12,128,128]{2,1,0:T(8,128)(2,1)S(1)}, bf16[12,128,128]{2,1,0:T(8,128)(2,1)S(1)}, u32[]{:S(2)}, u32[]{:S(2)}) collective-permute-start(bf16[12,128,128]{2,1,0:T(8,128)(2,1)S(1)} %collective-permute-done.3.refs_6_), channel_id=1, source_target_pairs={{0,112},{16,0},{32,16},{48,32},{64,48},{80,64},{96,80},{112,96},{1... | collective-permute-start | bytes 1179656 | tf_op jit(solution)/shard_map/ppermute | solution.py:26
  22.6 0.0 collective-permute-done.1.refs_5_
  22.6 0.0 collective-permute-start.2
  22.6 0.0 collective-permute-done.6.refs_2_.refs_3_
  22.6 3.0 %collective-permute-start.7 = (bf16[2,6,128,128]{3,2,1,0:T(8,128)(2,1)S(1)}, bf16[2,6,128,128]{3,2,1,0:T(8,128)(2,1)S(1)}, u32[]{:S(2)}, u32[]{:S(2)}) collective-permute-start(bf16[2,6,128,128]{3,2,1,0:T(8,128)(2,1)S(1)} %pad_maximum_fusion.refs_0_.refs_1_), channel_id=1, source_target_pairs={{0,8},{4,12},{8,0},{12,4},{1,9},{5,13},{9,1},{13,5},{2,10},{6,14},... | collective-permute-start | bytes 1179656 | tf_op jit(solution)/shard_map/ppermute | solution.py:26
  25.7 0.0 collective-permute-done.5.refs_1_.refs_2_
  25.7 3.4 %collective-permute-done.4.refs_8_ = bf16[12,128,128]{2,1,0:T(8,128)(2,1)S(1)} collective-permute-done((bf16[12,128,128]{2,1,0:T(8,128)(2,1)S(1)}, bf16[12,128,128]{2,1,0:T(8,128)(2,1)S(1)}, u32[]{:S(2)}, u32[]{:S(2)}) %collective-permute-start.4) | collective-permute-done | bytes 393248 | tf_op jit(solution)/shard_map/ppermute | solution.py:26
  29.0 3.2 %collective-permute-done.2.refs_7_ = bf16[12,128,128]{2,1,0:T(8,128)(2,1)} collective-permute-done((bf16[12,128,128]{2,1,0:T(8,128)(2,1)S(1)}, bf16[12,128,128]{2,1,0:T(8,128)(2,1)}, u32[]{:S(2)}, u32[]{:S(2)}) %collective-permute-start.2) | collective-permute-done | bytes 393248 | tf_op jit(solution)/shard_map/ppermute | solution.py:26
  32.3 0.0 collective-permute-start.8
  32.3 2.7 %collective-permute-start.9 = (bf16[12,128,128]{2,1,0:T(8,128)(2,1)S(1)}, bf16[12,128,128]{2,1,0:T(8,128)(2,1)S(1)}, u32[]{:S(2)}, u32[]{:S(2)}) collective-permute-start(bf16[12,128,128]{2,1,0:T(8,128)(2,1)S(1)} %collective-permute-done.4.refs_8_), channel_id=1, source_target_pairs={{0,112},{16,0},{32,16},{48,32},{64,48},{80,64},{96,80},{112,96},{1... | collective-permute-start | bytes 1179656 | tf_op jit(solution)/shard_map/ppermute | solution.py:26
  35.0 0.0 collective-permute-done.7.refs_3_.refs_4_
  35.0 0.0 copy-start
  35.0 1.0 %copy-done = bf16[12,128,128]{2,1,0:T(8,128)(2,1)S(1)} copy-done((bf16[12,128,128]{2,1,0:T(8,128)(2,1)S(1)}, bf16[12,128,128]{2,1,0:T(8,128)(2,1)}, u32[]{:S(2)}) %copy-start) | copy-done | bytes 393240
  36.0 6.4 %attend640.1 = (f32[4,3,256,256]{3,2,1,0:T(8,128)S(1)}, f32[4,3,8,256]{3,2,1,0:T(8,128)S(1)}) custom-call(bf16[2,6,128,128]{3,2,1,0:T(8,128)(2,1)S(1)} %pad_maximum_fusion.refs_0_.refs_1_, bf16[2,6,128,128]{3,2,1,0:T(8,128)(2,1)S(1)} %collective-permute-done.5.refs_1_.refs_2_, bf16[2,6,128,128]{3,2,1,0:T(8,128)(2,1)S(1)} %collective-permute-done.6.refs_2_.refs_3_, ...), custom_call_target="tpu_custom_call" | custom-call | flops 4026531840 | bytes 8388608 | tf_op jit(solution)/shard_map/attend640/pallas_call | solution.py:170
  42.3 0.0 collective-permute-done.8.refs_4_
  42.4 0.0 collective-permute-done.9.refs_5_
  42.4 0.1 collective-permute-start.10
  42.5 3.4 %collective-permute-start.11 = (bf16[6,128,128]{2,1,0:T(8,128)(2,1)S(1)}, bf16[6,128,128]{2,1,0:T(8,128)(2,1)S(1)}, u32[]{:S(2)}, u32[]{:S(2)}) collective-permute-start(bf16[6,128,128]{2,1,0:T(8,128)(2,1)S(1)} %slice.7), channel_id=1, source_target_pairs={{0,112},{16,0},{32,16},{48,32},{64,48},{80,64},{96,80},{112,96},{1... | collective-permute-start | bytes 589832 | tf_op jit(solution)/shard_map/ppermute | solution.py:26
  45.9 0.1 pad_add_fusion.refs_0_
  46.0 2.6 %attend256.1 = (f32[4,3,256,256]{3,2,1,0:T(8,128)S(1)}, f32[4,3,8,256]{3,2,1,0:T(8,128)S(1)}) custom-call(bf16[2,6,128,128]{3,2,1,0:T(8,128)(2,1)S(1)} %pad_maximum_fusion.refs_0_.refs_1_, bf16[2,6,128,128]{3,2,1,0:T(8,128)(2,1)S(1)} %collective-permute-done.5.refs_1_.refs_2_, ...), custom_call_target="tpu_custom_call", output_to_operand_aliasing={{0}: (6, {}), {1}: (7, {})} | custom-call | flops 1610612736 | bytes 8388608 | tf_op jit(solution)/shard_map/attend256/pallas_call | solution.py:170
  48.5 1.9 %collective-permute-done.10.refs_5_ = bf16[6,128,128]{2,1,0:T(8,128)(2,1)S(1)} collective-permute-done((bf16[6,128,128]{2,1,0:T(8,128)(2,1)S(1)}, bf16[6,128,128]{2,1,0:T(8,128)(2,1)S(1)}, u32[]{:S(2)}, u32[]{:S(2)}) %collective-permute-start.10) | collective-permute-done | bytes 196640 | tf_op jit(solution)/shard_map/ppermute | solution.py:26
  50.5 0.0 collective-permute-done.11.refs_6_
  50.5 3.8 %attend128.1 = bf16[8,4,208,128]{3,2,1,0:T(8,128)(2,1)} custom-call(s32[2]{0:T(128)S(1)} %pad_add_fusion.refs_0_, bf16[2,6,128,128]{3,2,1,0:T(8,128)(2,1)S(1)} %pad_maximum_fusion.refs_0_.refs_1_, bf16[2,6,128,128]{3,2,1,0:T(8,128)(2,1)S(1)} %collective-permute-done.5.refs_1_.refs_2_, bf16[2,6,128,128]{3,2,1,0:T(8,128)(2,1)S(1)} %collective-permute-done.6.refs_2_.refs_3_, ...), custom_call_target="tpu_custom_call" | custom-call | flops 805306368 | bytes 8388608 | tf_op jit(solution)/shard_map/attend128/pallas_call | solution.py:170
  54.3 0.0 collective-permute-done.12.w2
  54.3 6.9 %collective-permute-start.13 = (bf16[384,3072]{1,0:T(8,128)(2,1)}, bf16[384,3072]{1,0:T(8,128)(2,1)}, u32[]{:S(2)}, u32[]{:S(2)}) collective-permute-start(bf16[384,3072]{1,0:T(8,128)(2,1)} %w0), channel_id=1, source_target_pairs={{0,1},{1,0},{2,3},{3,2},{4,5},{5,4},{6,7},{7,6},{8,9},{9,8},{10,11... | collective-permute-start | bytes 7077896 | tf_op jit(solution)/shard_map/ppermute | solution.py:26
  61.2 0.0 collective-permute-start.14
  61.2 4.1 %all-to-all-start = ((bf16[32,208,128]{2,1,0:T(8,128)(2,1)}), bf16[32,208,128]{2,1,0:T(8,128)(2,1)S(1)}, u32[]{:S(2)}, u32[]{:S(2)}) async-start(bf16[32,208,128]{2,1,0:T(8,128)(2,1)} %bitcast.5), calls=%async_computation | async-start | bytes 3407872 | tf_op jit(solution)/shard_map/all_to_all | solution.py:269
  65.3 24.2 %all-to-all-done = bf16[32,208,128]{2,1,0:T(8,128)(2,1)S(1)} async-done(((bf16[32,208,128]{2,1,0:T(8,128)(2,1)}), bf16[32,208,128]{2,1,0:T(8,128)(2,1)S(1)}, u32[]{:S(2)}, u32[]{:S(2)}) %all-to-all-start) | async-done | bytes 1703968 | tf_op jit(solution)/shard_map/all_to_all | solution.py:269
  89.5 0.0 collective-permute-done.13.w1
  89.5 0.0 collective-permute-done.14.w3
  89.5 6.7 %project.1 = (bf16[32,3072]{1,0:T(8,128)(2,1)}, bf16[32,3072]{1,0:T(8,128)(2,1)}) custom-call(s32[1]{0:T(128)} %bitcast.me, bf16[8,4,208,128]{3,2,1,0:T(8,128)(2,1)S(1)} %bitcast.7, bf16[384,3072]{1,0:T(8,128)(2,1)} %w0, bf16[384,3072]{1,0:T(8,128)(2,1)} %collective-permute-done.13.w1, bf16[384,3072]{1,0:T(8,128)(2,1)} %collective-permute-done.12.w2, ...), custom_call_target="tpu_custom_call" | custom-call | flops 603979776 | bytes 9437184 | tf_op jit(solution)/shard_map/project/pallas_call | solution.py:231
  (2 shorter events, 0.0 us)
Async XLA Ops:
  0.6 53.7 %collective-permute-start.12 = (bf16[384,3072]{1,0:T(8,128)(2,1)}, bf16[384,3072]{1,0:T(8,128)(2,1)}, u32[]{:S(2)}, u32[]{:S(2)}) collective-permute-start(bf16[384,3072]{1,0:T(8,128)(2,1)} %w0), channel_id=1, source_target_pairs={{128,2},{2,128},{130,0},{0,130},{129,3},{3,129},{131,1},{1,131},{1... | collective-permute-start | bytes 7077896 | tf_op jit(solution)/shard_map/ppermute | solution.py:250
  6.1 5.8 %collective-permute-start = (bf16[6,128,128]{2,1,0:T(8,128)(2,1)}, bf16[6,128,128]{2,1,0:T(8,128)(2,1)S(1)}, u32[]{:S(2)}, u32[]{:S(2)}) collective-permute-start(bf16[6,128,128]{2,1,0:T(8,128)(2,1)} %get-tuple-element.19), channel_id=1, source_target_pairs={{0,128},{128,0},{1,129},{129,1},{2,130},{130,2},{3,131},{131,3},{4... | collective-permute-start | bytes 589832 | tf_op jit(solution)/shard_map/ppermute | solution.py:26
  6.1 13.1 %collective-permute-start.3 = (bf16[12,128,128]{2,1,0:T(8,128)(2,1)}, bf16[12,128,128]{2,1,0:T(8,128)(2,1)S(1)}, u32[]{:S(2)}, u32[]{:S(2)}) collective-permute-start(bf16[12,128,128]{2,1,0:T(8,128)(2,1)} %get-tuple-element.20.refs_4_), channel_id=1, source_target_pairs={{0,112},{16,0},{32,16},{48,32},{64,48},{80,64},{96,80},{112,96},{1... | collective-permute-start | bytes 1179656 | tf_op jit(solution)/shard_map/ppermute | solution.py:26
  11.7 11.0 %collective-permute-start.1 = (bf16[12,128,128]{2,1,0:T(8,128)(2,1)}, bf16[12,128,128]{2,1,0:T(8,128)(2,1)S(1)}, u32[]{:S(2)}, u32[]{:S(2)}) collective-permute-start(bf16[12,128,128]{2,1,0:T(8,128)(2,1)} %get-tuple-element.20.refs_4_), channel_id=1, source_target_pairs={{0,16},{16,32},{32,48},{48,64},{64,80},{80,96},{96,112},{112,0},{1... | collective-permute-start | bytes 1179656 | tf_op jit(solution)/shard_map/ppermute | solution.py:26
  12.8 9.8 %collective-permute-start.6 = (bf16[2,6,128,128]{3,2,1,0:T(8,128)(2,1)S(1)}, bf16[2,6,128,128]{3,2,1,0:T(8,128)(2,1)S(1)}, u32[]{:S(2)}, u32[]{:S(2)}) collective-permute-start(bf16[2,6,128,128]{3,2,1,0:T(8,128)(2,1)S(1)} %pad_maximum_fusion.refs_0_.refs_1_), channel_id=1, source_target_pairs={{0,12},{4,0},{8,4},{12,8},{1,13},{5,1},{9,5},{13,9},{2,14},{6,2},{... | collective-permute-start | bytes 1179656 | tf_op jit(solution)/shard_map/ppermute | solution.py:26
  15.6 10.0 %collective-permute-start.5 = (bf16[2,6,128,128]{3,2,1,0:T(8,128)(2,1)S(1)}, bf16[2,6,128,128]{3,2,1,0:T(8,128)(2,1)S(1)}, u32[]{:S(2)}, u32[]{:S(2)}) collective-permute-start(bf16[2,6,128,128]{3,2,1,0:T(8,128)(2,1)S(1)} %pad_maximum_fusion.refs_0_.refs_1_), channel_id=1, source_target_pairs={{0,4},{4,8},{8,12},{12,0},{1,5},{5,9},{9,13},{13,1},{2,6},{6,10},{... | collective-permute-start | bytes 1179656 | tf_op jit(solution)/shard_map/ppermute | solution.py:26
  19.2 9.8 %collective-permute-start.4 = (bf16[12,128,128]{2,1,0:T(8,128)(2,1)S(1)}, bf16[12,128,128]{2,1,0:T(8,128)(2,1)S(1)}, u32[]{:S(2)}, u32[]{:S(2)}) collective-permute-start(bf16[12,128,128]{2,1,0:T(8,128)(2,1)S(1)} %collective-permute-done.3.refs_6_), channel_id=1, source_target_pairs={{0,112},{16,0},{32,16},{48,32},{64,48},{80,64},{96,80},{112,96},{1... | collective-permute-start | bytes 1179656 | tf_op jit(solution)/shard_map/ppermute | solution.py:26
  22.6 9.6 %collective-permute-start.2 = (bf16[12,128,128]{2,1,0:T(8,128)(2,1)S(1)}, bf16[12,128,128]{2,1,0:T(8,128)(2,1)}, u32[]{:S(2)}, u32[]{:S(2)}) collective-permute-start(bf16[12,128,128]{2,1,0:T(8,128)(2,1)S(1)} %collective-permute-done.1.refs_5_), channel_id=1, source_target_pairs={{0,16},{16,32},{32,48},{48,64},{64,80},{80,96},{96,112},{112,0},{1... | collective-permute-start | bytes 1179656 | tf_op jit(solution)/shard_map/ppermute | solution.py:26
  22.6 12.3 %collective-permute-start.7 = (bf16[2,6,128,128]{3,2,1,0:T(8,128)(2,1)S(1)}, bf16[2,6,128,128]{3,2,1,0:T(8,128)(2,1)S(1)}, u32[]{:S(2)}, u32[]{:S(2)}) collective-permute-start(bf16[2,6,128,128]{3,2,1,0:T(8,128)(2,1)S(1)} %pad_maximum_fusion.refs_0_.refs_1_), channel_id=1, source_target_pairs={{0,8},{4,12},{8,0},{12,4},{1,9},{5,13},{9,1},{13,5},{2,10},{6,14},... | collective-permute-start | bytes 1179656 | tf_op jit(solution)/shard_map/ppermute | solution.py:26
  32.3 10.1 %collective-permute-start.8 = (bf16[12,128,128]{2,1,0:T(8,128)(2,1)}, bf16[12,128,128]{2,1,0:T(8,128)(2,1)S(1)}, u32[]{:S(2)}, u32[]{:S(2)}) collective-permute-start(bf16[12,128,128]{2,1,0:T(8,128)(2,1)} %collective-permute-done.2.refs_7_), channel_id=1, source_target_pairs={{0,16},{16,32},{32,48},{48,64},{64,80},{80,96},{96,112},{112,0},{1... | collective-permute-start | bytes 1179656 | tf_op jit(solution)/shard_map/ppermute | solution.py:26
  32.3 10.1 %collective-permute-start.9 = (bf16[12,128,128]{2,1,0:T(8,128)(2,1)S(1)}, bf16[12,128,128]{2,1,0:T(8,128)(2,1)S(1)}, u32[]{:S(2)}, u32[]{:S(2)}) collective-permute-start(bf16[12,128,128]{2,1,0:T(8,128)(2,1)S(1)} %collective-permute-done.4.refs_8_), channel_id=1, source_target_pairs={{0,112},{16,0},{32,16},{48,32},{64,48},{80,64},{96,80},{112,96},{1... | collective-permute-start | bytes 1179656 | tf_op jit(solution)/shard_map/ppermute | solution.py:26
  35.0 1.0 %copy-start = (bf16[12,128,128]{2,1,0:T(8,128)(2,1)S(1)}, bf16[12,128,128]{2,1,0:T(8,128)(2,1)}, u32[]{:S(2)}) copy-start(bf16[12,128,128]{2,1,0:T(8,128)(2,1)} %get-tuple-element.20.refs_4_) | copy-start | bytes 1179652
  42.4 8.1 %collective-permute-start.10 = (bf16[6,128,128]{2,1,0:T(8,128)(2,1)S(1)}, bf16[6,128,128]{2,1,0:T(8,128)(2,1)S(1)}, u32[]{:S(2)}, u32[]{:S(2)}) collective-permute-start(bf16[6,128,128]{2,1,0:T(8,128)(2,1)S(1)} %slice.6), channel_id=1, source_target_pairs={{0,16},{16,32},{32,48},{48,64},{64,80},{80,96},{96,112},{112,0},{1... | collective-permute-start | bytes 589832 | tf_op jit(solution)/shard_map/ppermute | solution.py:26
  42.5 8.0 %collective-permute-start.11 = (bf16[6,128,128]{2,1,0:T(8,128)(2,1)S(1)}, bf16[6,128,128]{2,1,0:T(8,128)(2,1)S(1)}, u32[]{:S(2)}, u32[]{:S(2)}) collective-permute-start(bf16[6,128,128]{2,1,0:T(8,128)(2,1)S(1)} %slice.7), channel_id=1, source_target_pairs={{0,112},{16,0},{32,16},{48,32},{64,48},{80,64},{96,80},{112,96},{1... | collective-permute-start | bytes 589832 | tf_op jit(solution)/shard_map/ppermute | solution.py:26
  54.3 35.2 %collective-permute-start.13 = (bf16[384,3072]{1,0:T(8,128)(2,1)}, bf16[384,3072]{1,0:T(8,128)(2,1)}, u32[]{:S(2)}, u32[]{:S(2)}) collective-permute-start(bf16[384,3072]{1,0:T(8,128)(2,1)} %w0), channel_id=1, source_target_pairs={{0,1},{1,0},{2,3},{3,2},{4,5},{5,4},{6,7},{7,6},{8,9},{9,8},{10,11... | collective-permute-start | bytes 7077896 | tf_op jit(solution)/shard_map/ppermute | solution.py:26
  61.2 28.4 %collective-permute-start.14 = (bf16[384,3072]{1,0:T(8,128)(2,1)}, bf16[384,3072]{1,0:T(8,128)(2,1)}, u32[]{:S(2)}, u32[]{:S(2)}) collective-permute-start(bf16[384,3072]{1,0:T(8,128)(2,1)} %collective-permute-done.12.w2), channel_id=1, source_target_pairs={{0,1},{1,0},{2,3},{3,2},{4,5},{5,4},{6,7},{7,6},{8,9},{9,8},{10,11... | collective-permute-start | bytes 7077896 | tf_op jit(solution)/shard_map/ppermute | solution.py:26
  61.2 28.4 %all-to-all-start = ((bf16[32,208,128]{2,1,0:T(8,128)(2,1)}), bf16[32,208,128]{2,1,0:T(8,128)(2,1)S(1)}, u32[]{:S(2)}, u32[]{:S(2)}) async-start(bf16[32,208,128]{2,1,0:T(8,128)(2,1)} %bitcast.5), calls=%async_computation | async-start | bytes 3407872 | tf_op jit(solution)/shard_map/all_to_all | solution.py:269

commit v3 on v2

--- a/solution.py
+++ b/solution.py
@@ -16,6 +16,7 @@
 SIZES = {"xlo": 2, "z": 8, "y": 4, "xhi": 2, "core": 2}
 AXES = ("xlo", "z", "y", "xhi", "core")
 PART = 2 * NH * 32 + 16
+CHUNK = 512
 F32, BF16 = jnp.float32, jnp.bfloat16
 VMEM = pl.BlockSpec(memory_space=pltpu.VMEM)
 SMEM = pl.BlockSpec(memory_space=pltpu.SMEM)
@@ -80,9 +81,10 @@
     else:
         acc_out, st_out = refs
     stat_rows = {}
-
-    def block(s, x):
-        return lax.bitwise_xor(at[0], x) * 4 + lax.bitwise_and(at[1] + (0, 3, 1, 2)[s], 3)
+    if last:
+        places = [
+            [lax.bitwise_xor(at[0], x) * 4 + lax.bitwise_and(at[1] + d, 3) for x in range(2)] for d in (0, 3, 1, 2)
+        ]
 
     def finish(s, h, scores, tan):
         top = jnp.max(scores, axis=0, keepdims=True) * SCALE2
@@ -128,8 +130,8 @@
             tt = t[:, lanes].astype(BF16).T
             for to in range(4):
                 rows = slice(to * 32, (to + 1) * 32)
-                out[block(s, x), to, 64 * h : 64 * h + 32] = ot[rows]
-                out[block(s, x), to, 64 * h + 32 : 64 * h + 64] = tt[rows]
+                out[places[s][x], to, 64 * h : 64 * h + 32] = ot[rows]
+                out[places[s][x], to, 64 * h + 32 : 64 * h + 64] = tt[rows]
             stat_rows.setdefault((s, x), []).extend(
                 piece[:, lanes].astype(F32) for piece in (l0, l1, l2, r0, r1)
             )
@@ -137,7 +139,7 @@
             for x in range(2):
                 rows = jnp.concatenate(stat_rows[s, x] + [jnp.zeros((1, TB), F32)], axis=0).astype(BF16)
                 for to in range(4):
-                    out[block(s, x), to, 64 * NH : PART] = rows
+                    out[places[s][x], to, 64 * NH : PART] = rows
 
     waiting = []
     for s in range(4):
@@ -173,7 +175,7 @@
         in_specs=specs,
         out_specs=out_specs,
         input_output_aliases=alias,
-        compiler_params=pltpu.CompilerParams(vmem_limit_bytes=32 << 20),
+        compiler_params=pltpu.CompilerParams(vmem_limit_bytes=16 << 20),
         cost_estimate=pl.CostEstimate(
             flops=2 * 8 * TB * DH * NH * keys * 8, bytes_accessed=8 << 20, transcendentals=8 * TB * NH * keys
         ),
@@ -181,17 +183,33 @@
     )(*operands)
 
 
-def project_kernel(me, got, w0, w1, w2, w3, out, tan_out, rows):
+def project_kernel(me, got, w0, w1a, w1b, w2, w3a, w3b, out, tan_out, rows, w, total, sems):
+    half = w1a.shape[0]
+    whole = [
+        [(w0, 0)],
+        [(w1a, 0), (w1b, half)],
+        [(w2, 0)],
+        [(w3a, 0), (w3b, half)],
+    ]
+    copies = [
+        [
+            pltpu.make_async_copy(src, w.at[g, pl.ds(at, src.shape[0])], sems.at[g, i])
+            for i, (src, at) in enumerate(parts)
+        ]
+        for g, parts in enumerate(whole)
+    ]
+    for copy in sum(copies, []):
+        copy.start()
     share, tilt = [], []
     for g in range(4):
         st = got[:, lax.bitwise_xor(me[0], g), 64 * NH : PART].astype(F32)
         for h in range(NH):
             lse = st[:, 5 * h] + st[:, 5 * h + 1] + st[:, 5 * h + 2]
             ratio = st[:, 5 * h + 3] + st[:, 5 * h + 4]
-            w = jnp.exp2(lse - jnp.max(lse, axis=0, keepdims=True))
-            w = w / jnp.sum(w, axis=0, keepdims=True)
-            share.append(w)
-            tilt.append(w * (ratio - jnp.sum(w * ratio, axis=0, keepdims=True)))
+            part_of = jnp.exp2(lse - jnp.max(lse, axis=0, keepdims=True))
+            part_of = part_of / jnp.sum(part_of, axis=0, keepdims=True)
+            share.append(part_of)
+            tilt.append(part_of * (ratio - jnp.sum(part_of * ratio, axis=0, keepdims=True)))
     group = lax.broadcasted_iota(jnp.int32, (8, TB), 1) // 32
     part = lax.broadcasted_iota(jnp.int32, (8, TB), 0) % 4
     row = lax.broadcasted_iota(jnp.int32, (32, TB), 0)
@@ -216,13 +234,20 @@
             rows[g, :32, h * DH : (h + 1) * DH] = both[:32, :DH].astype(BF16)
             rows[g, 32:, h * DH : (h + 1) * DH] = (both[:32, DH:] + both[32:, :DH]).astype(BF16)
 
-    width = out.shape[1]
-    for c in range(0, width, 512):
-        cols = slice(c, c + 512)
-        total = mm(rows[0], w0[:, cols]) + mm(rows[1], w1[:, cols])
-        total = total + mm(rows[2], w2[:, cols]) + mm(rows[3], w3[:, cols])
-        out[:, cols] = total[:32].astype(BF16)
-        tan_out[:, cols] = total[32:].astype(BF16)
+    for g in range(4):
+        for copy in copies[g]:
+            copy.wait()
+        for c in range(0, out.shape[1], CHUNK):
+            cols = slice(c, c + CHUNK)
+            term = mm(rows[g], w[g, :, cols])
+            if g == 0:
+                total[:, cols] = term
+            elif g < 3:
+                total[:, cols] += term
+            else:
+                term = term + total[:, cols]
+                out[:, cols] = term[:32].astype(BF16)
+                tan_out[:, cols] = term[32:].astype(BF16)
 
 
 def project(me, got, weights):
@@ -231,10 +256,15 @@
     return pl.pallas_call(
         project_kernel,
         out_shape=(oshape, oshape),
-        in_specs=[SMEM] + [VMEM] * 5,
+        in_specs=[SMEM, VMEM] + [pl.BlockSpec(memory_space=pl.ANY)] * 6,
         out_specs=(VMEM, VMEM),
-        scratch_shapes=[pltpu.VMEM((4, 64, NH * DH), BF16)],
-        compiler_params=pltpu.CompilerParams(vmem_limit_bytes=32 << 20),
+        scratch_shapes=[
+            pltpu.VMEM((4, 64, NH * DH), BF16),
+            pltpu.VMEM((4, depth, width), BF16),
+            pltpu.VMEM((64, width), F32),
+            pltpu.SemaphoreType.DMA((4, 2)),
+        ],
+        compiler_params=pltpu.CompilerParams(vmem_limit_bytes=20 << 20),
         cost_estimate=pl.CostEstimate(
             flops=2 * 64 * 4 * depth * width, bytes_accessed=4 * depth * width * 2, transcendentals=0
         ),
@@ -253,20 +283,23 @@
     q0 = jnp.stack([qp, shift(qp, "xlo", 1)])
     qa, qb = shift(q0, "y", 1), shift(q0, "y", -1)
     r2, l2 = shift(r1, "z", 1), shift(l1, "z", -1)
-    r2, l2, qa, qb = lax.optimization_barrier((r2, l2, qa, qb))
+    q0, qa, qb = lax.optimization_barrier((q0, qa, qb))
     qc = shift(q0, "y", 2)
     r3, l3 = shift(r2, "z", 1), shift(l2, "z", -1)
     qs = (q0, qa, qb, qc)
     at = jnp.stack([xlo, y]).astype(jnp.int32)
 
-    state = attend(qs, (kp, r1, l1, r2, l2))
+    state = attend(qs, (kp, r1, l1))
     r3, l3, *state = lax.optimization_barrier((r3, l3, *state))
     far = (shift(r3[: 2 * NH], "z", 1), shift(l3[2 * NH :], "z", -1))
-    state = attend(qs, (r3, l3), state)
+    state = attend(qs, (r2, l2, r3, l3), state)
     sent = attend(qs, far, state, at)
-    sent, across, out_weight = lax.optimization_barrier((sent, across, out_weight))
-    weights = (out_weight, shift(out_weight, "core", 1), across, shift(across, "core", 1))
     got = lax.all_to_all(sent.reshape(32, PART, DH), ("xlo", "y", "xhi", "core"), 0, 0, tiled=True)
+    across, own = lax.optimization_barrier((across, out_weight))
+    half = out_weight.shape[0] // 2
+    other = [shift(own[i : i + half], "core", 1) for i in (0, half)]
+    across_other = [shift(across[i : i + half], "core", 1) for i in (0, half)]
+    weights = (out_weight, *other, across, *across_other)
     return project(jnp.reshape(me, (1,)).astype(jnp.int32), got.reshape(8, 4, PART, DH), weights)
 
 

time: 96.6 us -> 92.1 us (0.953)
  waiting for transfers between devices: 36.5 us -> 30.1 us
  local copies, waits for them, and re-layouts: 1.03 us -> 5.98 us
  starting transfers between devices: 35.4 us -> 33.3 us
  Pallas kernels: 21.6 us -> 20.5 us
    ppermute x14 -> x16, starting transfers between devices: 27.8 us -> 20.7 us  [shift(): return lax.ppermute(x, axis, [(i, (i + by) % n) for i in range(n)])]
    all_to_all x1, waiting for transfers between devices: 24.2 us -> 18.2 us  [on_device(): lax.all_to_all(sent.reshape(32, PART, DH), ('xlo', 'y', 'xhi', 'core'), 0...]
    all_to_all x1, starting transfers between devices: 4.14 us -> 9.19 us  [on_device(): lax.all_to_all(sent.reshape(32, PART, DH), ('xlo', 'y', 'xhi', 'core'), 0...]
    slice x0 -> x2, local copies, waits for them, and re-layouts: none -> 4.95 us  [the longest x1 3.33 us: on_device(): across_other = [shift(across[i:i + half], 'core', 1) for i in (0, half)]]
    pallas_call x1, Pallas kernels: 6.75 us -> 5.78 us  [project(): pl.pallas_call(project_kernel, out_shape=(oshape, oshape), in_specs=[SMEM...]
    ppermute x14 -> x16, waiting for transfers between devices: 12.3 us -> 11.9 us  [shift(): return lax.ppermute(x, axis, [(i, (i + by) % n) for i in range(n)])]
  transfers between devices with their start and end apart: 16 -> 18, of which waited for: 6 -> 6; matrix products, arithmetic and copies ran while one was open for 1% -> 7% of each run, Pallas kernels for 15% -> 16%
where the time goes in v3:
time: 92.1 us; the launch traced here: 91.7 us
  starting transfers between devices  33.3 us (36%)
  waiting for transfers between devices  30.1 us (33%)
  Pallas kernels  20.5 us (22%)
  local copies, waits for them, and re-layouts  5.98 us (6%)
  other arithmetic  1.04 us (1%)
    ppermute x16, starting transfers between devices, shift(): return lax.ppermute(x, axis, [(i, (i + by) % n) for i in range(n)])  20.7 us
    all_to_all x1, waiting for transfers between devices, on_device(): lax.all_to_all(sent.reshape(32, PART, DH), ('xlo', 'y', 'xhi', 'core'), 0...  18.2 us
    pallas_call x3, Pallas kernels, attend(): pl.pallas_call(functools.partial(attend_kernel, nk, first, last), out_sha...  12.6 us
    ppermute x16, waiting for transfers between devices, shift(): return lax.ppermute(x, axis, [(i, (i + by) % n) for i in range(n)])  11.9 us
    all_to_all x1, starting transfers between devices, on_device(): lax.all_to_all(sent.reshape(32, PART, DH), ('xlo', 'y', 'xhi', 'core'), 0...  9.19 us
    pallas_call x1, Pallas kernels, project(): pl.pallas_call(project_kernel, out_shape=(oshape, oshape), in_specs=[SMEM...  5.78 us
    ppermute x1, starting transfers between devices, on_device(): lax.ppermute(out_weight, ('xlo', 'xhi'), [(2, 1), (1, 2), (3, 0), (0, 3)])  3.39 us
    slice x1, local copies, waits for them, and re-layouts, on_device(): across_other = [shift(across[i:i + half], 'core', 1) for i in (0, half)]  3.33 us
  transfers between devices with their start and end apart: 18, of which 6 were waited for; matrix products, arithmetic and copies ran while one was open for 7% of the time, Pallas kernels for 16%

profile of v3, /device:TPU:1, one launch (start us, length us, event | category | flops | bytes accessed | tf_op | source)
XLA Modules:
  0.0 91.7 jit_solution(16899566601140557745)
XLA Ops:
  0.6 3.4 %collective-permute-start.12 = (bf16[384,3072]{1,0:T(8,128)(2,1)}, bf16[384,3072]{1,0:T(8,128)(2,1)}, u32[]{:S(2)}, u32[]{:S(2)}) collective-permute-start(bf16[384,3072]{1,0:T(8,128)(2,1)} %w0.1), channel_id=1, source_target_pairs={{128,2},{2,128},{130,0},{0,130},{129,3},{3,129},{131,1},{1,131},{1... | collective-permute-start | bytes 7077896 | tf_op jit(solution)/shard_map/ppermute | solution.py:280
  4.0 2.1 %pack.1 = (bf16[12,128,128]{2,1,0:T(8,128)(2,1)}, bf16[6,128,128]{2,1,0:T(8,128)(2,1)}) custom-call(bf16[128,384]{1,0:T(8,128)(2,1)} %q.1, bf16[128,384]{1,0:T(8,128)(2,1)} %k.1, bf16[128,384]{1,0:T(8,128)(2,1)} %v.1, bf16[128,384]{1,0:T(8,128)(2,1)} %tq.1, bf16[128,384]{1,0:T(8,128)(2,1)} %tk.1, bf16[128,384]{1,0:T(8,128)(2,1)} %tv.1), custom_call_target="tpu_custom_call" | custom-call | tf_op jit(solution)/shard_map/pack/pallas_call | solution.py:46
  6.1 0.0 collective-permute-start
  6.1 1.6 %collective-permute-start.4 = (bf16[12,128,128]{2,1,0:T(8,128)(2,1)}, bf16[12,128,128]{2,1,0:T(8,128)(2,1)S(1)}, u32[]{:S(2)}, u32[]{:S(2)}) collective-permute-start(bf16[12,128,128]{2,1,0:T(8,128)(2,1)} %get-tuple-element.21.refs_4_), channel_id=1, source_target_pairs={{0,16},{16,32},{32,48},{48,64},{64,80},{80,96},{96,112},{112,0},{1... | collective-permute-start | bytes 1179656 | tf_op jit(solution)/shard_map/ppermute | solution.py:27
  7.7 4.0 %collective-permute-start.7 = (bf16[12,128,128]{2,1,0:T(8,128)(2,1)}, bf16[12,128,128]{2,1,0:T(8,128)(2,1)S(1)}, u32[]{:S(2)}, u32[]{:S(2)}) collective-permute-start(bf16[12,128,128]{2,1,0:T(8,128)(2,1)} %get-tuple-element.21.refs_4_), channel_id=1, source_target_pairs={{0,112},{16,0},{32,16},{48,32},{64,48},{80,64},{96,80},{112,96},{1... | collective-permute-start | bytes 1179656 | tf_op jit(solution)/shard_map/ppermute | solution.py:27
  11.8 0.1 collective-permute-done
  11.9 1.0 %pad_maximum_fusion.refs_0_.refs_1_ = bf16[2,6,128,128]{3,2,1,0:T(8,128)(2,1)S(1)} fusion(bf16[1,6,128,128]{3,2,1,0:T(8,128)(2,1)S(1)} %bitcast.8, bf16[1,6,128,128]{3,2,1,0:T(8,128)(2,1)} %bitcast.7), kind=kLoop, calls=%fused_computation | loop fusion | flops 196608 | bytes 786432 | tf_op jit(solution)/shard_map/stack | solution.py:283
  12.8 1.4 %collective-permute-start.1 = (bf16[2,6,128,128]{3,2,1,0:T(8,128)(2,1)S(1)}, bf16[2,6,128,128]{3,2,1,0:T(8,128)(2,1)S(1)}, u32[]{:S(2)}, u32[]{:S(2)}) collective-permute-start(bf16[2,6,128,128]{3,2,1,0:T(8,128)(2,1)S(1)} %pad_maximum_fusion.refs_0_.refs_1_), channel_id=1, source_target_pairs={{0,4},{4,8},{8,12},{12,0},{1,5},{5,9},{9,13},{13,1},{2,6},{6,10},{... | collective-permute-start | bytes 1179656 | tf_op jit(solution)/shard_map/ppermute | solution.py:27
  14.2 1.5 %collective-permute-start.2 = (bf16[2,6,128,128]{3,2,1,0:T(8,128)(2,1)S(1)}, bf16[2,6,128,128]{3,2,1,0:T(8,128)(2,1)S(1)}, u32[]{:S(2)}, u32[]{:S(2)}) collective-permute-start(bf16[2,6,128,128]{3,2,1,0:T(8,128)(2,1)S(1)} %pad_maximum_fusion.refs_0_.refs_1_), channel_id=1, source_target_pairs={{0,12},{4,0},{8,4},{12,8},{1,13},{5,1},{9,5},{13,9},{2,14},{6,2},{... | collective-permute-start | bytes 1179656 | tf_op jit(solution)/shard_map/ppermute | solution.py:27
  15.7 4.5 %collective-permute-done.4.refs_5_ = bf16[12,128,128]{2,1,0:T(8,128)(2,1)S(1)} collective-permute-done((bf16[12,128,128]{2,1,0:T(8,128)(2,1)}, bf16[12,128,128]{2,1,0:T(8,128)(2,1)S(1)}, u32[]{:S(2)}, u32[]{:S(2)}) %collective-permute-start.4) | collective-permute-done | bytes 393248 | tf_op jit(solution)/shard_map/ppermute | solution.py:27
  20.3 0.0 collective-permute-start.5
  20.3 0.0 collective-permute-done.7.refs_6_
  20.3 2.7 %collective-permute-start.8 = (bf16[12,128,128]{2,1,0:T(8,128)(2,1)S(1)}, bf16[12,128,128]{2,1,0:T(8,128)(2,1)}, u32[]{:S(2)}, u32[]{:S(2)}) collective-permute-start(bf16[12,128,128]{2,1,0:T(8,128)(2,1)S(1)} %collective-permute-done.7.refs_6_), channel_id=1, source_target_pairs={{0,112},{16,0},{32,16},{48,32},{64,48},{80,64},{96,80},{112,96},{1... | collective-permute-start | bytes 1179656 | tf_op jit(solution)/shard_map/ppermute | solution.py:27
  22.9 0.3 collective-permute-done.1.refs_1_.refs_2_
  23.2 0.0 collective-permute-done.2.refs_2_.refs_3_
  23.2 2.7 %collective-permute-start.3 = (bf16[2,6,128,128]{3,2,1,0:T(8,128)(2,1)S(1)}, bf16[2,6,128,128]{3,2,1,0:T(8,128)(2,1)S(1)}, u32[]{:S(2)}, u32[]{:S(2)}) collective-permute-start(bf16[2,6,128,128]{3,2,1,0:T(8,128)(2,1)S(1)} %pad_maximum_fusion.refs_0_.refs_1_), channel_id=1, source_target_pairs={{0,8},{4,12},{8,0},{12,4},{1,9},{5,13},{9,1},{13,5},{2,10},{6,14},... | collective-permute-start | bytes 1179656 | tf_op jit(solution)/shard_map/ppermute | solution.py:27
  25.9 4.6 %collective-permute-done.5.refs_4_ = bf16[12,128,128]{2,1,0:T(8,128)(2,1)S(1)} collective-permute-done((bf16[12,128,128]{2,1,0:T(8,128)(2,1)S(1)}, bf16[12,128,128]{2,1,0:T(8,128)(2,1)S(1)}, u32[]{:S(2)}, u32[]{:S(2)}) %collective-permute-start.5) | collective-permute-done | bytes 393248 | tf_op jit(solution)/shard_map/ppermute | solution.py:27
  30.5 0.0 collective-permute-start.6
  30.5 0.0 collective-permute-done.8.refs_5_
  30.5 2.7 %collective-permute-start.9 = (bf16[12,128,128]{2,1,0:T(8,128)(2,1)}, bf16[12,128,128]{2,1,0:T(8,128)(2,1)S(1)}, u32[]{:S(2)}, u32[]{:S(2)}) collective-permute-start(bf16[12,128,128]{2,1,0:T(8,128)(2,1)} %collective-permute-done.8.refs_5_), channel_id=1, source_target_pairs={{0,112},{16,0},{32,16},{48,32},{64,48},{80,64},{96,80},{112,96},{1... | collective-permute-start | bytes 1179656 | tf_op jit(solution)/shard_map/ppermute | solution.py:27
  33.2 0.1 pad_add_fusion.refs_0_
  33.2 0.0 collective-permute-done.3.refs_3_.refs_4_
  33.2 1.0 %copy-done.1 = bf16[12,128,128]{2,1,0:T(8,128)(2,1)S(1)} copy-done((bf16[12,128,128]{2,1,0:T(8,128)(2,1)S(1)}, bf16[12,128,128]{2,1,0:T(8,128)(2,1)}, u32[]{:S(2)}) %copy-start.1) | copy-done | bytes 393240
  34.2 3.3 %attend384.1 = (f32[4,3,256,256]{3,2,1,0:T(8,128)S(1)}, f32[4,3,8,256]{3,2,1,0:T(8,128)S(1)}) custom-call(bf16[2,6,128,128]{3,2,1,0:T(8,128)(2,1)S(1)} %pad_maximum_fusion.refs_0_.refs_1_, bf16[2,6,128,128]{3,2,1,0:T(8,128)(2,1)S(1)} %collective-permute-done.1.refs_1_.refs_2_, bf16[2,6,128,128]{3,2,1,0:T(8,128)(2,1)S(1)} %collective-permute-done.2.refs_2_.refs_3_, ...), custom_call_target="tpu_custom_call" | custom-call | flops 2415919104 | bytes 8388608 | tf_op jit(solution)/shard_map/attend384/pallas_call | solution.py:172
  37.5 2.3 %collective-permute-done.6.refs_6_ = bf16[12,128,128]{2,1,0:T(8,128)(2,1)S(1)} collective-permute-done((bf16[12,128,128]{2,1,0:T(8,128)(2,1)S(1)}, bf16[12,128,128]{2,1,0:T(8,128)(2,1)S(1)}, u32[]{:S(2)}, u32[]{:S(2)}) %collective-permute-start.6) | collective-permute-done | bytes 393248 | tf_op jit(solution)/shard_map/ppermute | solution.py:27
  39.9 0.0 collective-permute-done.9.refs_7_
  39.9 0.1 collective-permute-start.10
  40.0 3.0 %collective-permute-start.11 = (bf16[6,128,128]{2,1,0:T(8,128)(2,1)S(1)}, bf16[6,128,128]{2,1,0:T(8,128)(2,1)S(1)}, u32[]{:S(2)}, u32[]{:S(2)}) collective-permute-start(bf16[6,128,128]{2,1,0:T(8,128)(2,1)S(1)} %slice.19), channel_id=1, source_target_pairs={{0,112},{16,0},{32,16},{48,32},{64,48},{80,64},{96,80},{112,96},{1... | collective-permute-start | bytes 589832 | tf_op jit(solution)/shard_map/ppermute | solution.py:27
  43.1 5.5 %attend512.1 = (f32[4,3,256,256]{3,2,1,0:T(8,128)S(1)}, f32[4,3,8,256]{3,2,1,0:T(8,128)S(1)}) custom-call(bf16[2,6,128,128]{3,2,1,0:T(8,128)(2,1)S(1)} %pad_maximum_fusion.refs_0_.refs_1_, bf16[2,6,128,128]{3,2,1,0:T(8,128)(2,1)S(1)} %collective-permute-done.1.refs_1_.refs_2_, ...), custom_call_target="tpu_custom_call", output_to_operand_aliasing={{0}: (8, {}), {1}: (9, {})} | custom-call | flops 3221225472 | bytes 8388608 | tf_op jit(solution)/shard_map/attend512/pallas_call | solution.py:172
  48.6 0.0 collective-permute-done.10.refs_5_
  48.6 0.0 collective-permute-done.11.refs_6_
  48.6 3.8 %attend128.1 = bf16[8,4,208,128]{3,2,1,0:T(8,128)(2,1)} custom-call(s32[2]{0:T(128)S(1)} %pad_add_fusion.refs_0_, bf16[2,6,128,128]{3,2,1,0:T(8,128)(2,1)S(1)} %pad_maximum_fusion.refs_0_.refs_1_, bf16[2,6,128,128]{3,2,1,0:T(8,128)(2,1)S(1)} %collective-permute-done.1.refs_1_.refs_2_, bf16[2,6,128,128]{3,2,1,0:T(8,128)(2,1)S(1)} %collective-permute-done.2.refs_2_.refs_3_, ...), custom_call_target="tpu_custom_call" | custom-call | flops 805306368 | bytes 8388608 | tf_op jit(solution)/shard_map/attend128/pallas_call | solution.py:172
  52.4 9.2 %all-to-all-start = ((bf16[32,208,128]{2,1,0:T(8,128)(2,1)}), bf16[32,208,128]{2,1,0:T(8,128)(2,1)}, u32[]{:S(2)}, u32[]{:S(2)}) async-start(bf16[32,208,128]{2,1,0:T(8,128)(2,1)} %bitcast.5), calls=%async_computation | async-start | bytes 3407872 | tf_op jit(solution)/shard_map/all_to_all | solution.py:297
  61.6 0.0 collective-permute-done.12.w2
  61.6 0.0 copy-start
  61.6 3.3 %fusion = (bf16[192,3072]{1,0:T(8,128)(2,1)}, bf16[192,3072]{1,0:T(8,128)(2,1)}) fusion(bf16[384,3072]{1,0:T(8,128)(2,1)} %collective-permute-done.12.w2), kind=kLoop, calls=%fused_computation.2 | loop fusion | bytes 4718592 | tf_op jit(solution)/shard_map/slice | solution.py:301
  64.9 0.3 collective-permute-start.15
  65.2 0.2 collective-permute-start.16
  65.5 0.0 copy-done
  65.5 1.6 %fusion.1 = (bf16[192,3072]{1,0:T(8,128)(2,1)}, bf16[192,3072]{1,0:T(8,128)(2,1)}) fusion(bf16[384,3072]{1,0:T(8,128)(2,1)S(1)} %copy-done), kind=kLoop, calls=%fused_computation.3 | loop fusion | bytes 4718592 | tf_op jit(solution)/shard_map/slice | solution.py:300
  67.1 0.3 collective-permute-start.13
  67.4 0.2 collective-permute-start.14
  67.6 18.2 %all-to-all-done = bf16[32,208,128]{2,1,0:T(8,128)(2,1)} async-done(((bf16[32,208,128]{2,1,0:T(8,128)(2,1)}), bf16[32,208,128]{2,1,0:T(8,128)(2,1)}, u32[]{:S(2)}, u32[]{:S(2)}) %all-to-all-start) | async-done | bytes 1703968 | tf_op jit(solution)/shard_map/all_to_all | solution.py:297
  85.8 0.0 collective-permute-done.15.w3a
  85.8 0.0 collective-permute-done.16.w3b
  85.8 0.0 collective-permute-done.13.w1a
  85.8 0.0 collective-permute-done.14.w1b
  85.8 5.8 %project.1 = (bf16[32,3072]{1,0:T(8,128)(2,1)}, bf16[32,3072]{1,0:T(8,128)(2,1)}) custom-call(s32[1]{0:T(128)} %bitcast.me, bf16[8,4,208,128]{3,2,1,0:T(8,128)(2,1)} %bitcast.6.got, bf16[384,3072]{1,0:T(8,128)(2,1)S(1)} %copy-done, bf16[192,3072]{1,0:T(8,128)(2,1)} %collective-permute-done.13.w1a, bf16[192,3072]{1,0:T(8,128)(2,1)} %collective-permute-done.14.w1b, ...), custom_call_target="tpu_custom_call" | custom-call | flops 603979776 | bytes 9437184 | tf_op jit(solution)/shard_map/project/pallas_call | solution.py:256
  (3 shorter events, 0.0 us)
Async XLA Ops:
  0.6 61.0 %collective-permute-start.12 = (bf16[384,3072]{1,0:T(8,128)(2,1)}, bf16[384,3072]{1,0:T(8,128)(2,1)}, u32[]{:S(2)}, u32[]{:S(2)}) collective-permute-start(bf16[384,3072]{1,0:T(8,128)(2,1)} %w0.1), channel_id=1, source_target_pairs={{128,2},{2,128},{130,0},{0,130},{129,3},{3,129},{131,1},{1,131},{1... | collective-permute-start | bytes 7077896 | tf_op jit(solution)/shard_map/ppermute | solution.py:280
  6.1 5.8 %collective-permute-start = (bf16[6,128,128]{2,1,0:T(8,128)(2,1)}, bf16[6,128,128]{2,1,0:T(8,128)(2,1)S(1)}, u32[]{:S(2)}, u32[]{:S(2)}) collective-permute-start(bf16[6,128,128]{2,1,0:T(8,128)(2,1)} %get-tuple-element.17), channel_id=1, source_target_pairs={{0,128},{128,0},{1,129},{129,1},{2,130},{130,2},{3,131},{131,3},{4... | collective-permute-start | bytes 589832 | tf_op jit(solution)/shard_map/ppermute | solution.py:27
  6.1 14.2 %collective-permute-start.4 = (bf16[12,128,128]{2,1,0:T(8,128)(2,1)}, bf16[12,128,128]{2,1,0:T(8,128)(2,1)S(1)}, u32[]{:S(2)}, u32[]{:S(2)}) collective-permute-start(bf16[12,128,128]{2,1,0:T(8,128)(2,1)} %get-tuple-element.21.refs_4_), channel_id=1, source_target_pairs={{0,16},{16,32},{32,48},{48,64},{64,80},{80,96},{96,112},{112,0},{1... | collective-permute-start | bytes 1179656 | tf_op jit(solution)/shard_map/ppermute | solution.py:27
  7.7 12.5 %collective-permute-start.7 = (bf16[12,128,128]{2,1,0:T(8,128)(2,1)}, bf16[12,128,128]{2,1,0:T(8,128)(2,1)S(1)}, u32[]{:S(2)}, u32[]{:S(2)}) collective-permute-start(bf16[12,128,128]{2,1,0:T(8,128)(2,1)} %get-tuple-element.21.refs_4_), channel_id=1, source_target_pairs={{0,112},{16,0},{32,16},{48,32},{64,48},{80,64},{96,80},{112,96},{1... | collective-permute-start | bytes 1179656 | tf_op jit(solution)/shard_map/ppermute | solution.py:27
  12.8 10.4 %collective-permute-start.1 = (bf16[2,6,128,128]{3,2,1,0:T(8,128)(2,1)S(1)}, bf16[2,6,128,128]{3,2,1,0:T(8,128)(2,1)S(1)}, u32[]{:S(2)}, u32[]{:S(2)}) collective-permute-start(bf16[2,6,128,128]{3,2,1,0:T(8,128)(2,1)S(1)} %pad_maximum_fusion.refs_0_.refs_1_), channel_id=1, source_target_pairs={{0,4},{4,8},{8,12},{12,0},{1,5},{5,9},{9,13},{13,1},{2,6},{6,10},{... | collective-permute-start | bytes 1179656 | tf_op jit(solution)/shard_map/ppermute | solution.py:27
  14.2 9.0 %collective-permute-start.2 = (bf16[2,6,128,128]{3,2,1,0:T(8,128)(2,1)S(1)}, bf16[2,6,128,128]{3,2,1,0:T(8,128)(2,1)S(1)}, u32[]{:S(2)}, u32[]{:S(2)}) collective-permute-start(bf16[2,6,128,128]{3,2,1,0:T(8,128)(2,1)S(1)} %pad_maximum_fusion.refs_0_.refs_1_), channel_id=1, source_target_pairs={{0,12},{4,0},{8,4},{12,8},{1,13},{5,1},{9,5},{13,9},{2,14},{6,2},{... | collective-permute-start | bytes 1179656 | tf_op jit(solution)/shard_map/ppermute | solution.py:27
  20.3 10.2 %collective-permute-start.5 = (bf16[12,128,128]{2,1,0:T(8,128)(2,1)S(1)}, bf16[12,128,128]{2,1,0:T(8,128)(2,1)S(1)}, u32[]{:S(2)}, u32[]{:S(2)}) collective-permute-start(bf16[12,128,128]{2,1,0:T(8,128)(2,1)S(1)} %collective-permute-done.4.refs_5_), channel_id=1, source_target_pairs={{0,16},{16,32},{32,48},{48,64},{64,80},{80,96},{96,112},{112,0},{1... | collective-permute-start | bytes 1179656 | tf_op jit(solution)/shard_map/ppermute | solution.py:27
  20.3 10.2 %collective-permute-start.8 = (bf16[12,128,128]{2,1,0:T(8,128)(2,1)S(1)}, bf16[12,128,128]{2,1,0:T(8,128)(2,1)}, u32[]{:S(2)}, u32[]{:S(2)}) collective-permute-start(bf16[12,128,128]{2,1,0:T(8,128)(2,1)S(1)} %collective-permute-done.7.refs_6_), channel_id=1, source_target_pairs={{0,112},{16,0},{32,16},{48,32},{64,48},{80,64},{96,80},{112,96},{1... | collective-permute-start | bytes 1179656 | tf_op jit(solution)/shard_map/ppermute | solution.py:27
  23.2 10.0 %collective-permute-start.3 = (bf16[2,6,128,128]{3,2,1,0:T(8,128)(2,1)S(1)}, bf16[2,6,128,128]{3,2,1,0:T(8,128)(2,1)S(1)}, u32[]{:S(2)}, u32[]{:S(2)}) collective-permute-start(bf16[2,6,128,128]{3,2,1,0:T(8,128)(2,1)S(1)} %pad_maximum_fusion.refs_0_.refs_1_), channel_id=1, source_target_pairs={{0,8},{4,12},{8,0},{12,4},{1,9},{5,13},{9,1},{13,5},{2,10},{6,14},... | collective-permute-start | bytes 1179656 | tf_op jit(solution)/shard_map/ppermute | solution.py:27
  30.5 9.4 %collective-permute-start.6 = (bf16[12,128,128]{2,1,0:T(8,128)(2,1)S(1)}, bf16[12,128,128]{2,1,0:T(8,128)(2,1)S(1)}, u32[]{:S(2)}, u32[]{:S(2)}) collective-permute-start(bf16[12,128,128]{2,1,0:T(8,128)(2,1)S(1)} %collective-permute-done.5.refs_4_), channel_id=1, source_target_pairs={{0,16},{16,32},{32,48},{48,64},{64,80},{80,96},{96,112},{112,0},{1... | collective-permute-start | bytes 1179656 | tf_op jit(solution)/shard_map/ppermute | solution.py:27
  30.5 9.4 %collective-permute-start.9 = (bf16[12,128,128]{2,1,0:T(8,128)(2,1)}, bf16[12,128,128]{2,1,0:T(8,128)(2,1)S(1)}, u32[]{:S(2)}, u32[]{:S(2)}) collective-permute-start(bf16[12,128,128]{2,1,0:T(8,128)(2,1)} %collective-permute-done.8.refs_5_), channel_id=1, source_target_pairs={{0,112},{16,0},{32,16},{48,32},{64,48},{80,64},{96,80},{112,96},{1... | collective-permute-start | bytes 1179656 | tf_op jit(solution)/shard_map/ppermute | solution.py:27
  33.2 1.0 %copy-start.1 = (bf16[12,128,128]{2,1,0:T(8,128)(2,1)S(1)}, bf16[12,128,128]{2,1,0:T(8,128)(2,1)}, u32[]{:S(2)}) copy-start(bf16[12,128,128]{2,1,0:T(8,128)(2,1)} %get-tuple-element.21.refs_4_) | copy-start | bytes 1179652
  39.9 8.7 %collective-permute-start.10 = (bf16[6,128,128]{2,1,0:T(8,128)(2,1)S(1)}, bf16[6,128,128]{2,1,0:T(8,128)(2,1)S(1)}, u32[]{:S(2)}, u32[]{:S(2)}) collective-permute-start(bf16[6,128,128]{2,1,0:T(8,128)(2,1)S(1)} %slice.18), channel_id=1, source_target_pairs={{0,16},{16,32},{32,48},{48,64},{64,80},{80,96},{96,112},{112,0},{1... | collective-permute-start | bytes 589832 | tf_op jit(solution)/shard_map/ppermute | solution.py:27
  40.0 8.6 %collective-permute-start.11 = (bf16[6,128,128]{2,1,0:T(8,128)(2,1)S(1)}, bf16[6,128,128]{2,1,0:T(8,128)(2,1)S(1)}, u32[]{:S(2)}, u32[]{:S(2)}) collective-permute-start(bf16[6,128,128]{2,1,0:T(8,128)(2,1)S(1)} %slice.19), channel_id=1, source_target_pairs={{0,112},{16,0},{32,16},{48,32},{64,48},{80,64},{96,80},{112,96},{1... | collective-permute-start | bytes 589832 | tf_op jit(solution)/shard_map/ppermute | solution.py:27
  52.4 33.4 %all-to-all-start = ((bf16[32,208,128]{2,1,0:T(8,128)(2,1)}), bf16[32,208,128]{2,1,0:T(8,128)(2,1)}, u32[]{:S(2)}, u32[]{:S(2)}) async-start(bf16[32,208,128]{2,1,0:T(8,128)(2,1)} %bitcast.5), calls=%async_computation | async-start | bytes 3407872 | tf_op jit(solution)/shard_map/all_to_all | solution.py:297
  61.6 3.9 %copy-start = (bf16[384,3072]{1,0:T(8,128)(2,1)S(1)}, bf16[384,3072]{1,0:T(8,128)(2,1)}, u32[]{:S(2)}) copy-start(bf16[384,3072]{1,0:T(8,128)(2,1)} %w0.1) | copy-start | bytes 7077892
  64.9 20.8 %collective-permute-start.15 = (bf16[192,3072]{1,0:T(8,128)(2,1)}, bf16[192,3072]{1,0:T(8,128)(2,1)S(1)}, u32[]{:S(2)}, u32[]{:S(2)}) collective-permute-start(bf16[192,3072]{1,0:T(8,128)(2,1)} %get-tuple-element.33), channel_id=1, source_target_pairs={{0,1},{1,0},{2,3},{3,2},{4,5},{5,4},{6,7},{7,6},{8,9},{9,8},{10,11... | collective-permute-start | bytes 3538952 | tf_op jit(solution)/shard_map/ppermute | solution.py:27
  65.2 20.5 %collective-permute-start.16 = (bf16[192,3072]{1,0:T(8,128)(2,1)}, bf16[192,3072]{1,0:T(8,128)(2,1)}, u32[]{:S(2)}, u32[]{:S(2)}) collective-permute-start(bf16[192,3072]{1,0:T(8,128)(2,1)} %get-tuple-element.32), channel_id=1, source_target_pairs={{0,1},{1,0},{2,3},{3,2},{4,5},{5,4},{6,7},{7,6},{8,9},{9,8},{10,11... | collective-permute-start | bytes 3538952 | tf_op jit(solution)/shard_map/ppermute | solution.py:27
  67.1 18.7 %collective-permute-start.13 = (bf16[192,3072]{1,0:T(8,128)(2,1)}, bf16[192,3072]{1,0:T(8,128)(2,1)}, u32[]{:S(2)}, u32[]{:S(2)}) collective-permute-start(bf16[192,3072]{1,0:T(8,128)(2,1)} %get-tuple-element.35), channel_id=1, source_target_pairs={{0,1},{1,0},{2,3},{3,2},{4,5},{5,4},{6,7},{7,6},{8,9},{9,8},{10,11... | collective-permute-start | bytes 3538952 | tf_op jit(solution)/shard_map/ppermute | solution.py:27
  67.4 18.4 %collective-permute-start.14 = (bf16[192,3072]{1,0:T(8,128)(2,1)}, bf16[192,3072]{1,0:T(8,128)(2,1)}, u32[]{:S(2)}, u32[]{:S(2)}) collective-permute-start(bf16[192,3072]{1,0:T(8,128)(2,1)} %get-tuple-element.34), channel_id=1, source_target_pairs={{0,1},{1,0},{2,3},{3,2},{4,5},{5,4},{6,7},{7,6},{8,9},{9,8},{10,11... | collective-permute-start | bytes 3538952 | tf_op jit(solution)/shard_map/ppermute | solution.py:27

commit v4 on v3

v4 whole, which is shorter than its diff:
```python
import functools
import math

import jax
import jax.numpy as jnp
from jax import lax
from jax.experimental import pallas as pl
from jax.experimental.pallas import tpu as pltpu
from jax.sharding import Mesh, PartitionSpec as P

DH = 128
NH = 3
TB = 128
SCALE = 1.0 / math.sqrt(DH)
SCALE2 = SCALE * math.log2(math.e)
SIZES = {"xlo": 2, "z": 8, "y": 4, "xhi": 2, "core": 2}
AXES = ("xlo", "z", "y", "xhi", "core")
PART = 2 * NH * 32 + 16
CHUNK = 512
F32, BF16 = jnp.float32, jnp.bfloat16
VMEM = pl.BlockSpec(memory_space=pltpu.VMEM)
SMEM = pl.BlockSpec(memory_space=pltpu.SMEM)
HBM = pl.BlockSpec(memory_space=pltpu.HBM)


def shift(x, axis, by):
    n = SIZES[axis]
    return lax.ppermute(x, axis, [(i, (i + by) % n) for i in range(n)])


def mm(a, b):
    return jnp.dot(a, b, preferred_element_type=F32)


def pack_keys(k, v, tk, tv, kp):
    for h in range(NH):
        cols = slice(h * DH, (h + 1) * DH)
        kp[2 * h] = k[:, cols]
        kp[2 * h + 1] = tk[:, cols]
        kp[2 * NH + 2 * h] = v[:, cols].T
        kp[2 * NH + 2 * h + 1] = tv[:, cols].T


def pack_kernel(q, k, v, tq, tk, tv, kp, qp):
    pack_keys(k, v, tk, tv, kp)
    for h in range(NH):
        cols = slice(h * DH, (h + 1) * DH)
        qp[2 * h] = q[:, cols].T
        qp[2 * h + 1] = tq[:, cols].T


def pack(q, k, v, tq, tk, tv):
    return pl.pallas_call(
        pack_kernel,
        out_shape=(
            jax.ShapeDtypeStruct((4 * NH, TB, DH), BF16),
            jax.ShapeDtypeStruct((2 * NH, DH, TB), BF16),
        ),
        in_specs=[VMEM] * 6,
        out_specs=(VMEM, VMEM),
        name="pack",
    )(q, k, v, tq, tk, tv)


def scores_of(q_ref, kparts, h):
    q = jnp.concatenate([q_ref[0, 2 * h], q_ref[1, 2 * h]], axis=1)
    tq = jnp.concatenate([q_ref[0, 2 * h + 1], q_ref[1, 2 * h + 1]], axis=1)
    k = jnp.concatenate([r[2 * h] for r in kparts], axis=0)
    tk = jnp.concatenate([r[2 * h + 1] for r in kparts], axis=0)
    return mm(k, q), mm(jnp.concatenate([k, tk], axis=1), jnp.concatenate([tq, q], axis=0))


def absorb(scores, tan, vparts, vbase, h, state):
    top = jnp.max(scores, axis=0, keepdims=True) * SCALE2
    if state is not None:
        acc, st = state
        top = jnp.maximum(st[0:1], top)
        keep = jnp.exp2(st[0:1] - top)
    w = jnp.exp2(scores * SCALE2 - top)
    tw = w * tan
    den = jnp.sum(w, axis=0, keepdims=True)
    tden = jnp.sum(tw, axis=0, keepdims=True)
    v = jnp.concatenate([r[vbase + 2 * h] for r in vparts], axis=1)
    tv = jnp.concatenate([r[vbase + 2 * h + 1] for r in vparts], axis=1)
    both = mm(jnp.concatenate([v, tv], axis=0), w.astype(BF16))
    a = both[:DH]
    b = both[DH:] + mm(v, tw.astype(BF16)) * SCALE
    if state is not None:
        a = a + acc[:DH] * keep
        b = b + acc[DH:] * keep
        den = den + st[1:2] * keep
        tden = tden + st[2:3] * keep
    return top, den, tden, a, b


def pipeline(units):
    waiting = []
    for front, back in units:
        waiting.append((back, front()))
        if len(waiting) > 2:
            ready, made = waiting.pop(0)
            ready(*made)
    for ready, made in waiting:
        ready(*made)


def attend_kernel(plan, nk, had, *refs):
    qs, blocks, refs = refs[:4], refs[4 : 4 + nk], refs[4 + nk :]
    if had:
        acc_in, st_in, acc_out, st_out = refs
    else:
        acc_out, st_out, own = refs
        pack_keys(*blocks[:4], own)
        blocks = (own, *blocks[4:])

    def make(s, h):
        parts = [blocks[i] for i in plan[s][0]]

        def back(scores, tan):
            state = (acc_in[s, h], st_in[s, h]) if plan[s][1] else None
            top, den, tden, a, b = absorb(scores, tan, parts, 2 * NH, h, state)
            acc_out[s, h, :DH] = a
            acc_out[s, h, DH:] = b
            st_out[s, h] = jnp.concatenate([top, den, tden, jnp.zeros((5, 2 * TB), F32)], axis=0)

        return lambda: scores_of(qs[s], parts, h), back

    pipeline([make(s, h) for s in range(4) for h in range(NH) if plan[s][0]])


def attend(qs, blocks, plan, state=()):
    operands = [*qs, *blocks, *state]
    n, had = len(operands), bool(state)
    keys = TB * sum(len(numbers) for numbers, _ in plan)
    return pl.pallas_call(
        functools.partial(attend_kernel, plan, len(blocks), had),
        out_shape=(
            jax.ShapeDtypeStruct((4, NH, 2 * DH, 2 * TB), F32),
            jax.ShapeDtypeStruct((4, NH, 8, 2 * TB), F32),
        ),
        in_specs=[VMEM] * n,
        out_specs=(VMEM, VMEM),
        input_output_aliases={n - 2: 0, n - 1: 1} if had else {},
        scratch_shapes=[] if had else [pltpu.VMEM((4 * NH, TB, DH), BF16)],
        compiler_params=pltpu.CompilerParams(vmem_limit_bytes=16 << 20),
        cost_estimate=pl.CostEstimate(
            flops=2 * 2 * TB * DH * NH * keys * 8, bytes_accessed=8 << 20, transcendentals=2 * TB * NH * keys
        ),
        name=f"attend{keys}",
    )(*operands)


def close_kernel(at, q0, q1, q2, q3, kfar, vfar, acc, st, out, held, sems):
    qs = (q0, q1, q2, q3)
    places = [[lax.bitwise_xor(at[0], x) * 4 + lax.bitwise_and(at[1] + d, 3) for x in range(2)] for d in (0, 3, 1, 2)]
    stat_rows, copies = {}, []

    def make(s, h):
        def back(scores, tan):
            top, den, tden, a, b = absorb(scores, tan, [vfar], 0, h, (acc[s, h], st[s, h]))
            inv = 1.0 / den
            ratio = tden * SCALE * inv
            o = a * inv
            t = b * inv - o * ratio
            lse = top + jnp.log2(den)
            l0 = lse.astype(BF16)
            rest = lse - l0.astype(F32)
            l1 = rest.astype(BF16)
            l2 = (rest - l1.astype(F32)).astype(BF16)
            r0 = ratio.astype(BF16)
            r1 = (ratio - r0.astype(F32)).astype(BF16)
            for x in range(2):
                lanes = slice(x * TB, (x + 1) * TB)
                ot, tt = o[:, lanes].astype(BF16).T, t[:, lanes].astype(BF16).T
                for to in range(4):
                    rows = slice(to * 32, (to + 1) * 32)
                    held[2 * s + x, to, 64 * h : 64 * h + 32] = ot[rows]
                    held[2 * s + x, to, 64 * h + 32 : 64 * h + 64] = tt[rows]
                stat_rows.setdefault((s, x), []).extend(
                    piece[:, lanes].astype(F32) for piece in (l0, l1, l2, r0, r1)
                )
            if h == NH - 1:
                for x in range(2):
                    rows = jnp.concatenate(stat_rows[s, x] + [jnp.zeros((1, TB), F32)], axis=0).astype(BF16)
                    for to in range(4):
                        held[2 * s + x, to, 64 * NH : PART] = rows
                    copies.append(
                        pltpu.make_async_copy(held.at[2 * s + x], out.at[places[s][x]], sems.at[2 * s + x])
                    )
                    copies[-1].start()

        return lambda: scores_of(qs[s], [kfar], h), back

    pipeline([make(s, h) for s in range(4) for h in range(NH)])
    for copy in copies:
        copy.wait()


def close(at, qs, far, state):
    return pl.pallas_call(
        close_kernel,
        out_shape=jax.ShapeDtypeStruct((8, 4, PART, DH), BF16),
        in_specs=[SMEM] + [VMEM] * 8,
        out_specs=HBM,
        scratch_shapes=[pltpu.VMEM((8, 4, PART, DH), BF16), pltpu.SemaphoreType.DMA((8,))],
        compiler_params=pltpu.CompilerParams(vmem_limit_bytes=16 << 20),
        cost_estimate=pl.CostEstimate(
            flops=2 * 8 * TB * DH * NH * TB * 8, bytes_accessed=8 << 20, transcendentals=8 * TB * NH * TB
        ),
        name="close",
    )(at, *qs, *far, *state)


def project_kernel(me, got_hbm, w0, w1a, w1b, w2, w3a, w3b, out, tan_out, rows, w, total, got, sems, got_sem):
    received = pltpu.make_async_copy(got_hbm, got, got_sem)
    received.start()
    half = w1a.shape[0]
    whole = [
        [(w0, 0)],
        [(w1a, 0), (w1b, half)],
        [(w2, 0)],
        [(w3a, 0), (w3b, half)],
    ]
    copies = [
        [
            pltpu.make_async_copy(src, w.at[g, pl.ds(at, src.shape[0])], sems.at[g, i])
            for i, (src, at) in enumerate(parts)
        ]
        for g, parts in enumerate(whole)
    ]
    for copy in sum(copies, []):
        copy.start()
    received.wait()
    share, tilt = [], []
    for g in range(4):
        st = got[:, lax.bitwise_xor(me[0], g), 64 * NH : PART].astype(F32)
        for h in range(NH):
            lse = st[:, 5 * h] + st[:, 5 * h + 1] + st[:, 5 * h + 2]
            ratio = st[:, 5 * h + 3] + st[:, 5 * h + 4]
            part_of = jnp.exp2(lse - jnp.max(lse, axis=0, keepdims=True))
            part_of = part_of / jnp.sum(part_of, axis=0, keepdims=True)
            share.append(part_of)
            tilt.append(part_of * (ratio - jnp.sum(part_of * ratio, axis=0, keepdims=True)))
    group = lax.broadcasted_iota(jnp.int32, (8, TB), 1) // 32
    part = lax.broadcasted_iota(jnp.int32, (8, TB), 0) % 4
    row = lax.broadcasted_iota(jnp.int32, (32, TB), 0)
    diagonal = lax.broadcasted_iota(jnp.int32, (32, TB), 1) % 32 == row

    def spread(w):
        turned = w
        for i in range(1, 4):
            turned = jnp.where(part == i, pltpu.roll(w, 32 * i, axis=1), turned)
        turned = pltpu.roll(turned, lax.rem(4 - me[0], 4) * 32, axis=1)
        picked = jnp.where(group == part, turned, 0.0)
        halves = [jnp.sum(picked[4 * i : 4 * i + 4], axis=0, keepdims=True) for i in range(2)]
        return jnp.concatenate([jnp.where(diagonal, half, 0.0) for half in halves], axis=1).astype(BF16)

    for g in range(4):
        j = lax.bitwise_xor(me[0], g)
        for h in range(NH):
            mix = jnp.concatenate([spread(share[g * NH + h]), spread(tilt[g * NH + h])], axis=0)
            o = jnp.concatenate([got[i, j, 64 * h : 64 * h + 32] for i in range(8)], axis=0)
            t = jnp.concatenate([got[i, j, 64 * h + 32 : 64 * h + 64] for i in range(8)], axis=0)
            both = mm(mix, jnp.concatenate([o, t], axis=1))
            rows[g, :32, h * DH : (h + 1) * DH] = both[:32, :DH].astype(BF16)
            rows[g, 32:, h * DH : (h + 1) * DH] = (both[:32, DH:] + both[32:, :DH]).astype(BF16)

    for g in range(4):
        for copy in copies[g]:
            copy.wait()
        for c in range(0, out.shape[1], CHUNK):
            cols = slice(c, c + CHUNK)
            term = mm(rows[g], w[g, :, cols])
            if g == 0:
                total[:, cols] = term
            elif g < 3:
                total[:, cols] += term
            else:
                term = term + total[:, cols]
                out[:, cols] = term[:32].astype(BF16)
                tan_out[:, cols] = term[32:].astype(BF16)


def project(me, got, weights):
    depth, width = weights[0].shape
    oshape = jax.ShapeDtypeStruct((32, width), BF16)
    return pl.pallas_call(
        project_kernel,
        out_shape=(oshape, oshape),
        in_specs=[SMEM] + [pl.BlockSpec(memory_space=pl.ANY)] * 7,
        out_specs=(VMEM, VMEM),
        scratch_shapes=[
            pltpu.VMEM((4, 64, NH * DH), BF16),
            pltpu.VMEM((4, depth, width), BF16),
            pltpu.VMEM((64, width), F32),
            pltpu.VMEM((8, 4, PART, DH), BF16),
            pltpu.SemaphoreType.DMA((4, 2)),
            pltpu.SemaphoreType.DMA,
        ],
        compiler_params=pltpu.CompilerParams(vmem_limit_bytes=20 << 20),
        cost_estimate=pl.CostEstimate(
            flops=2 * 64 * 4 * depth * width, bytes_accessed=4 * depth * width * 2, transcendentals=0
        ),
        name="project",
    )(me, got, *weights)


def on_device(queries, keys, values, tan_queries, tan_keys, tan_values, out_weight):
    xlo, y = lax.axis_index("xlo"), lax.axis_index("y")
    me = lax.axis_index("xhi") * 2 + lax.axis_index("core")
    kp, qp = pack(queries, keys, values, tan_queries, tan_keys, tan_values)

    across = lax.ppermute(out_weight, ("xlo", "xhi"), [(2, 1), (1, 2), (3, 0), (0, 3)])

    r1, l1 = shift(kp, "z", 1), shift(kp, "z", -1)
    q0 = jnp.stack([qp, shift(qp, "xlo", 1)])
    qa, qb = shift(q0, "y", 1), shift(q0, "y", -1)
    r2, l2 = shift(r1, "z", 1), shift(l1, "z", -1)
    q0, qa, qb = lax.optimization_barrier((q0, qa, qb))
    qc = shift(q0, "y", 2)
    r3, l3 = shift(r2, "z", 1), shift(l2, "z", -1)
    qs = (q0, qa, qb, qc)
    at = jnp.stack([xlo, y]).astype(jnp.int32)

    state = attend(qs, (keys, values, tan_keys, tan_values, r1, l1, r2), [((0, 1, 2, 3), False)] * 4)
    r3, l3, *state = lax.optimization_barrier((r3, l3, *state))
    far = (shift(r3[: 2 * NH], "z", 1), shift(l3[2 * NH :], "z", -1))
    state = attend(qs, (l2, r3, l3), [((0, 1, 2), True)] * 4, state)
    sent = close(at, qs, far, state)
    got = lax.all_to_all(sent.reshape(32, PART, DH), ("xlo", "y", "xhi", "core"), 0, 0, tiled=True)
    across, own = lax.optimization_barrier((across, out_weight))
    half = out_weight.shape[0] // 2
    other = [shift(own[i : i + half], "core", 1) for i in (0, half)]
    across_other = [shift(across[i : i + half], "core", 1) for i in (0, half)]
    weights = (out_weight, *other, across, *across_other)
    return project(jnp.reshape(me, (1,)).astype(jnp.int32), got.reshape(8, 4, PART, DH), weights)


def solution(mesh):
    fine = Mesh(mesh.devices.reshape([SIZES[a] for a in AXES]), AXES)
    blk, head = ("xlo", "z", "y"), ("xhi", "core")
    spec = P(blk, head)
    return jax.shard_map(
        on_device,
        mesh=fine,
        in_specs=(spec,) * 6 + (P(head, None),),
        out_specs=(P(blk + head, None),) * 2,
        check_vma=False,
    )
```

time: 92.1 us -> 88.8 us (0.964)
  Pallas kernels: 20.5 us -> 18 us
  local copies, waits for them, and re-layouts: 5.98 us -> 5.01 us
    pallas_call x3, Pallas kernels: 12.6 us -> 11.3 us  [the longest x2 7.9 us: attend(): pl.pallas_call(functools.partial(attend_kernel, plan, len(blocks), had),...]
    pallas_call x1, Pallas kernels: 5.78 us -> 4.73 us  [project(): pl.pallas_call(project_kernel, out_shape=(oshape, oshape), in_specs=[SMEM...]
    unnamed x4 -> x10, local copies, waits for them, and re-layouts: 1 us -> 0.02 us
  transfers between devices with their start and end apart: 18 -> 18, of which waited for: 6 -> 6; matrix products, arithmetic and copies ran while one was open for 7% -> 7% of each run, Pallas kernels for 16% -> 15%
where the time goes in v4:
time: 88.8 us; the launch traced here: 88.6 us
  starting transfers between devices  33.3 us (37%)
  waiting for transfers between devices  30.2 us (34%)
  Pallas kernels  18 us (20%)
  local copies, waits for them, and re-layouts  5.01 us (6%)
  other arithmetic  1.04 us (1%)
  between operations  0.95 us (1%)
    ppermute x16, starting transfers between devices, shift(): return lax.ppermute(x, axis, [(i, (i + by) % n) for i in range(n)])  20.6 us
    all_to_all x1, waiting for transfers between devices, on_device(): lax.all_to_all(sent.reshape(32, PART, DH), ('xlo', 'y', 'xhi', 'core'), 0...  18.2 us
    ppermute x16, waiting for transfers between devices, shift(): return lax.ppermute(x, axis, [(i, (i + by) % n) for i in range(n)])  12.1 us
    all_to_all x1, starting transfers between devices, on_device(): lax.all_to_all(sent.reshape(32, PART, DH), ('xlo', 'y', 'xhi', 'core'), 0...  9.29 us
    pallas_call x2, Pallas kernels, attend(): pl.pallas_call(functools.partial(attend_kernel, plan, len(blocks), had),...  7.9 us
    pallas_call x1, Pallas kernels, project(): pl.pallas_call(project_kernel, out_shape=(oshape, oshape), in_specs=[SMEM...  4.73 us
    ppermute x1, starting transfers between devices, on_device(): lax.ppermute(out_weight, ('xlo', 'xhi'), [(2, 1), (1, 2), (3, 0), (0, 3)])  3.39 us
    pallas_call x1, Pallas kernels, close(): pl.pallas_call(close_kernel, out_shape=jax.ShapeDtypeStruct((8, 4, PART,...  3.36 us
  transfers between devices with their start and end apart: 18, of which 6 were waited for; matrix products, arithmetic and copies ran while one was open for 7% of the time, Pallas kernels for 15%

profile of v4, /device:TPU:1, one launch (start us, length us, event | category | flops | bytes accessed | tf_op | source)
XLA Modules:
  0.0 88.6 jit_solution(14381948011272968801)
XLA Ops:
  0.6 0.0 copy-start.3
  0.7 3.4 %collective-permute-start.12 = (bf16[384,3072]{1,0:T(8,128)(2,1)}, bf16[384,3072]{1,0:T(8,128)(2,1)}, u32[]{:S(2)}, u32[]{:S(2)}) collective-permute-start(bf16[384,3072]{1,0:T(8,128)(2,1)} %w0.1), channel_id=1, source_target_pairs={{128,2},{2,128},{130,0},{0,130},{129,3},{3,129},{131,1},{1,131},{1... | collective-permute-start | bytes 7077896 | tf_op jit(solution)/shard_map/ppermute | solution.py:313
  4.1 2.1 %pack.1 = (bf16[12,128,128]{2,1,0:T(8,128)(2,1)}, bf16[6,128,128]{2,1,0:T(8,128)(2,1)}) custom-call(bf16[128,384]{1,0:T(8,128)(2,1)} %q.1, bf16[128,384]{1,0:T(8,128)(2,1)} %refs_4_.1, bf16[128,384]{1,0:T(8,128)(2,1)} %refs_5_.1, bf16[128,384]{1,0:T(8,128)(2,1)} %tq.1, bf16[128,384]{1,0:T(8,128)(2,1)} %refs_6_.1, bf16[128,384]{1,0:T(8,128)(2,1)} %refs_7_.1), custom_call_target="tpu_custom_call" | custom-call | tf_op jit(solution)/shard_map/pack/pallas_call | solution.py:53
  6.1 0.0 collective-permute-start
  6.1 1.6 %collective-permute-start.4 = (bf16[12,128,128]{2,1,0:T(8,128)(2,1)}, bf16[12,128,128]{2,1,0:T(8,128)(2,1)S(1)}, u32[]{:S(2)}, u32[]{:S(2)}) collective-permute-start(bf16[12,128,128]{2,1,0:T(8,128)(2,1)} %get-tuple-element.21), channel_id=1, source_target_pairs={{0,16},{16,32},{32,48},{48,64},{64,80},{80,96},{96,112},{112,0},{1... | collective-permute-start | bytes 1179656 | tf_op jit(solution)/shard_map/ppermute | solution.py:28
  7.8 4.0 %collective-permute-start.7 = (bf16[12,128,128]{2,1,0:T(8,128)(2,1)}, bf16[12,128,128]{2,1,0:T(8,128)(2,1)S(1)}, u32[]{:S(2)}, u32[]{:S(2)}) collective-permute-start(bf16[12,128,128]{2,1,0:T(8,128)(2,1)} %get-tuple-element.21), channel_id=1, source_target_pairs={{0,112},{16,0},{32,16},{48,32},{64,48},{80,64},{96,80},{112,96},{1... | collective-permute-start | bytes 1179656 | tf_op jit(solution)/shard_map/ppermute | solution.py:28
  11.8 0.1 collective-permute-done
  11.9 1.0 %pad_maximum_fusion.refs_0_.q0 = bf16[2,6,128,128]{3,2,1,0:T(8,128)(2,1)S(1)} fusion(bf16[1,6,128,128]{3,2,1,0:T(8,128)(2,1)S(1)} %bitcast.8, bf16[1,6,128,128]{3,2,1,0:T(8,128)(2,1)} %bitcast.7), kind=kLoop, calls=%fused_computation | loop fusion | flops 196608 | bytes 786432 | tf_op jit(solution)/shard_map/stack | solution.py:316
  12.9 1.4 %collective-permute-start.1 = (bf16[2,6,128,128]{3,2,1,0:T(8,128)(2,1)S(1)}, bf16[2,6,128,128]{3,2,1,0:T(8,128)(2,1)S(1)}, u32[]{:S(2)}, u32[]{:S(2)}) collective-permute-start(bf16[2,6,128,128]{3,2,1,0:T(8,128)(2,1)S(1)} %pad_maximum_fusion.refs_0_.q0), channel_id=1, source_target_pairs={{0,4},{4,8},{8,12},{12,0},{1,5},{5,9},{9,13},{13,1},{2,6},{6,10},{... | collective-permute-start | bytes 1179656 | tf_op jit(solution)/shard_map/ppermute | solution.py:28
  14.2 1.5 %collective-permute-start.2 = (bf16[2,6,128,128]{3,2,1,0:T(8,128)(2,1)S(1)}, bf16[2,6,128,128]{3,2,1,0:T(8,128)(2,1)S(1)}, u32[]{:S(2)}, u32[]{:S(2)}) collective-permute-start(bf16[2,6,128,128]{3,2,1,0:T(8,128)(2,1)S(1)} %pad_maximum_fusion.refs_0_.q0), channel_id=1, source_target_pairs={{0,12},{4,0},{8,4},{12,8},{1,13},{5,1},{9,5},{13,9},{2,14},{6,2},{... | collective-permute-start | bytes 1179656 | tf_op jit(solution)/shard_map/ppermute | solution.py:28
  15.8 4.5 %collective-permute-done.4.refs_8_ = bf16[12,128,128]{2,1,0:T(8,128)(2,1)S(1)} collective-permute-done((bf16[12,128,128]{2,1,0:T(8,128)(2,1)}, bf16[12,128,128]{2,1,0:T(8,128)(2,1)S(1)}, u32[]{:S(2)}, u32[]{:S(2)}) %collective-permute-start.4) | collective-permute-done | bytes 393248 | tf_op jit(solution)/shard_map/ppermute | solution.py:28
  20.3 0.0 collective-permute-start.5
  20.3 0.0 collective-permute-done.7.refs_9_
  20.3 2.7 %collective-permute-start.8 = (bf16[12,128,128]{2,1,0:T(8,128)(2,1)S(1)}, bf16[12,128,128]{2,1,0:T(8,128)(2,1)S(1)}, u32[]{:S(2)}, u32[]{:S(2)}) collective-permute-start(bf16[12,128,128]{2,1,0:T(8,128)(2,1)S(1)} %collective-permute-done.7.refs_9_), channel_id=1, source_target_pairs={{0,112},{16,0},{32,16},{48,32},{64,48},{80,64},{96,80},{112,96},{1... | collective-permute-start | bytes 1179656 | tf_op jit(solution)/shard_map/ppermute | solution.py:28
  23.0 0.3 collective-permute-done.1.refs_1_.q1
  23.2 0.0 collective-permute-done.2.refs_2_.q2
  23.2 2.7 %collective-permute-start.3 = (bf16[2,6,128,128]{3,2,1,0:T(8,128)(2,1)S(1)}, bf16[2,6,128,128]{3,2,1,0:T(8,128)(2,1)S(1)}, u32[]{:S(2)}, u32[]{:S(2)}) collective-permute-start(bf16[2,6,128,128]{3,2,1,0:T(8,128)(2,1)S(1)} %pad_maximum_fusion.refs_0_.q0), channel_id=1, source_target_pairs={{0,8},{4,12},{8,0},{12,4},{1,9},{5,13},{9,1},{13,5},{2,10},{6,14},... | collective-permute-start | bytes 1179656 | tf_op jit(solution)/shard_map/ppermute | solution.py:28
  25.9 4.6 %collective-permute-done.5.refs_10_ = bf16[12,128,128]{2,1,0:T(8,128)(2,1)S(1)} collective-permute-done((bf16[12,128,128]{2,1,0:T(8,128)(2,1)S(1)}, bf16[12,128,128]{2,1,0:T(8,128)(2,1)S(1)}, u32[]{:S(2)}, u32[]{:S(2)}) %collective-permute-start.5) | collective-permute-done | bytes 393248 | tf_op jit(solution)/shard_map/ppermute | solution.py:28
  30.5 0.0 collective-permute-start.6
  30.5 0.0 collective-permute-done.8.refs_4_
  30.5 2.7 %collective-permute-start.9 = (bf16[12,128,128]{2,1,0:T(8,128)(2,1)S(1)}, bf16[12,128,128]{2,1,0:T(8,128)(2,1)S(1)}, u32[]{:S(2)}, u32[]{:S(2)}) collective-permute-start(bf16[12,128,128]{2,1,0:T(8,128)(2,1)S(1)} %collective-permute-done.8.refs_4_), channel_id=1, source_target_pairs={{0,112},{16,0},{32,16},{48,32},{64,48},{80,64},{96,80},{112,96},{1... | collective-permute-start | bytes 1179656 | tf_op jit(solution)/shard_map/ppermute | solution.py:28
  33.2 0.1 pad_add_fusion.at
  33.3 0.0 collective-permute-done.3.refs_3_.q3
  33.3 0.0 copy-done.3
  33.3 4.1 %attend2048.1 = (f32[4,3,256,256]{3,2,1,0:T(8,128)S(1)}, f32[4,3,8,256]{3,2,1,0:T(8,128)S(1)}) custom-call(bf16[2,6,128,128]{3,2,1,0:T(8,128)(2,1)S(1)} %pad_maximum_fusion.refs_0_.q0, bf16[2,6,128,128]{3,2,1,0:T(8,128)(2,1)S(1)} %collective-permute-done.1.refs_1_.q1, bf16[2,6,128,128]{3,2,1,0:T(8,128)(2,1)S(1)} %collective-permute-done.2.refs_2_.q2, ...), custom_call_target="tpu_custom_call" | custom-call | flops 3221225472 | bytes 8388608 | tf_op jit(solution)/shard_map/attend2048/pallas_call | solution.py:135
  37.4 2.5 %collective-permute-done.6.refs_5_ = bf16[12,128,128]{2,1,0:T(8,128)(2,1)S(1)} collective-permute-done((bf16[12,128,128]{2,1,0:T(8,128)(2,1)S(1)}, bf16[12,128,128]{2,1,0:T(8,128)(2,1)S(1)}, u32[]{:S(2)}, u32[]{:S(2)}) %collective-permute-start.6) | collective-permute-done | bytes 393248 | tf_op jit(solution)/shard_map/ppermute | solution.py:28
  39.9 0.0 collective-permute-done.9.refs_6_
  39.9 0.3 collective-permute-start.10
  40.2 2.7 %collective-permute-start.11 = (bf16[6,128,128]{2,1,0:T(8,128)(2,1)S(1)}, bf16[6,128,128]{2,1,0:T(8,128)(2,1)S(1)}, u32[]{:S(2)}, u32[]{:S(2)}) collective-permute-start(bf16[6,128,128]{2,1,0:T(8,128)(2,1)S(1)} %slice.19), channel_id=1, source_target_pairs={{0,112},{16,0},{32,16},{48,32},{64,48},{80,64},{96,80},{112,96},{1... | collective-permute-start | bytes 589832 | tf_op jit(solution)/shard_map/ppermute | solution.py:28
  43.0 3.8 %attend1536.1 = (f32[4,3,256,256]{3,2,1,0:T(8,128)S(1)}, f32[4,3,8,256]{3,2,1,0:T(8,128)S(1)}) custom-call(bf16[2,6,128,128]{3,2,1,0:T(8,128)(2,1)S(1)} %pad_maximum_fusion.refs_0_.q0, bf16[2,6,128,128]{3,2,1,0:T(8,128)(2,1)S(1)} %collective-permute-done.1.refs_1_.q1, ...), custom_call_target="tpu_custom_call", output_to_operand_aliasing={{0}: (7, {}), {1}: (8, {})} | custom-call | flops 2415919104 | bytes 8388608 | tf_op jit(solution)/shard_map/attend1536/pallas_call | solution.py:135
  46.8 0.0 collective-permute-done.10.kfar
  46.8 0.0 collective-permute-done.11.vfar
  46.8 3.4 %close.1 = bf16[8,4,208,128]{3,2,1,0:T(8,128)(2,1)} custom-call(s32[2]{0:T(128)S(1)} %pad_add_fusion.at, bf16[2,6,128,128]{3,2,1,0:T(8,128)(2,1)S(1)} %pad_maximum_fusion.refs_0_.q0, bf16[2,6,128,128]{3,2,1,0:T(8,128)(2,1)S(1)} %collective-permute-done.1.refs_1_.q1, bf16[2,6,128,128]{3,2,1,0:T(8,128)(2,1)S(1)} %collective-permute-done.2.refs_2_.q2, ...), custom_call_target="tpu_custom_call" | custom-call | flops 805306368 | bytes 8388608 | tf_op jit(solution)/shard_map/close/pallas_call | solution.py:200
  50.2 9.3 %all-to-all-start = ((bf16[32,208,128]{2,1,0:T(8,128)(2,1)}), bf16[32,208,128]{2,1,0:T(8,128)(2,1)}, u32[]{:S(2)}, u32[]{:S(2)}) async-start(bf16[32,208,128]{2,1,0:T(8,128)(2,1)} %bitcast.5), calls=%async_computation | async-start | bytes 3407872 | tf_op jit(solution)/shard_map/all_to_all | solution.py:330
  59.5 0.0 collective-permute-done.12.w2
  59.5 0.0 copy-start
  59.5 3.3 %fusion = (bf16[192,3072]{1,0:T(8,128)(2,1)}, bf16[192,3072]{1,0:T(8,128)(2,1)}) fusion(bf16[384,3072]{1,0:T(8,128)(2,1)} %collective-permute-done.12.w2), kind=kLoop, calls=%fused_computation.2 | loop fusion | bytes 4718592 | tf_op jit(solution)/shard_map/slice | solution.py:334
  62.8 0.3 collective-permute-start.15
  63.1 0.2 collective-permute-start.16
  63.3 1.6 %fusion.1 = (bf16[192,3072]{1,0:T(8,128)(2,1)}, bf16[192,3072]{1,0:T(8,128)(2,1)}) fusion(bf16[384,3072]{1,0:T(8,128)(2,1)S(1)} %copy-done), kind=kLoop, calls=%fused_computation.3 | loop fusion | bytes 4718592 | tf_op jit(solution)/shard_map/slice | solution.py:333
  64.9 0.3 collective-permute-start.13
  65.2 0.2 collective-permute-start.14
  65.5 18.2 %all-to-all-done = bf16[32,208,128]{2,1,0:T(8,128)(2,1)} async-done(((bf16[32,208,128]{2,1,0:T(8,128)(2,1)}), bf16[32,208,128]{2,1,0:T(8,128)(2,1)}, u32[]{:S(2)}, u32[]{:S(2)}) %all-to-all-start) | async-done | bytes 1703968 | tf_op jit(solution)/shard_map/all_to_all | solution.py:330
  83.6 0.0 collective-permute-done.15.w3a
  83.6 0.0 collective-permute-done.16.w3b
  83.6 0.0 collective-permute-done.13.w1a
  83.7 0.0 collective-permute-done.14.w1b
  83.7 4.7 %project.1 = (bf16[32,3072]{1,0:T(8,128)(2,1)}, bf16[32,3072]{1,0:T(8,128)(2,1)}) custom-call(s32[1]{0:T(128)} %bitcast.me, bf16[8,4,208,128]{3,2,1,0:T(8,128)(2,1)} %bitcast.6.got_hbm, bf16[384,3072]{1,0:T(8,128)(2,1)S(1)} %copy-done, bf16[192,3072]{1,0:T(8,128)(2,1)} %collective-permute-done.13.w1a, bf16[192,3072]{1,0:T(8,128)(2,1)} %collective-permute-done.14.w1b, ...), custom_call_target="tpu_custom_call" | custom-call | flops 603979776 | bytes 9437184 | tf_op jit(solution)/shard_map/project/pallas_call | solution.py:287
  (9 shorter events, 0.0 us)
Async XLA Ops:
  0.6 32.6 %copy-start.3 = (bf16[128,384]{1,0:T(8,128)(2,1)S(1)}, bf16[128,384]{1,0:T(8,128)(2,1)}, u32[]{:S(2)}) copy-start(bf16[128,384]{1,0:T(8,128)(2,1)} %refs_6_.1) | copy-start | bytes 294916
  0.6 32.6 %copy-start.4 = (bf16[128,384]{1,0:T(8,128)(2,1)S(1)}, bf16[128,384]{1,0:T(8,128)(2,1)}, u32[]{:S(2)}) copy-start(bf16[128,384]{1,0:T(8,128)(2,1)} %refs_7_.1) | copy-start | bytes 294916
  0.7 32.6 %copy-start.1 = (bf16[128,384]{1,0:T(8,128)(2,1)S(1)}, bf16[128,384]{1,0:T(8,128)(2,1)}, u32[]{:S(2)}) copy-start(bf16[128,384]{1,0:T(8,128)(2,1)} %refs_4_.1) | copy-start | bytes 294916
  0.7 32.6 %copy-start.2 = (bf16[128,384]{1,0:T(8,128)(2,1)S(1)}, bf16[128,384]{1,0:T(8,128)(2,1)}, u32[]{:S(2)}) copy-start(bf16[128,384]{1,0:T(8,128)(2,1)} %refs_5_.1) | copy-start | bytes 294916
  0.7 58.8 %collective-permute-start.12 = (bf16[384,3072]{1,0:T(8,128)(2,1)}, bf16[384,3072]{1,0:T(8,128)(2,1)}, u32[]{:S(2)}, u32[]{:S(2)}) collective-permute-start(bf16[384,3072]{1,0:T(8,128)(2,1)} %w0.1), channel_id=1, source_target_pairs={{128,2},{2,128},{130,0},{0,130},{129,3},{3,129},{131,1},{1,131},{1... | collective-permute-start | bytes 7077896 | tf_op jit(solution)/shard_map/ppermute | solution.py:313
  6.1 5.8 %collective-permute-start = (bf16[6,128,128]{2,1,0:T(8,128)(2,1)}, bf16[6,128,128]{2,1,0:T(8,128)(2,1)S(1)}, u32[]{:S(2)}, u32[]{:S(2)}) collective-permute-start(bf16[6,128,128]{2,1,0:T(8,128)(2,1)} %get-tuple-element.17), channel_id=1, source_target_pairs={{0,128},{128,0},{1,129},{129,1},{2,130},{130,2},{3,131},{131,3},{4... | collective-permute-start | bytes 589832 | tf_op jit(solution)/shard_map/ppermute | solution.py:28
  6.1 14.2 %collective-permute-start.4 = (bf16[12,128,128]{2,1,0:T(8,128)(2,1)}, bf16[12,128,128]{2,1,0:T(8,128)(2,1)S(1)}, u32[]{:S(2)}, u32[]{:S(2)}) collective-permute-start(bf16[12,128,128]{2,1,0:T(8,128)(2,1)} %get-tuple-element.21), channel_id=1, source_target_pairs={{0,16},{16,32},{32,48},{48,64},{64,80},{80,96},{96,112},{112,0},{1... | collective-permute-start | bytes 1179656 | tf_op jit(solution)/shard_map/ppermute | solution.py:28
  7.8 12.5 %collective-permute-start.7 = (bf16[12,128,128]{2,1,0:T(8,128)(2,1)}, bf16[12,128,128]{2,1,0:T(8,128)(2,1)S(1)}, u32[]{:S(2)}, u32[]{:S(2)}) collective-permute-start(bf16[12,128,128]{2,1,0:T(8,128)(2,1)} %get-tuple-element.21), channel_id=1, source_target_pairs={{0,112},{16,0},{32,16},{48,32},{64,48},{80,64},{96,80},{112,96},{1... | collective-permute-start | bytes 1179656 | tf_op jit(solution)/shard_map/ppermute | solution.py:28
  12.9 10.4 %collective-permute-start.1 = (bf16[2,6,128,128]{3,2,1,0:T(8,128)(2,1)S(1)}, bf16[2,6,128,128]{3,2,1,0:T(8,128)(2,1)S(1)}, u32[]{:S(2)}, u32[]{:S(2)}) collective-permute-start(bf16[2,6,128,128]{3,2,1,0:T(8,128)(2,1)S(1)} %pad_maximum_fusion.refs_0_.q0), channel_id=1, source_target_pairs={{0,4},{4,8},{8,12},{12,0},{1,5},{5,9},{9,13},{13,1},{2,6},{6,10},{... | collective-permute-start | bytes 1179656 | tf_op jit(solution)/shard_map/ppermute | solution.py:28
  14.2 9.0 %collective-permute-start.2 = (bf16[2,6,128,128]{3,2,1,0:T(8,128)(2,1)S(1)}, bf16[2,6,128,128]{3,2,1,0:T(8,128)(2,1)S(1)}, u32[]{:S(2)}, u32[]{:S(2)}) collective-permute-start(bf16[2,6,128,128]{3,2,1,0:T(8,128)(2,1)S(1)} %pad_maximum_fusion.refs_0_.q0), channel_id=1, source_target_pairs={{0,12},{4,0},{8,4},{12,8},{1,13},{5,1},{9,5},{13,9},{2,14},{6,2},{... | collective-permute-start | bytes 1179656 | tf_op jit(solution)/shard_map/ppermute | solution.py:28
  20.3 10.2 %collective-permute-start.5 = (bf16[12,128,128]{2,1,0:T(8,128)(2,1)S(1)}, bf16[12,128,128]{2,1,0:T(8,128)(2,1)S(1)}, u32[]{:S(2)}, u32[]{:S(2)}) collective-permute-start(bf16[12,128,128]{2,1,0:T(8,128)(2,1)S(1)} %collective-permute-done.4.refs_8_), channel_id=1, source_target_pairs={{0,16},{16,32},{32,48},{48,64},{64,80},{80,96},{96,112},{112,0},{1... | collective-permute-start | bytes 1179656 | tf_op jit(solution)/shard_map/ppermute | solution.py:28
  20.3 10.2 %collective-permute-start.8 = (bf16[12,128,128]{2,1,0:T(8,128)(2,1)S(1)}, bf16[12,128,128]{2,1,0:T(8,128)(2,1)S(1)}, u32[]{:S(2)}, u32[]{:S(2)}) collective-permute-start(bf16[12,128,128]{2,1,0:T(8,128)(2,1)S(1)} %collective-permute-done.7.refs_9_), channel_id=1, source_target_pairs={{0,112},{16,0},{32,16},{48,32},{64,48},{80,64},{96,80},{112,96},{1... | collective-permute-start | bytes 1179656 | tf_op jit(solution)/shard_map/ppermute | solution.py:28
  23.2 10.0 %collective-permute-start.3 = (bf16[2,6,128,128]{3,2,1,0:T(8,128)(2,1)S(1)}, bf16[2,6,128,128]{3,2,1,0:T(8,128)(2,1)S(1)}, u32[]{:S(2)}, u32[]{:S(2)}) collective-permute-start(bf16[2,6,128,128]{3,2,1,0:T(8,128)(2,1)S(1)} %pad_maximum_fusion.refs_0_.q0), channel_id=1, source_target_pairs={{0,8},{4,12},{8,0},{12,4},{1,9},{5,13},{9,1},{13,5},{2,10},{6,14},... | collective-permute-start | bytes 1179656 | tf_op jit(solution)/shard_map/ppermute | solution.py:28
  30.5 9.4 %collective-permute-start.6 = (bf16[12,128,128]{2,1,0:T(8,128)(2,1)S(1)}, bf16[12,128,128]{2,1,0:T(8,128)(2,1)S(1)}, u32[]{:S(2)}, u32[]{:S(2)}) collective-permute-start(bf16[12,128,128]{2,1,0:T(8,128)(2,1)S(1)} %collective-permute-done.5.refs_10_), channel_id=1, source_target_pairs={{0,16},{16,32},{32,48},{48,64},{64,80},{80,96},{96,112},{112,0},{1... | collective-permute-start | bytes 1179656 | tf_op jit(solution)/shard_map/ppermute | solution.py:28
  30.5 9.4 %collective-permute-start.9 = (bf16[12,128,128]{2,1,0:T(8,128)(2,1)S(1)}, bf16[12,128,128]{2,1,0:T(8,128)(2,1)S(1)}, u32[]{:S(2)}, u32[]{:S(2)}) collective-permute-start(bf16[12,128,128]{2,1,0:T(8,128)(2,1)S(1)} %collective-permute-done.8.refs_4_), channel_id=1, source_target_pairs={{0,112},{16,0},{32,16},{48,32},{64,48},{80,64},{96,80},{112,96},{1... | collective-permute-start | bytes 1179656 | tf_op jit(solution)/shard_map/ppermute | solution.py:28
  39.9 6.8 %collective-permute-start.10 = (bf16[6,128,128]{2,1,0:T(8,128)(2,1)S(1)}, bf16[6,128,128]{2,1,0:T(8,128)(2,1)S(1)}, u32[]{:S(2)}, u32[]{:S(2)}) collective-permute-start(bf16[6,128,128]{2,1,0:T(8,128)(2,1)S(1)} %slice.18), channel_id=1, source_target_pairs={{0,16},{16,32},{32,48},{48,64},{64,80},{80,96},{96,112},{112,0},{1... | collective-permute-start | bytes 589832 | tf_op jit(solution)/shard_map/ppermute | solution.py:28
  40.2 6.6 %collective-permute-start.11 = (bf16[6,128,128]{2,1,0:T(8,128)(2,1)S(1)}, bf16[6,128,128]{2,1,0:T(8,128)(2,1)S(1)}, u32[]{:S(2)}, u32[]{:S(2)}) collective-permute-start(bf16[6,128,128]{2,1,0:T(8,128)(2,1)S(1)} %slice.19), channel_id=1, source_target_pairs={{0,112},{16,0},{32,16},{48,32},{64,48},{80,64},{96,80},{112,96},{1... | collective-permute-start | bytes 589832 | tf_op jit(solution)/shard_map/ppermute | solution.py:28
  50.2 33.5 %all-to-all-start = ((bf16[32,208,128]{2,1,0:T(8,128)(2,1)}), bf16[32,208,128]{2,1,0:T(8,128)(2,1)}, u32[]{:S(2)}, u32[]{:S(2)}) async-start(bf16[32,208,128]{2,1,0:T(8,128)(2,1)} %bitcast.5), calls=%async_computation | async-start | bytes 3407872 | tf_op jit(solution)/shard_map/all_to_all | solution.py:330
  59.5 3.9 %copy-start = (bf16[384,3072]{1,0:T(8,128)(2,1)S(1)}, bf16[384,3072]{1,0:T(8,128)(2,1)}, u32[]{:S(2)}) copy-start(bf16[384,3072]{1,0:T(8,128)(2,1)} %w0.1) | copy-start | bytes 7077892
  62.8 20.8 %collective-permute-start.15 = (bf16[192,3072]{1,0:T(8,128)(2,1)}, bf16[192,3072]{1,0:T(8,128)(2,1)S(1)}, u32[]{:S(2)}, u32[]{:S(2)}) collective-permute-start(bf16[192,3072]{1,0:T(8,128)(2,1)} %get-tuple-element.33), channel_id=1, source_target_pairs={{0,1},{1,0},{2,3},{3,2},{4,5},{5,4},{6,7},{7,6},{8,9},{9,8},{10,11... | collective-permute-start | bytes 3538952 | tf_op jit(solution)/shard_map/ppermute | solution.py:28
  63.1 20.5 %collective-permute-start.16 = (bf16[192,3072]{1,0:T(8,128)(2,1)}, bf16[192,3072]{1,0:T(8,128)(2,1)}, u32[]{:S(2)}, u32[]{:S(2)}) collective-permute-start(bf16[192,3072]{1,0:T(8,128)(2,1)} %get-tuple-element.32), channel_id=1, source_target_pairs={{0,1},{1,0},{2,3},{3,2},{4,5},{5,4},{6,7},{7,6},{8,9},{9,8},{10,11... | collective-permute-start | bytes 3538952 | tf_op jit(solution)/shard_map/ppermute | solution.py:28
  64.9 18.7 %collective-permute-start.13 = (bf16[192,3072]{1,0:T(8,128)(2,1)}, bf16[192,3072]{1,0:T(8,128)(2,1)}, u32[]{:S(2)}, u32[]{:S(2)}) collective-permute-start(bf16[192,3072]{1,0:T(8,128)(2,1)} %get-tuple-element.35), channel_id=1, source_target_pairs={{0,1},{1,0},{2,3},{3,2},{4,5},{5,4},{6,7},{7,6},{8,9},{9,8},{10,11... | collective-permute-start | bytes 3538952 | tf_op jit(solution)/shard_map/ppermute | solution.py:28
  65.2 18.4 %collective-permute-start.14 = (bf16[192,3072]{1,0:T(8,128)(2,1)}, bf16[192,3072]{1,0:T(8,128)(2,1)}, u32[]{:S(2)}, u32[]{:S(2)}) collective-permute-start(bf16[192,3072]{1,0:T(8,128)(2,1)} %get-tuple-element.34), channel_id=1, source_target_pairs={{0,1},{1,0},{2,3},{3,2},{4,5},{5,4},{6,7},{7,6},{8,9},{9,8},{10,11... | collective-permute-start | bytes 3538952 | tf_op jit(solution)/shard_map/ppermute | solution.py:28

commit v5 on v4

--- a/solution.py
+++ b/solution.py
@@ -310,6 +310,7 @@
     me = lax.axis_index("xhi") * 2 + lax.axis_index("core")
     kp, qp = pack(queries, keys, values, tan_queries, tan_keys, tan_values)
 
+    _, qp = lax.optimization_barrier((shift(kp[0, :16], "core", 1), qp))
     across = lax.ppermute(out_weight, ("xlo", "xhi"), [(2, 1), (1, 2), (3, 0), (0, 3)])
 
     r1, l1 = shift(kp, "z", 1), shift(kp, "z", -1)

time: 88.8 us -> 88.8 us (level)
  no operation moved by 1% of the time
where the time goes in v5:
time: 88.8 us; the launch traced here: 88.6 us
  starting transfers between devices  33.3 us (37%)
  waiting for transfers between devices  30.2 us (34%)
  Pallas kernels  18 us (20%)
  local copies, waits for them, and re-layouts  5.01 us (6%)
  other arithmetic  1.04 us (1%)
  between operations  0.95 us (1%)
    ppermute x16, starting transfers between devices, shift(): return lax.ppermute(x, axis, [(i, (i + by) % n) for i in range(n)])  20.6 us
    all_to_all x1, waiting for transfers between devices, on_device(): lax.all_to_all(sent.reshape(32, PART, DH), ('xlo', 'y', 'xhi', 'core'), 0...  18.2 us
    ppermute x16, waiting for transfers between devices, shift(): return lax.ppermute(x, axis, [(i, (i + by) % n) for i in range(n)])  12.1 us
    all_to_all x1, starting transfers between devices, on_device(): lax.all_to_all(sent.reshape(32, PART, DH), ('xlo', 'y', 'xhi', 'core'), 0...  9.29 us
    pallas_call x2, Pallas kernels, attend(): pl.pallas_call(functools.partial(attend_kernel, plan, len(blocks), had),...  7.9 us
    pallas_call x1, Pallas kernels, project(): pl.pallas_call(project_kernel, out_shape=(oshape, oshape), in_specs=[SMEM...  4.73 us
    ppermute x1, starting transfers between devices, on_device(): lax.ppermute(out_weight, ('xlo', 'xhi'), [(2, 1), (1, 2), (3, 0), (0, 3)])  3.39 us
    pallas_call x1, Pallas kernels, close(): pl.pallas_call(close_kernel, out_shape=jax.ShapeDtypeStruct((8, 4, PART,...  3.36 us
  transfers between devices with their start and end apart: 18, of which 6 were waited for; matrix products, arithmetic and copies ran while one was open for 7% of the time, Pallas kernels for 15%

profile of v5, /device:TPU:1, one launch (start us, length us, event | category | flops | bytes accessed | tf_op | source)
XLA Modules:
  0.0 88.6 jit_solution(14381948011272968801)
XLA Ops:
  0.6 0.0 copy-start.3
  0.7 3.4 %collective-permute-start.12 = (bf16[384,3072]{1,0:T(8,128)(2,1)}, bf16[384,3072]{1,0:T(8,128)(2,1)}, u32[]{:S(2)}, u32[]{:S(2)}) collective-permute-start(bf16[384,3072]{1,0:T(8,128)(2,1)} %w0.1), channel_id=1, source_target_pairs={{128,2},{2,128},{130,0},{0,130},{129,3},{3,129},{131,1},{1,131},{1... | collective-permute-start | bytes 7077896 | tf_op jit(solution)/shard_map/ppermute | solution.py:314
  4.1 2.1 %pack.1 = (bf16[12,128,128]{2,1,0:T(8,128)(2,1)}, bf16[6,128,128]{2,1,0:T(8,128)(2,1)}) custom-call(bf16[128,384]{1,0:T(8,128)(2,1)} %q.1, bf16[128,384]{1,0:T(8,128)(2,1)} %refs_4_.1, bf16[128,384]{1,0:T(8,128)(2,1)} %refs_5_.1, bf16[128,384]{1,0:T(8,128)(2,1)} %tq.1, bf16[128,384]{1,0:T(8,128)(2,1)} %refs_6_.1, bf16[128,384]{1,0:T(8,128)(2,1)} %refs_7_.1), custom_call_target="tpu_custom_call" | custom-call | tf_op jit(solution)/shard_map/pack/pallas_call | solution.py:53
  6.1 0.0 collective-permute-start
  6.1 1.6 %collective-permute-start.4 = (bf16[12,128,128]{2,1,0:T(8,128)(2,1)}, bf16[12,128,128]{2,1,0:T(8,128)(2,1)S(1)}, u32[]{:S(2)}, u32[]{:S(2)}) collective-permute-start(bf16[12,128,128]{2,1,0:T(8,128)(2,1)} %get-tuple-element.21), channel_id=1, source_target_pairs={{0,16},{16,32},{32,48},{48,64},{64,80},{80,96},{96,112},{112,0},{1... | collective-permute-start | bytes 1179656 | tf_op jit(solution)/shard_map/ppermute | solution.py:28
  7.8 4.0 %collective-permute-start.7 = (bf16[12,128,128]{2,1,0:T(8,128)(2,1)}, bf16[12,128,128]{2,1,0:T(8,128)(2,1)S(1)}, u32[]{:S(2)}, u32[]{:S(2)}) collective-permute-start(bf16[12,128,128]{2,1,0:T(8,128)(2,1)} %get-tuple-element.21), channel_id=1, source_target_pairs={{0,112},{16,0},{32,16},{48,32},{64,48},{80,64},{96,80},{112,96},{1... | collective-permute-start | bytes 1179656 | tf_op jit(solution)/shard_map/ppermute | solution.py:28
  11.8 0.1 collective-permute-done
  11.9 1.0 %pad_maximum_fusion.refs_0_.q0 = bf16[2,6,128,128]{3,2,1,0:T(8,128)(2,1)S(1)} fusion(bf16[1,6,128,128]{3,2,1,0:T(8,128)(2,1)S(1)} %bitcast.8, bf16[1,6,128,128]{3,2,1,0:T(8,128)(2,1)} %bitcast.7), kind=kLoop, calls=%fused_computation | loop fusion | flops 196608 | bytes 786432 | tf_op jit(solution)/shard_map/stack | solution.py:317
  12.9 1.4 %collective-permute-start.1 = (bf16[2,6,128,128]{3,2,1,0:T(8,128)(2,1)S(1)}, bf16[2,6,128,128]{3,2,1,0:T(8,128)(2,1)S(1)}, u32[]{:S(2)}, u32[]{:S(2)}) collective-permute-start(bf16[2,6,128,128]{3,2,1,0:T(8,128)(2,1)S(1)} %pad_maximum_fusion.refs_0_.q0), channel_id=1, source_target_pairs={{0,4},{4,8},{8,12},{12,0},{1,5},{5,9},{9,13},{13,1},{2,6},{6,10},{... | collective-permute-start | bytes 1179656 | tf_op jit(solution)/shard_map/ppermute | solution.py:28
  14.2 1.5 %collective-permute-start.2 = (bf16[2,6,128,128]{3,2,1,0:T(8,128)(2,1)S(1)}, bf16[2,6,128,128]{3,2,1,0:T(8,128)(2,1)S(1)}, u32[]{:S(2)}, u32[]{:S(2)}) collective-permute-start(bf16[2,6,128,128]{3,2,1,0:T(8,128)(2,1)S(1)} %pad_maximum_fusion.refs_0_.q0), channel_id=1, source_target_pairs={{0,12},{4,0},{8,4},{12,8},{1,13},{5,1},{9,5},{13,9},{2,14},{6,2},{... | collective-permute-start | bytes 1179656 | tf_op jit(solution)/shard_map/ppermute | solution.py:28
  15.8 4.5 %collective-permute-done.4.refs_8_ = bf16[12,128,128]{2,1,0:T(8,128)(2,1)S(1)} collective-permute-done((bf16[12,128,128]{2,1,0:T(8,128)(2,1)}, bf16[12,128,128]{2,1,0:T(8,128)(2,1)S(1)}, u32[]{:S(2)}, u32[]{:S(2)}) %collective-permute-start.4) | collective-permute-done | bytes 393248 | tf_op jit(solution)/shard_map/ppermute | solution.py:28
  20.3 0.0 collective-permute-start.5
  20.3 0.0 collective-permute-done.7.refs_9_
  20.3 2.7 %collective-permute-start.8 = (bf16[12,128,128]{2,1,0:T(8,128)(2,1)S(1)}, bf16[12,128,128]{2,1,0:T(8,128)(2,1)S(1)}, u32[]{:S(2)}, u32[]{:S(2)}) collective-permute-start(bf16[12,128,128]{2,1,0:T(8,128)(2,1)S(1)} %collective-permute-done.7.refs_9_), channel_id=1, source_target_pairs={{0,112},{16,0},{32,16},{48,32},{64,48},{80,64},{96,80},{112,96},{1... | collective-permute-start | bytes 1179656 | tf_op jit(solution)/shard_map/ppermute | solution.py:28
  23.0 0.3 collective-permute-done.1.refs_1_.q1
  23.2 0.0 collective-permute-done.2.refs_2_.q2
  23.2 2.7 %collective-permute-start.3 = (bf16[2,6,128,128]{3,2,1,0:T(8,128)(2,1)S(1)}, bf16[2,6,128,128]{3,2,1,0:T(8,128)(2,1)S(1)}, u32[]{:S(2)}, u32[]{:S(2)}) collective-permute-start(bf16[2,6,128,128]{3,2,1,0:T(8,128)(2,1)S(1)} %pad_maximum_fusion.refs_0_.q0), channel_id=1, source_target_pairs={{0,8},{4,12},{8,0},{12,4},{1,9},{5,13},{9,1},{13,5},{2,10},{6,14},... | collective-permute-start | bytes 1179656 | tf_op jit(solution)/shard_map/ppermute | solution.py:28
  25.9 4.6 %collective-permute-done.5.refs_10_ = bf16[12,128,128]{2,1,0:T(8,128)(2,1)S(1)} collective-permute-done((bf16[12,128,128]{2,1,0:T(8,128)(2,1)S(1)}, bf16[12,128,128]{2,1,0:T(8,128)(2,1)S(1)}, u32[]{:S(2)}, u32[]{:S(2)}) %collective-permute-start.5) | collective-permute-done | bytes 393248 | tf_op jit(solution)/shard_map/ppermute | solution.py:28
  30.5 0.0 collective-permute-start.6
  30.5 0.0 collective-permute-done.8.refs_4_
  30.5 2.7 %collective-permute-start.9 = (bf16[12,128,128]{2,1,0:T(8,128)(2,1)S(1)}, bf16[12,128,128]{2,1,0:T(8,128)(2,1)S(1)}, u32[]{:S(2)}, u32[]{:S(2)}) collective-permute-start(bf16[12,128,128]{2,1,0:T(8,128)(2,1)S(1)} %collective-permute-done.8.refs_4_), channel_id=1, source_target_pairs={{0,112},{16,0},{32,16},{48,32},{64,48},{80,64},{96,80},{112,96},{1... | collective-permute-start | bytes 1179656 | tf_op jit(solution)/shard_map/ppermute | solution.py:28
  33.2 0.1 pad_add_fusion.at
  33.3 0.0 collective-permute-done.3.refs_3_.q3
  33.3 0.0 copy-done.3
  33.3 4.1 %attend2048.1 = (f32[4,3,256,256]{3,2,1,0:T(8,128)S(1)}, f32[4,3,8,256]{3,2,1,0:T(8,128)S(1)}) custom-call(bf16[2,6,128,128]{3,2,1,0:T(8,128)(2,1)S(1)} %pad_maximum_fusion.refs_0_.q0, bf16[2,6,128,128]{3,2,1,0:T(8,128)(2,1)S(1)} %collective-permute-done.1.refs_1_.q1, bf16[2,6,128,128]{3,2,1,0:T(8,128)(2,1)S(1)} %collective-permute-done.2.refs_2_.q2, ...), custom_call_target="tpu_custom_call" | custom-call | flops 3221225472 | bytes 8388608 | tf_op jit(solution)/shard_map/attend2048/pallas_call | solution.py:135
  37.4 2.5 %collective-permute-done.6.refs_5_ = bf16[12,128,128]{2,1,0:T(8,128)(2,1)S(1)} collective-permute-done((bf16[12,128,128]{2,1,0:T(8,128)(2,1)S(1)}, bf16[12,128,128]{2,1,0:T(8,128)(2,1)S(1)}, u32[]{:S(2)}, u32[]{:S(2)}) %collective-permute-start.6) | collective-permute-done | bytes 393248 | tf_op jit(solution)/shard_map/ppermute | solution.py:28
  39.9 0.0 collective-permute-done.9.refs_6_
  39.9 0.3 collective-permute-start.10
  40.2 2.7 %collective-permute-start.11 = (bf16[6,128,128]{2,1,0:T(8,128)(2,1)S(1)}, bf16[6,128,128]{2,1,0:T(8,128)(2,1)S(1)}, u32[]{:S(2)}, u32[]{:S(2)}) collective-permute-start(bf16[6,128,128]{2,1,0:T(8,128)(2,1)S(1)} %slice.20), channel_id=1, source_target_pairs={{0,112},{16,0},{32,16},{48,32},{64,48},{80,64},{96,80},{112,96},{1... | collective-permute-start | bytes 589832 | tf_op jit(solution)/shard_map/ppermute | solution.py:28
  43.0 3.8 %attend1536.1 = (f32[4,3,256,256]{3,2,1,0:T(8,128)S(1)}, f32[4,3,8,256]{3,2,1,0:T(8,128)S(1)}) custom-call(bf16[2,6,128,128]{3,2,1,0:T(8,128)(2,1)S(1)} %pad_maximum_fusion.refs_0_.q0, bf16[2,6,128,128]{3,2,1,0:T(8,128)(2,1)S(1)} %collective-permute-done.1.refs_1_.q1, ...), custom_call_target="tpu_custom_call", output_to_operand_aliasing={{0}: (7, {}), {1}: (8, {})} | custom-call | flops 2415919104 | bytes 8388608 | tf_op jit(solution)/shard_map/attend1536/pallas_call | solution.py:135
  46.8 0.0 collective-permute-done.10.kfar
  46.8 0.0 collective-permute-done.11.vfar
  46.8 3.4 %close.1 = bf16[8,4,208,128]{3,2,1,0:T(8,128)(2,1)} custom-call(s32[2]{0:T(128)S(1)} %pad_add_fusion.at, bf16[2,6,128,128]{3,2,1,0:T(8,128)(2,1)S(1)} %pad_maximum_fusion.refs_0_.q0, bf16[2,6,128,128]{3,2,1,0:T(8,128)(2,1)S(1)} %collective-permute-done.1.refs_1_.q1, bf16[2,6,128,128]{3,2,1,0:T(8,128)(2,1)S(1)} %collective-permute-done.2.refs_2_.q2, ...), custom_call_target="tpu_custom_call" | custom-call | flops 805306368 | bytes 8388608 | tf_op jit(solution)/shard_map/close/pallas_call | solution.py:200
  50.2 9.3 %all-to-all-start = ((bf16[32,208,128]{2,1,0:T(8,128)(2,1)}), bf16[32,208,128]{2,1,0:T(8,128)(2,1)}, u32[]{:S(2)}, u32[]{:S(2)}) async-start(bf16[32,208,128]{2,1,0:T(8,128)(2,1)} %bitcast.5), calls=%async_computation | async-start | bytes 3407872 | tf_op jit(solution)/shard_map/all_to_all | solution.py:331
  59.5 0.0 collective-permute-done.12.w2
  59.5 0.0 copy-start
  59.5 3.3 %fusion = (bf16[192,3072]{1,0:T(8,128)(2,1)}, bf16[192,3072]{1,0:T(8,128)(2,1)}) fusion(bf16[384,3072]{1,0:T(8,128)(2,1)} %collective-permute-done.12.w2), kind=kLoop, calls=%fused_computation.2 | loop fusion | bytes 4718592 | tf_op jit(solution)/shard_map/slice | solution.py:335
  62.8 0.3 collective-permute-start.15
  63.1 0.2 collective-permute-start.16
  63.3 1.6 %fusion.1 = (bf16[192,3072]{1,0:T(8,128)(2,1)}, bf16[192,3072]{1,0:T(8,128)(2,1)}) fusion(bf16[384,3072]{1,0:T(8,128)(2,1)S(1)} %copy-done), kind=kLoop, calls=%fused_computation.3 | loop fusion | bytes 4718592 | tf_op jit(solution)/shard_map/slice | solution.py:334
  64.9 0.3 collective-permute-start.13
  65.2 0.2 collective-permute-start.14
  65.5 18.2 %all-to-all-done = bf16[32,208,128]{2,1,0:T(8,128)(2,1)} async-done(((bf16[32,208,128]{2,1,0:T(8,128)(2,1)}), bf16[32,208,128]{2,1,0:T(8,128)(2,1)}, u32[]{:S(2)}, u32[]{:S(2)}) %all-to-all-start) | async-done | bytes 1703968 | tf_op jit(solution)/shard_map/all_to_all | solution.py:331
  83.6 0.0 collective-permute-done.15.w3a
  83.6 0.0 collective-permute-done.16.w3b
  83.6 0.0 collective-permute-done.13.w1a
  83.7 0.0 collective-permute-done.14.w1b
  83.7 4.7 %project.1 = (bf16[32,3072]{1,0:T(8,128)(2,1)}, bf16[32,3072]{1,0:T(8,128)(2,1)}) custom-call(s32[1]{0:T(128)} %bitcast.me, bf16[8,4,208,128]{3,2,1,0:T(8,128)(2,1)} %bitcast.6.got_hbm, bf16[384,3072]{1,0:T(8,128)(2,1)S(1)} %copy-done, bf16[192,3072]{1,0:T(8,128)(2,1)} %collective-permute-done.13.w1a, bf16[192,3072]{1,0:T(8,128)(2,1)} %collective-permute-done.14.w1b, ...), custom_call_target="tpu_custom_call" | custom-call | flops 603979776 | bytes 9437184 | tf_op jit(solution)/shard_map/project/pallas_call | solution.py:287
  (9 shorter events, 0.0 us)
Async XLA Ops:
  0.6 32.6 %copy-start.3 = (bf16[128,384]{1,0:T(8,128)(2,1)S(1)}, bf16[128,384]{1,0:T(8,128)(2,1)}, u32[]{:S(2)}) copy-start(bf16[128,384]{1,0:T(8,128)(2,1)} %refs_6_.1) | copy-start | bytes 294916
  0.6 32.6 %copy-start.4 = (bf16[128,384]{1,0:T(8,128)(2,1)S(1)}, bf16[128,384]{1,0:T(8,128)(2,1)}, u32[]{:S(2)}) copy-start(bf16[128,384]{1,0:T(8,128)(2,1)} %refs_7_.1) | copy-start | bytes 294916
  0.7 32.6 %copy-start.1 = (bf16[128,384]{1,0:T(8,128)(2,1)S(1)}, bf16[128,384]{1,0:T(8,128)(2,1)}, u32[]{:S(2)}) copy-start(bf16[128,384]{1,0:T(8,128)(2,1)} %refs_4_.1) | copy-start | bytes 294916
  0.7 32.6 %copy-start.2 = (bf16[128,384]{1,0:T(8,128)(2,1)S(1)}, bf16[128,384]{1,0:T(8,128)(2,1)}, u32[]{:S(2)}) copy-start(bf16[128,384]{1,0:T(8,128)(2,1)} %refs_5_.1) | copy-start | bytes 294916
  0.7 58.8 %collective-permute-start.12 = (bf16[384,3072]{1,0:T(8,128)(2,1)}, bf16[384,3072]{1,0:T(8,128)(2,1)}, u32[]{:S(2)}, u32[]{:S(2)}) collective-permute-start(bf16[384,3072]{1,0:T(8,128)(2,1)} %w0.1), channel_id=1, source_target_pairs={{128,2},{2,128},{130,0},{0,130},{129,3},{3,129},{131,1},{1,131},{1... | collective-permute-start | bytes 7077896 | tf_op jit(solution)/shard_map/ppermute | solution.py:314
  6.1 5.8 %collective-permute-start = (bf16[6,128,128]{2,1,0:T(8,128)(2,1)}, bf16[6,128,128]{2,1,0:T(8,128)(2,1)S(1)}, u32[]{:S(2)}, u32[]{:S(2)}) collective-permute-start(bf16[6,128,128]{2,1,0:T(8,128)(2,1)} %get-tuple-element.17), channel_id=1, source_target_pairs={{0,128},{128,0},{1,129},{129,1},{2,130},{130,2},{3,131},{131,3},{4... | collective-permute-start | bytes 589832 | tf_op jit(solution)/shard_map/ppermute | solution.py:28
  6.1 14.2 %collective-permute-start.4 = (bf16[12,128,128]{2,1,0:T(8,128)(2,1)}, bf16[12,128,128]{2,1,0:T(8,128)(2,1)S(1)}, u32[]{:S(2)}, u32[]{:S(2)}) collective-permute-start(bf16[12,128,128]{2,1,0:T(8,128)(2,1)} %get-tuple-element.21), channel_id=1, source_target_pairs={{0,16},{16,32},{32,48},{48,64},{64,80},{80,96},{96,112},{112,0},{1... | collective-permute-start | bytes 1179656 | tf_op jit(solution)/shard_map/ppermute | solution.py:28
  7.8 12.5 %collective-permute-start.7 = (bf16[12,128,128]{2,1,0:T(8,128)(2,1)}, bf16[12,128,128]{2,1,0:T(8,128)(2,1)S(1)}, u32[]{:S(2)}, u32[]{:S(2)}) collective-permute-start(bf16[12,128,128]{2,1,0:T(8,128)(2,1)} %get-tuple-element.21), channel_id=1, source_target_pairs={{0,112},{16,0},{32,16},{48,32},{64,48},{80,64},{96,80},{112,96},{1... | collective-permute-start | bytes 1179656 | tf_op jit(solution)/shard_map/ppermute | solution.py:28
  12.9 10.4 %collective-permute-start.1 = (bf16[2,6,128,128]{3,2,1,0:T(8,128)(2,1)S(1)}, bf16[2,6,128,128]{3,2,1,0:T(8,128)(2,1)S(1)}, u32[]{:S(2)}, u32[]{:S(2)}) collective-permute-start(bf16[2,6,128,128]{3,2,1,0:T(8,128)(2,1)S(1)} %pad_maximum_fusion.refs_0_.q0), channel_id=1, source_target_pairs={{0,4},{4,8},{8,12},{12,0},{1,5},{5,9},{9,13},{13,1},{2,6},{6,10},{... | collective-permute-start | bytes 1179656 | tf_op jit(solution)/shard_map/ppermute | solution.py:28
  14.2 9.0 %collective-permute-start.2 = (bf16[2,6,128,128]{3,2,1,0:T(8,128)(2,1)S(1)}, bf16[2,6,128,128]{3,2,1,0:T(8,128)(2,1)S(1)}, u32[]{:S(2)}, u32[]{:S(2)}) collective-permute-start(bf16[2,6,128,128]{3,2,1,0:T(8,128)(2,1)S(1)} %pad_maximum_fusion.refs_0_.q0), channel_id=1, source_target_pairs={{0,12},{4,0},{8,4},{12,8},{1,13},{5,1},{9,5},{13,9},{2,14},{6,2},{... | collective-permute-start | bytes 1179656 | tf_op jit(solution)/shard_map/ppermute | solution.py:28
  20.3 10.2 %collective-permute-start.5 = (bf16[12,128,128]{2,1,0:T(8,128)(2,1)S(1)}, bf16[12,128,128]{2,1,0:T(8,128)(2,1)S(1)}, u32[]{:S(2)}, u32[]{:S(2)}) collective-permute-start(bf16[12,128,128]{2,1,0:T(8,128)(2,1)S(1)} %collective-permute-done.4.refs_8_), channel_id=1, source_target_pairs={{0,16},{16,32},{32,48},{48,64},{64,80},{80,96},{96,112},{112,0},{1... | collective-permute-start | bytes 1179656 | tf_op jit(solution)/shard_map/ppermute | solution.py:28
  20.3 10.2 %collective-permute-start.8 = (bf16[12,128,128]{2,1,0:T(8,128)(2,1)S(1)}, bf16[12,128,128]{2,1,0:T(8,128)(2,1)S(1)}, u32[]{:S(2)}, u32[]{:S(2)}) collective-permute-start(bf16[12,128,128]{2,1,0:T(8,128)(2,1)S(1)} %collective-permute-done.7.refs_9_), channel_id=1, source_target_pairs={{0,112},{16,0},{32,16},{48,32},{64,48},{80,64},{96,80},{112,96},{1... | collective-permute-start | bytes 1179656 | tf_op jit(solution)/shard_map/ppermute | solution.py:28
  23.2 10.0 %collective-permute-start.3 = (bf16[2,6,128,128]{3,2,1,0:T(8,128)(2,1)S(1)}, bf16[2,6,128,128]{3,2,1,0:T(8,128)(2,1)S(1)}, u32[]{:S(2)}, u32[]{:S(2)}) collective-permute-start(bf16[2,6,128,128]{3,2,1,0:T(8,128)(2,1)S(1)} %pad_maximum_fusion.refs_0_.q0), channel_id=1, source_target_pairs={{0,8},{4,12},{8,0},{12,4},{1,9},{5,13},{9,1},{13,5},{2,10},{6,14},... | collective-permute-start | bytes 1179656 | tf_op jit(solution)/shard_map/ppermute | solution.py:28
  30.5 9.4 %collective-permute-start.6 = (bf16[12,128,128]{2,1,0:T(8,128)(2,1)S(1)}, bf16[12,128,128]{2,1,0:T(8,128)(2,1)S(1)}, u32[]{:S(2)}, u32[]{:S(2)}) collective-permute-start(bf16[12,128,128]{2,1,0:T(8,128)(2,1)S(1)} %collective-permute-done.5.refs_10_), channel_id=1, source_target_pairs={{0,16},{16,32},{32,48},{48,64},{64,80},{80,96},{96,112},{112,0},{1... | collective-permute-start | bytes 1179656 | tf_op jit(solution)/shard_map/ppermute | solution.py:28
  30.5 9.4 %collective-permute-start.9 = (bf16[12,128,128]{2,1,0:T(8,128)(2,1)S(1)}, bf16[12,128,128]{2,1,0:T(8,128)(2,1)S(1)}, u32[]{:S(2)}, u32[]{:S(2)}) collective-permute-start(bf16[12,128,128]{2,1,0:T(8,128)(2,1)S(1)} %collective-permute-done.8.refs_4_), channel_id=1, source_target_pairs={{0,112},{16,0},{32,16},{48,32},{64,48},{80,64},{96,80},{112,96},{1... | collective-permute-start | bytes 1179656 | tf_op jit(solution)/shard_map/ppermute | solution.py:28
  39.9 6.8 %collective-permute-start.10 = (bf16[6,128,128]{2,1,0:T(8,128)(2,1)S(1)}, bf16[6,128,128]{2,1,0:T(8,128)(2,1)S(1)}, u32[]{:S(2)}, u32[]{:S(2)}) collective-permute-start(bf16[6,128,128]{2,1,0:T(8,128)(2,1)S(1)} %slice.19), channel_id=1, source_target_pairs={{0,16},{16,32},{32,48},{48,64},{64,80},{80,96},{96,112},{112,0},{1... | collective-permute-start | bytes 589832 | tf_op jit(solution)/shard_map/ppermute | solution.py:28
  40.2 6.6 %collective-permute-start.11 = (bf16[6,128,128]{2,1,0:T(8,128)(2,1)S(1)}, bf16[6,128,128]{2,1,0:T(8,128)(2,1)S(1)}, u32[]{:S(2)}, u32[]{:S(2)}) collective-permute-start(bf16[6,128,128]{2,1,0:T(8,128)(2,1)S(1)} %slice.20), channel_id=1, source_target_pairs={{0,112},{16,0},{32,16},{48,32},{64,48},{80,64},{96,80},{112,96},{1... | collective-permute-start | bytes 589832 | tf_op jit(solution)/shard_map/ppermute | solution.py:28
  50.2 33.5 %all-to-all-start = ((bf16[32,208,128]{2,1,0:T(8,128)(2,1)}), bf16[32,208,128]{2,1,0:T(8,128)(2,1)}, u32[]{:S(2)}, u32[]{:S(2)}) async-start(bf16[32,208,128]{2,1,0:T(8,128)(2,1)} %bitcast.5), calls=%async_computation | async-start | bytes 3407872 | tf_op jit(solution)/shard_map/all_to_all | solution.py:331
  59.5 3.9 %copy-start = (bf16[384,3072]{1,0:T(8,128)(2,1)S(1)}, bf16[384,3072]{1,0:T(8,128)(2,1)}, u32[]{:S(2)}) copy-start(bf16[384,3072]{1,0:T(8,128)(2,1)} %w0.1) | copy-start | bytes 7077892
  62.8 20.8 %collective-permute-start.15 = (bf16[192,3072]{1,0:T(8,128)(2,1)}, bf16[192,3072]{1,0:T(8,128)(2,1)S(1)}, u32[]{:S(2)}, u32[]{:S(2)}) collective-permute-start(bf16[192,3072]{1,0:T(8,128)(2,1)} %get-tuple-element.33), channel_id=1, source_target_pairs={{0,1},{1,0},{2,3},{3,2},{4,5},{5,4},{6,7},{7,6},{8,9},{9,8},{10,11... | collective-permute-start | bytes 3538952 | tf_op jit(solution)/shard_map/ppermute | solution.py:28
  63.1 20.5 %collective-permute-start.16 = (bf16[192,3072]{1,0:T(8,128)(2,1)}, bf16[192,3072]{1,0:T(8,128)(2,1)}, u32[]{:S(2)}, u32[]{:S(2)}) collective-permute-start(bf16[192,3072]{1,0:T(8,128)(2,1)} %get-tuple-element.32), channel_id=1, source_target_pairs={{0,1},{1,0},{2,3},{3,2},{4,5},{5,4},{6,7},{7,6},{8,9},{9,8},{10,11... | collective-permute-start | bytes 3538952 | tf_op jit(solution)/shard_map/ppermute | solution.py:28
  64.9 18.7 %collective-permute-start.13 = (bf16[192,3072]{1,0:T(8,128)(2,1)}, bf16[192,3072]{1,0:T(8,128)(2,1)}, u32[]{:S(2)}, u32[]{:S(2)}) collective-permute-start(bf16[192,3072]{1,0:T(8,128)(2,1)} %get-tuple-element.35), channel_id=1, source_target_pairs={{0,1},{1,0},{2,3},{3,2},{4,5},{5,4},{6,7},{7,6},{8,9},{9,8},{10,11... | collective-permute-start | bytes 3538952 | tf_op jit(solution)/shard_map/ppermute | solution.py:28
  65.2 18.4 %collective-permute-start.14 = (bf16[192,3072]{1,0:T(8,128)(2,1)}, bf16[192,3072]{1,0:T(8,128)(2,1)}, u32[]{:S(2)}, u32[]{:S(2)}) collective-permute-start(bf16[192,3072]{1,0:T(8,128)(2,1)} %get-tuple-element.34), channel_id=1, source_target_pairs={{0,1},{1,0},{2,3},{3,2},{4,5},{5,4},{6,7},{7,6},{8,9},{9,8},{10,11... | collective-permute-start | bytes 3538952 | tf_op jit(solution)/shard_map/ppermute | solution.py:28
